TPU v7x, 32 devices: a whole 2x2x4 slice. The times are simulated.
32 devices in a mesh: row: 4 (over x, core), col: 8 (over z, y).
Axes of the slice: x: 2, y: 2, z: 4, core: 2. Of those that a mesh axis runs over, the one named last changes fastest.
Arguments:
- pair_input: bfloat16 [192, 384, 128], P('row', 'col'), may hold values from -6 to 6
- bin_features: bfloat16 [192, 512], P('row'), may hold values from -6 to 6
- context_features: bfloat16 [384, 512], replicated, may hold values from -6 to 6
- proj_weight: bfloat16 [512, 256], replicated, may hold values from -0.25 to 0.25
- conv_weight: bfloat16 [9, 128, 128], replicated, may hold values from -0.1875 to 0.1875
- valid_bins: int32 [576], replicated, may hold values 0 or 1
- cotangent: bfloat16 [192, 384, 128], P('row', 'col'), may hold values from -6 to 6
Outputs:
- pair_output: bfloat16 [192, 384, 128], P('row', 'col')
- pair_grad: bfloat16 [192, 384, 128], P('row', 'col')
- feature_grad: bfloat16 [192, 512], P('row')
- proj_grad: float32 [512, 256], replicated
- conv_grad: float32 [9, 128, 128], replicated
All inputs are finite; a program needn't handle non-finite values.
Results may differ from a plain program's by a relative error of at most 0.0065.
Values may be sent and summed in bfloat16 or wider, within the bound.
No kernel may reach another device: no remote copies, remote signals or barrier semaphores. Data moves between devices by JAX's collectives and lax.ppermute only.
A program may use at most 64 MiB of HBM per device.

v0:
```python
import jax
import jax.numpy as jnp
from jax import lax
from jax.sharding import PartitionSpec as P


def with_halo(block, sides, width):
    for axis, dim in sides:
        count = lax.axis_size(axis)
        forward = [(i, i + 1) for i in range(count - 1)]
        backward = [(target, source) for source, target in forward]
        low = lax.ppermute(
            lax.slice_in_dim(block, block.shape[dim] - width, None, axis=dim), axis, forward
        )
        high = lax.ppermute(lax.slice_in_dim(block, 0, width, axis=dim), axis, backward)
        block = jnp.concatenate([low, block, high], axis=dim)
    return block


def silu_parts(values):
    sigma = jax.nn.sigmoid(values)
    return (values * sigma, sigma * (1.0 + values * (1.0 - sigma)))


def with_rim(field):
    return with_halo(field, (("row", 0), ("col", 1)), 1)


def skew_sum(values, tile_rows, band_cols, channels):
    widened = jnp.pad(values, ((0, 0), (0, tile_rows), (0, 0)))
    length = tile_rows * (band_cols + tile_rows - 1)
    flat = widened.reshape(tile_rows * (band_cols + tile_rows), channels)[:length]
    return jnp.sum(flat.reshape(tile_rows, band_cols + tile_rows - 1, channels), axis=0)


def body(
    pair_input, bin_features, context_features, proj_weight, conv_weight, valid_bins, cotangent
):
    tile_rows, band_cols, channels = pair_input.shape
    row_count = lax.axis_size("row")
    row_index = lax.axis_index("row")
    col_index = lax.axis_index("col")
    all_bins = tile_rows * row_count
    band_total = band_cols * lax.axis_size("col")
    row_start = row_index * tile_rows
    col_start = row_start + col_index * band_cols
    span = tile_rows + band_cols
    proj = jnp.dot(bin_features, proj_weight, preferred_element_type=jnp.float32).astype(
        jnp.bfloat16
    )
    query_part = proj[:, :channels].astype(jnp.float32)
    context_key = jnp.dot(
        context_features, proj_weight[:, channels:], preferred_element_type=jnp.float32
    ).astype(jnp.bfloat16)
    key_gathered = lax.all_gather(proj[:, channels:], "row", axis=0, tiled=True)
    key_whole = jnp.concatenate([key_gathered, context_key], axis=0)
    key_window = lax.dynamic_slice_in_dim(
        jnp.pad(key_whole, ((0, span), (0, 0))), col_start, span, 0
    )
    valid_window = lax.dynamic_slice_in_dim(
        jnp.pad(valid_bins, (0, span)), col_start, span, 0
    ).astype(jnp.float32)
    valid_rows = lax.dynamic_slice_in_dim(valid_bins, row_start, tile_rows, 0).astype(jnp.float32)
    column_index = (
        jnp.arange(tile_rows, dtype=jnp.int32)[:, None]
        + jnp.arange(band_cols, dtype=jnp.int32)[None, :]
    )
    key_skew = key_window[column_index].astype(jnp.float32)
    mask = (valid_rows[:, None] * valid_window[column_index])[:, :, None]
    mixed = (mask * (pair_input.astype(jnp.float32) + query_part[:, None, :] + key_skew)).astype(
        jnp.bfloat16
    )
    padded = with_rim(mixed)
    conv = jnp.zeros((tile_rows, band_cols, channels), jnp.float32)
    for offset_index in range(9):
        row_step = offset_index // 3 - 1
        band_step = offset_index % 3 - 1
        shifted = padded[
            1 + row_step : 1 + row_step + tile_rows, 1 + band_step : 1 + band_step + band_cols
        ]
        conv = conv + jnp.einsum(
            "abc,cd->abd", shifted, conv_weight[offset_index], preferred_element_type=jnp.float32
        )
    activated, slope = silu_parts(conv)
    pair_output = (pair_input.astype(jnp.float32) + mask * activated).astype(jnp.bfloat16)
    conv_cot = (mask * cotangent.astype(jnp.float32) * slope).astype(jnp.bfloat16)
    cot_pad = with_rim(conv_cot)
    back = jnp.zeros((tile_rows, band_cols, channels), jnp.float32)
    tap_grads = []
    for offset_index in range(9):
        row_step = offset_index // 3 - 1
        band_step = offset_index % 3 - 1
        moved = cot_pad[
            1 - row_step : 1 - row_step + tile_rows, 1 - band_step : 1 - band_step + band_cols
        ]
        back = back + jnp.einsum(
            "abd,cd->abc", moved, conv_weight[offset_index], preferred_element_type=jnp.float32
        )
        shifted = padded[
            1 + row_step : 1 + row_step + tile_rows, 1 + band_step : 1 + band_step + band_cols
        ]
        tap_grads.append(
            jnp.einsum("abc,abd->cd", shifted, conv_cot, preferred_element_type=jnp.float32)
        )
    conv_part = jnp.stack(tap_grads)
    pair_grad = (cotangent.astype(jnp.float32) + mask * back).astype(jnp.bfloat16)
    masked = mask * back
    query_grad = jnp.sum(masked, axis=1)
    key_grad = skew_sum(masked, tile_rows, band_cols, channels)
    key_full = lax.dynamic_update_slice_in_dim(
        jnp.zeros((all_bins + band_total + span, channels), jnp.float32), key_grad, col_start, 0
    )
    key_buffer = key_full[:all_bins]
    tail_terms = key_full[all_bins : all_bins + band_total]
    context_grad = jnp.dot(
        context_features.astype(jnp.float32).T, tail_terms, precision=lax.Precision.HIGHEST
    )
    context_block = jnp.pad(context_grad, ((0, 0), (channels, 0)))
    feature_rows = bin_features.astype(jnp.float32).T
    first_col = (col_index == 0).astype(jnp.float32)
    query_buffer = lax.dynamic_update_slice_in_dim(
        jnp.zeros((all_bins, channels), jnp.float32), query_grad, row_start, 0
    )
    bin_terms = jnp.concatenate([query_buffer, key_buffer], axis=1)
    offset_total = lax.psum(bin_terms, "col")
    bin_grad = lax.psum_scatter(offset_total, "row", scatter_dimension=0, tiled=True)
    proj_part = jnp.dot(feature_rows, bin_grad, precision=lax.Precision.HIGHEST) * first_col
    proj_part = proj_part + context_block
    conv_grad, proj_grad = lax.psum((conv_part, proj_part), ("row", "col"))
    feature_grad = lax.dot_general(
        bin_grad.astype(jnp.bfloat16),
        proj_weight,
        (((1,), (1,)), ((), ())),
        preferred_element_type=jnp.float32,
    ).astype(jnp.bfloat16)
    return (pair_output, pair_grad, feature_grad, proj_grad, conv_grad)


def solution(mesh):
    in_specs = (P("row", "col", None), P("row", None), P(), P(), P(), P(), P("row", "col", None))
    out_specs = (P("row", "col", None), P("row", "col", None), P("row", None), P(), P())
    return jax.shard_map(body, mesh=mesh, in_specs=in_specs, out_specs=out_specs, check_vma=False)
```

profile of v0, /device:TPU:0, one launch (start us, length us, event | category | flops | bytes accessed | tf_op | source)
XLA Modules:
  0.0 281.7 jit_solution(1836260634804504137)
XLA Ops:
  8.1 13.3 %gather_fusion = f32[2304]{0:T(1024)S(1)} fusion(f32[96]{0:T(128)S(1)} %fusion.111, s32[3072]{0:T(1024)S(1)} %pad_clamp_fusion), kind=kCustom, calls=%fused_computation | custom fusion | bytes 27648 | tf_op jit(solution)/shard_map/gather | solution.py:69
  22.4 6.2 %all_gather.3 = bf16[192,128]{1,0:T(8,128)(2,1)S(1)} all-gather(bf16[48,128]{1,0:T(8,128)(2,1)S(1)} %get-tuple-element.34), channel_id=1, replica_groups=mesh['row'=4,'col'=8] {'row'}, dimensions={0}, use_global_device_ids=true | all-gather | bytes 61440 | tf_op jit(solution)/shard_map/all_gather | solution.py:55
  29.0 4.7 %gather_fusion.1 = bf16[2304,128]{1,0:T(8,128)(2,1)S(1)} fusion(bf16[96,128]{1,0:T(8,128)(2,1)S(1)} %fusion.109, s32[3072]{0:T(1024)S(1)} %pad_clamp_fusion), kind=kCustom, calls=%fused_computation.1 | custom fusion | bytes 1188864 | tf_op jit(solution)/shard_map/gather | solution.py:68
  34.2 2.2 collective-permute-start
  36.4 1.3 collective-permute-start.1
  38.1 2.7 collective-permute-done.1
  40.8 3.4 %collective-permute-start.2 = (bf16[50,1,128]{2,1,0:T(2,128)(2,1)S(1)}, bf16[50,1,128]{2,1,0:T(2,128)(2,1)S(1)}, u32[]{:S(2)}, u32[]{:S(2)}) collective-permute-start(bf16[50,1,128]{2,1,0:T(2,128)(2,1)S(1)} %get-tuple-element.27), channel_id=1, source_target_pairs={{0,1},{1,2},{2,3},{3,4},{4,5},{5,6},{6,7},{8,9},{9,10},{10,11},{11... | collective-permute-start | bytes 38408 | tf_op jit(solution)/shard_map/ppermute | solution.py:12
  44.3 1.3 collective-permute-start.3
  46.2 3.8 %collective-permute-done.3 = bf16[50,1,128]{2,1,0:T(2,128)(2,1)S(1)} collective-permute-done((bf16[50,1,128]{2,1,0:T(2,128)(2,1)S(1)}, bf16[50,1,128]{2,1,0:T(2,128)(2,1)S(1)}, u32[]{:S(2)}, u32[]{:S(2)}) %collective-permute-start.3) | collective-permute-done | bytes 12832 | tf_op jit(solution)/shard_map/ppermute | solution.py:15
  52.9 1.8 fusion.20
  57.7 1.3 collective-permute-start.5
  59.0 3.5 %collective-permute-start.4 = (bf16[1,48,128]{2,1,0:T(8,128)(2,1)S(1)}, bf16[1,48,128]{2,1,0:T(8,128)(2,1)S(1)}, u32[]{:S(2)}, u32[]{:S(2)}) collective-permute-start(bf16[1,48,128]{2,1,0:T(8,128)(2,1)S(1)} %get-tuple-element.29), channel_id=1, source_target_pairs={{0,8},{8,16},{16,24},{1,9},{9,17},{17,25},{2,10},{10,18},{18,26},{... | collective-permute-start | bytes 36872 | tf_op jit(solution)/shard_map/ppermute | solution.py:12
  63.4 1.3 collective-permute-start.6
  64.7 4.9 %collective-permute-start.7 = (bf16[50,1,128]{2,1,0:T(2,128)(2,1)S(1)}, bf16[50,1,128]{2,1,0:T(2,128)(2,1)S(1)}, u32[]{:S(2)}, u32[]{:S(2)}) collective-permute-start(bf16[50,1,128]{2,1,0:T(2,128)(2,1)S(1)} %get-tuple-element.24), channel_id=1, source_target_pairs={{0,1},{1,2},{2,3},{3,4},{4,5},{5,6},{6,7},{8,9},{9,10},{10,11},{11... | collective-permute-start | bytes 38408 | tf_op jit(solution)/shard_map/ppermute | solution.py:12
  70.3 0.9 collective-permute-done.7
  73.4 1.5 fusion.118
  75.2 1.6 slice.211
  76.8 1.7 reshape.61
  80.0 1.0 fusion.24
  81.4 24.2 %reduce-scatter.2.cloned.1.call-done = f32[48,256]{1,0:T(8,128)} async-done(((f32[192,256]{1,0:T(8,128)}), f32[48,256]{1,0:T(8,128)}) %reduce-scatter.2.cloned.1.call-update) | async-done | bytes 49168 | tf_op jit(solution)/shard_map/reduce_scatter | solution.py:126
  105.6 38.1 %psum.24 = f32[48,256]{1,0:T(8,128)S(1)} all-reduce(f32[48,256]{1,0:T(8,128)} %reduce-scatter.2.cloned.1.call-done), channel_id=1, replica_groups=mesh['row'=4,'col'=8] {'col'}, use_global_device_ids=true, to_apply=%region_2.3 | all-reduce | flops 12288 | bytes 98304 | tf_op jit(solution)/shard_map/psum | solution.py:125
  143.7 1.2 fusion.14
  145.8 126.2 %all-reduce.7.cloned.1.call-done = (f32[512,256]{0,1:T(8,128)}, f32[9,128,128]{2,1,0:T(8,128)}) async-done(((f32[512,256]{0,1:T(8,128)}, f32[9,128,128]{2,1,0:T(8,128)}), (f32[512,256]{0,1:T(8,128)}, f32[9,128,128]{2,1,0:T(8,128)})) %all-reduce.7.cloned.1.call-update) | async-done | bytes 1114128 | tf_op jit(solution)/shard_map/psum | solution.py:129
  272.0 2.1 copy.13
  (86 shorter events, 16.9 us)
Async XLA Ops:
  7.2 21.4 %copy-start = (bf16[384,512]{1,0:T(8,128)(2,1)S(1)}, bf16[384,512]{1,0:T(8,128)(2,1)}, u32[]{:S(2)}) copy-start(bf16[384,512]{1,0:T(8,128)(2,1)} %param.9) | copy-start | bytes 1179652
  7.2 98.4 %reduce-scatter.2.cloned.1.call-start = ((), (), s32[]{:S(2)}) async-start(), calls=%async_computation.1 | async-start | bytes 245760 | tf_op jit(solution)/shard_map/reduce_scatter | solution.py:126
  8.1 14.1 %copy-start.3 = (bf16[512,256]{1,0:T(8,128)(2,1)S(1)}, bf16[512,256]{1,0:T(8,128)(2,1)}, u32[]{:S(2)}) copy-start(bf16[512,256]{1,0:T(8,128)(2,1)} %param.10) | copy-start | bytes 786436
  8.1 14.1 %copy-start.11 = (bf16[48,512]{1,0:T(8,128)(2,1)S(1)}, bf16[48,512]{1,0:T(8,128)(2,1)}, u32[]{:S(2)}) copy-start(bf16[48,512]{1,0:T(8,128)(2,1)} %param.8) | copy-start | bytes 147460
  29.0 4.8 %copy-start.6 = (bf16[48,48,128]{2,1,0:T(8,128)(2,1)S(1)}, bf16[48,48,128]{2,1,0:T(8,128)(2,1)}, u32[]{:S(2)}) copy-start(bf16[48,48,128]{2,1,0:T(8,128)(2,1)} %param.7) | copy-start | bytes 1769476
  33.7 4.1 %copy-start.5 = (bf16[9,128,128]{2,1,0:T(8,128)(2,1)S(1)}, bf16[9,128,128]{2,1,0:T(8,128)(2,1)}, u32[]{:S(2)}) copy-start(bf16[9,128,128]{2,1,0:T(8,128)(2,1)} %param.11) | copy-start | bytes 884740
  34.2 3.9 %collective-permute-start = (bf16[1,48,128]{2,1,0:T(8,128)(2,1)S(1)}, bf16[1,48,128]{2,1,0:T(8,128)(2,1)S(1)}, u32[]{:S(2)}, u32[]{:S(2)}) collective-permute-start(bf16[1,48,128]{2,1,0:T(8,128)(2,1)S(1)} %get-tuple-element.31), channel_id=1, source_target_pairs={{0,8},{8,16},{16,24},{1,9},{9,17},{17,25},{2,10},{10,18},{18,26},{... | collective-permute-start | bytes 36872 | tf_op jit(solution)/shard_map/ppermute | solution.py:12
  36.4 4.3 %collective-permute-start.1 = (bf16[1,48,128]{2,1,0:T(8,128)(2,1)S(1)}, bf16[1,48,128]{2,1,0:T(8,128)(2,1)S(1)}, u32[]{:S(2)}, u32[]{:S(2)}) collective-permute-start(bf16[1,48,128]{2,1,0:T(8,128)(2,1)S(1)} %get-tuple-element.32), channel_id=1, source_target_pairs={{8,0},{16,8},{24,16},{9,1},{17,9},{25,17},{10,2},{18,10},{26,18},{... | collective-permute-start | bytes 36872 | tf_op jit(solution)/shard_map/ppermute | solution.py:15
  40.8 5.3 %collective-permute-start.2 = (bf16[50,1,128]{2,1,0:T(2,128)(2,1)S(1)}, bf16[50,1,128]{2,1,0:T(2,128)(2,1)S(1)}, u32[]{:S(2)}, u32[]{:S(2)}) collective-permute-start(bf16[50,1,128]{2,1,0:T(2,128)(2,1)S(1)} %get-tuple-element.27), channel_id=1, source_target_pairs={{0,1},{1,2},{2,3},{3,4},{4,5},{5,6},{6,7},{8,9},{9,10},{10,11},{11... | collective-permute-start | bytes 38408 | tf_op jit(solution)/shard_map/ppermute | solution.py:12
  44.3 5.7 %collective-permute-start.3 = (bf16[50,1,128]{2,1,0:T(2,128)(2,1)S(1)}, bf16[50,1,128]{2,1,0:T(2,128)(2,1)S(1)}, u32[]{:S(2)}, u32[]{:S(2)}) collective-permute-start(bf16[50,1,128]{2,1,0:T(2,128)(2,1)S(1)} %get-tuple-element.28), channel_id=1, source_target_pairs={{1,0},{2,1},{3,2},{4,3},{5,4},{6,5},{7,6},{9,8},{10,9},{11,10},{12... | collective-permute-start | bytes 38408 | tf_op jit(solution)/shard_map/ppermute | solution.py:15
  50.4 6.5 %copy-start.1 = (bf16[50,49,128]{2,1,0:T(8,128)(2,1)}, bf16[50,49,128]{2,1,0:T(8,128)(2,1)S(1)}, u32[]{:S(2)}) copy-start(bf16[50,49,128]{2,1,0:T(8,128)(2,1)S(1)} %get-tuple-element.26) | copy-start | bytes 1881604
  51.7 1.1 copy-start.7
  51.7 1.2 copy-start.10
  57.7 5.2 %collective-permute-start.5 = (bf16[1,48,128]{2,1,0:T(8,128)(2,1)S(1)}, bf16[1,48,128]{2,1,0:T(8,128)(2,1)S(1)}, u32[]{:S(2)}, u32[]{:S(2)}) collective-permute-start(bf16[1,48,128]{2,1,0:T(8,128)(2,1)S(1)} %get-tuple-element.30), channel_id=1, source_target_pairs={{8,0},{16,8},{24,16},{9,1},{17,9},{25,17},{10,2},{18,10},{26,18},{... | collective-permute-start | bytes 36872 | tf_op jit(solution)/shard_map/ppermute | solution.py:15
  59.0 4.4 %collective-permute-start.4 = (bf16[1,48,128]{2,1,0:T(8,128)(2,1)S(1)}, bf16[1,48,128]{2,1,0:T(8,128)(2,1)S(1)}, u32[]{:S(2)}, u32[]{:S(2)}) collective-permute-start(bf16[1,48,128]{2,1,0:T(8,128)(2,1)S(1)} %get-tuple-element.29), channel_id=1, source_target_pairs={{0,8},{8,16},{16,24},{1,9},{9,17},{17,25},{2,10},{10,18},{18,26},{... | collective-permute-start | bytes 36872 | tf_op jit(solution)/shard_map/ppermute | solution.py:12
  62.9 7.1 %copy-start.9 = (f32[9,128,128]{2,1,0:T(8,128)}, f32[9,128,128]{2,1,0:T(8,128)S(1)}, u32[]{:S(2)}) copy-start(f32[9,128,128]{2,1,0:T(8,128)S(1)} %fusion.22) | copy-start | bytes 1769476
  63.4 6.9 %collective-permute-start.6 = (bf16[50,1,128]{2,1,0:T(2,128)(2,1)S(1)}, bf16[50,1,128]{2,1,0:T(2,128)(2,1)S(1)}, u32[]{:S(2)}, u32[]{:S(2)}) collective-permute-start(bf16[50,1,128]{2,1,0:T(2,128)(2,1)S(1)} %get-tuple-element.23), channel_id=1, source_target_pairs={{1,0},{2,1},{3,2},{4,3},{5,4},{6,5},{7,6},{9,8},{10,9},{11,10},{12... | collective-permute-start | bytes 38408 | tf_op jit(solution)/shard_map/ppermute | solution.py:15
  64.7 6.5 %collective-permute-start.7 = (bf16[50,1,128]{2,1,0:T(2,128)(2,1)S(1)}, bf16[50,1,128]{2,1,0:T(2,128)(2,1)S(1)}, u32[]{:S(2)}, u32[]{:S(2)}) collective-permute-start(bf16[50,1,128]{2,1,0:T(2,128)(2,1)S(1)} %get-tuple-element.24), channel_id=1, source_target_pairs={{0,1},{1,2},{2,3},{3,4},{4,5},{5,6},{6,7},{8,9},{9,10},{10,11},{11... | collective-permute-start | bytes 38408 | tf_op jit(solution)/shard_map/ppermute | solution.py:12
  78.6 1.3 copy-start.2
  79.9 192.1 %all-reduce.7.cloned.1.call-start = ((), (), s32[]{:S(2)}) async-start(), calls=%async_computation.2 | async-start | bytes 2228224 | tf_op jit(solution)/shard_map/psum | solution.py:129
  81.4 63.6 %copy-start.4 = (bf16[512,256]{1,0:T(8,128)(2,1)S(1)}, bf16[512,256]{1,0:T(8,128)(2,1)}, u32[]{:S(2)}) copy-start(bf16[512,256]{1,0:T(8,128)(2,1)} %param.10) | copy-start | bytes 786436
  272.0 2.1 copy-start.8
Sparse Core Ops, SparseCore 0:
  80.0 25.5 reduce-scatter.1
  145.1 126.8 all-reduce.6
where the time goes:
time: 282 us
  waiting for transfers between devices  158 us (56%)
  blocking collectives  44.3 us (16%)
  local copies, waits for them, and re-layouts  25.9 us (9%)
  starting transfers between devices  19.4 us (7%)
  matrix products  15.5 us (5%)
  between operations  14.5 us (5%)
  other arithmetic  3.92 us (1%)
    psum x1, waiting for transfers between devices, body(): conv_grad, proj_grad = lax.psum((conv_part, proj_part), ('row', 'col'))  126 us
    psum x1, blocking collectives, body(): offset_total = lax.psum(bin_terms, 'col')  38.1 us
    reduce_scatter x1, waiting for transfers between devices, body(): lax.psum_scatter(offset_total, 'row', scatter_dimension=0, tiled=True)  24.2 us
    ppermute x4, starting transfers between devices, with_halo(): lax.ppermute(lax.slice_in_dim(block, block.shape[dim] - width, None, axis...  14.2 us
    gather x2, local copies, waits for them, and re-layouts, body(): mask = (valid_rows[:, None] * valid_window[column_index])[:, :, None]  13.3 us
    ppermute x4, waiting for transfers between devices, with_halo(): lax.ppermute(lax.slice_in_dim(block, 0, width, axis=dim), axis, backward)  6.54 us
    all_gather x1, blocking collectives, body(): key_gathered = lax.all_gather(proj[:, channels:], 'row', axis=0, tiled=True)  6.18 us
  transfers between devices with their start and end apart: 10, of which 6 were waited for; matrix products, arithmetic and copies ran while one was open for 1% of the time, Pallas kernels for 0%

commit v1 on v0

v1 whole, which is shorter than its diff:
```python
import functools

import jax
import jax.numpy as jnp
from jax import lax
from jax.experimental import pallas as pl
from jax.experimental.pallas import tpu as pltpu
from jax.sharding import Mesh, PartitionSpec as P

ROW = ("rx", "core")
CHIPS = ("rx", "col")
BF16 = jnp.bfloat16
F32 = jnp.float32
HALO = 2
SIDE = 16
MARGIN = 16
PARAMS = pltpu.CompilerParams(vmem_limit_bytes=56 * 1024 * 1024)


def halo_row(tile, edges, index, above, below, first, last):
    if index < 0:
        return edges[above, last + 1 + index]
    if index >= tile.shape[0]:
        return edges[below, first + index - tile.shape[0]]
    return tile[index]


def neighbours(edges):
    row = lax.axis_index(ROW)
    return jnp.maximum(row - 1, 0), jnp.minimum(row + 1, edges.shape[0] - 1)


def column_kernel(pair_low, pair_high, cot_low, cot_high, edges, to_low, to_high, work):
    tile_rows = pair_low.shape[0]
    band_cols = edges.shape[2]
    above, below = neighbours(edges)
    rows = tile_rows + 2 * HALO
    taken = work.shape[0] // SIDE
    work[rows * SIDE :, :] = jnp.zeros((work.shape[0] - rows * SIDE, work.shape[1]), F32)
    for out, pair, cot, start, picks in (
        (to_low, pair_low, cot_low, 0, (0, 1)),
        (to_high, pair_high, cot_high, band_cols - SIDE, (SIDE - 2, SIDE - 1)),
    ):
        out[:, taken:, :] = jnp.zeros((3, out.shape[1] - taken, out.shape[2]), out.dtype)
        for tile, first, last, columns, slot in (
            (pair, 0, 3, picks, 0),
            (cot, 4, 5, (picks[0] if start == 0 else picks[1],), 2),
        ):
            depth = HALO if slot == 0 else 1
            for index in range(-HALO, tile_rows + HALO):
                if index < -depth or index >= tile_rows + depth:
                    values = jnp.zeros((SIDE, work.shape[1]), F32)
                elif 0 <= index < tile_rows:
                    values = tile[index].astype(F32)
                elif index < 0:
                    values = edges[above, last + 1 + index, start : start + SIDE].astype(F32)
                else:
                    values = edges[below, first + index - tile_rows, start : start + SIDE].astype(F32)
                work[(index + HALO) * SIDE : (index + HALO + 1) * SIDE, :] = values
            for place, column in enumerate(columns):
                out[slot + place, :taken, :] = work[pl.ds(column, taken, stride=SIDE), :].astype(out.dtype)


def tile_kernel(
    valid, pair, cot, low, high, edges, features, context, proj_weight, conv_weight,
    pair_output, pair_grad, keep, send,
    bins, query, key, window, rows_valid, mixed, carry, mixed3, carry3, own, skew, totals,
):
    tile_rows, band_cols, channels = pair.shape
    pitch = 64
    pad = 8
    row, col = lax.axis_index(ROW), lax.axis_index("col")
    core = lax.axis_index("core")
    above, below = neighbours(edges)
    all_bins = features.shape[0]
    tail = context.shape[0]
    row_start = row * tile_rows
    col_start = row_start + col * band_cols
    total_rows = tile_rows + 2 * HALO

    def place(index, column):
        return (index + HALO) * pitch + pad + column

    bins[:MARGIN, :] = jnp.zeros((MARGIN, bins.shape[1]), bins.dtype)
    bins[MARGIN : MARGIN + all_bins, :] = features[...]
    bins[MARGIN + all_bins : MARGIN + all_bins + tail, :] = context[...]
    bins[MARGIN + all_bins + tail :, :] = jnp.zeros((bins.shape[0] - MARGIN - all_bins - tail, bins.shape[1]), bins.dtype)
    row_bins = bins[pl.ds(pl.multiple_of(row_start, 16), query.shape[0]), :]
    query[...] = jnp.dot(row_bins, proj_weight[:, :channels], preferred_element_type=F32).astype(BF16).astype(F32)
    col_bins = bins[pl.ds(pl.multiple_of(col_start, 16), key.shape[0]), :]
    key[...] = jnp.dot(col_bins, proj_weight[:, channels:], preferred_element_type=F32).astype(BF16).astype(F32)

    row_scalars = []
    for index in range(-HALO, tile_rows + HALO):
        bin_index = row_start + index
        inside = jnp.logical_and(bin_index >= 0, bin_index < all_bins)
        scalar = jnp.where(inside, valid[jnp.clip(bin_index, 0, all_bins - 1)], 0).astype(F32)
        row_scalars.append(scalar)
        rows_valid[index + HALO : index + HALO + 1, :] = jnp.full((1, channels), scalar, F32)
    rows_valid[total_rows:, :] = jnp.zeros((rows_valid.shape[0] - total_rows, channels), F32)
    for index in range(-2 * HALO, tile_rows + band_cols + 2 * HALO):
        bin_index = col_start + index
        inside = jnp.logical_and(bin_index >= 0, bin_index < all_bins + tail)
        scalar = jnp.where(inside, valid[jnp.clip(bin_index, 0, all_bins + tail - 1)], 0).astype(F32)
        window[MARGIN + index : MARGIN + index + 1, :] = jnp.full((1, channels), scalar, F32)

    def mask_of(index):
        return window[pl.ds(MARGIN + index, band_cols), :] * row_scalars[index + HALO]

    mixed[...] = jnp.zeros(mixed.shape, F32)
    carry[...] = jnp.zeros(carry.shape, F32)
    for index in range(-HALO, tile_rows + HALO):
        mask = mask_of(index)
        source = halo_row(pair, edges, index, above, below, 0, 3).astype(F32)
        value = mask * (source + query[pl.ds(MARGIN + index, 1), :] + key[pl.ds(MARGIN + index, band_cols), :])
        mixed[pl.ds(pad + place(index, 0), band_cols), :] = value
        if -1 <= index <= tile_rows:
            source = halo_row(cot, edges, index, above, below, 4, 5).astype(F32)
            carry[pl.ds(pad + place(index, 0), band_cols), :] = mask * source
    strided = rows_valid.shape[0]
    has_low = (col > 0).astype(F32)
    has_high = (col < lax.axis_size("col") - 1).astype(F32)
    for column, source, slot, has in (
        (-2, low, 0, has_low), (-1, low, 1, has_low), (band_cols, high, 0, has_high), (band_cols + 1, high, 1, has_high),
    ):
        begin = MARGIN + column - HALO
        mask = rows_valid[...] * window[pl.ds(begin, strided), :] * has
        value = source[slot, :strided].astype(F32) + query[pl.ds(MARGIN - HALO, strided), :] + key[pl.ds(begin, strided), :]
        mixed[pl.ds(pad + place(-HALO, column), strided, stride=pitch), :] = jnp.where(mask > 0.0, value, 0.0)
        if column in (-1, band_cols):
            value = jnp.where(mask > 0.0, source[2, :strided].astype(F32), 0.0)
            carry[pl.ds(pad + place(-HALO, column), strided, stride=pitch), :] = value

    span = total_rows * pitch
    block = 4 * pitch
    for start in range(0, span, block):
        for step in range(3):
            mixed3[start : start + block, step * channels : (step + 1) * channels] = mixed[
                pl.ds(pad + start + step - 1, block), :
            ].astype(BF16)

    weights = conv_weight[...].reshape(9 * channels, channels)
    per = 5
    for first in range(-1, tile_rows + 1, per):
        begin = (first + HALO) * pitch
        around = jnp.concatenate(
            [mixed3[begin + step * pitch : begin + (step + per) * pitch, :] for step in (-1, 0, 1)], axis=1
        )
        conv = jnp.dot(around, weights, preferred_element_type=F32)
        sigma = jax.nn.sigmoid(conv)
        activated = conv * sigma
        slope = sigma * (1.0 + conv * (1.0 - sigma))
        here = pl.ds(pad + begin, per * pitch)
        carry[here, :] = carry[here, :] * slope
        for index in range(max(first, 0), min(first + per, tile_rows)):
            at = (index - first) * pitch + pad
            pair_output[index] = (
                pair[index].astype(F32) + mask_of(index) * activated[at : at + band_cols, :]
            ).astype(BF16)

    for start in range(0, span, block):
        for step in range(3):
            carry3[start : start + block, step * channels : (step + 1) * channels] = carry[
                pl.ds(pad + start + 1 - step, block), :
            ].astype(BF16)
    spot = lax.broadcasted_iota(jnp.int32, (pitch, channels), 0)
    inner = jnp.logical_and(spot >= pad, spot < pad + band_cols)
    for index in range(tile_rows):
        begin = (index + HALO) * pitch
        own[index * pitch : (index + 1) * pitch, :] = jnp.where(inner, carry[pl.ds(pad + begin, pitch), :], 0.0).astype(BF16)

    totals[...] = jnp.zeros(totals.shape, F32)
    skew[...] = jnp.zeros(skew.shape, F32)
    turned = jnp.concatenate([conv_weight[tap] for tap in range(9)], axis=1)
    per = 6
    query_at = 9 * channels + all_bins + tail
    query_rows = []
    for first in range(0, tile_rows, per):
        begin = (first + HALO) * pitch
        around = jnp.concatenate(
            [carry3[begin - step * pitch : begin + (per - step) * pitch, :] for step in (-1, 0, 1)], axis=1
        )
        back = lax.dot_general(around, turned, (((1,), (1,)), ((), ())), preferred_element_type=F32)
        for index in range(first, first + per):
            at = (index - first) * pitch + pad
            masked = mask_of(index) * back[at : at + band_cols, :]
            pair_grad[index] = (cot[index].astype(F32) + masked).astype(BF16)
            query_rows.append(jnp.sum(masked, axis=0, keepdims=True))
            skew[index % 8, index - index % 8 : index - index % 8 + band_cols, :] += masked
    query_sum = jnp.concatenate(query_rows, axis=0)
    totals[pl.ds(pl.multiple_of(query_at + row_start, 16), tile_rows), :] = query_sum
    span_bins = tile_rows + band_cols
    for step in range(8):
        key_at = 9 * channels + col_start + step
        reach = span_bins - 8
        totals[pl.ds(key_at, reach), :] += skew[step, :reach, :]

    per = 12
    grads = jnp.zeros((channels, 9 * channels), F32)
    for first in range(0, tile_rows, per):
        begin = (first + HALO) * pitch
        around = jnp.concatenate(
            [mixed3[begin + step * pitch : begin + (per + step) * pitch, :] for step in (-1, 0, 1)], axis=1
        )
        grads = grads + lax.dot_general(
            own[first * pitch : (first + per) * pitch, :], around, (((0,), (0,)), ((), ())), preferred_element_type=F32
        )
    for tap in range(9):
        totals[tap * channels : (tap + 1) * channels, :] = grads[:, tap * channels : (tap + 1) * channels]
    half = keep.shape[0]
    keep[...] = totals[pl.ds(pl.multiple_of(core * half, half), half), :]
    send[...] = totals[pl.ds(pl.multiple_of((1 - core) * half, half), half), :].astype(BF16)


def finish_kernel(mine, theirs, features, context, proj_weight, feature_grad, proj_grad, conv_grad, whole):
    core = lax.axis_index("core")
    row = lax.axis_index(ROW)
    half = mine.shape[0]
    channels = mine.shape[1]
    all_bins, tail = features.shape[0], context.shape[0]
    tile_rows = feature_grad.shape[0]
    whole[pl.ds(pl.multiple_of(core * half, half), half), :] = mine[...]
    whole[pl.ds(pl.multiple_of((1 - core) * half, half), half), :] = theirs[...]
    for tap in range(9):
        conv_grad[tap] = whole[tap * channels : (tap + 1) * channels, :].astype(F32).T
    key_at = 9 * channels
    query_at = key_at + all_bins + tail
    flip = (((0,), (0,)), ((), ()))
    own = features[...]
    proj_grad[:, :channels] = lax.dot_general(own, whole[query_at : query_at + all_bins, :], flip, preferred_element_type=F32)
    proj_grad[:, channels:] = lax.dot_general(
        own, whole[key_at : key_at + all_bins, :], flip, preferred_element_type=F32
    ) + lax.dot_general(
        context[...], whole[key_at + all_bins : query_at, :], flip, preferred_element_type=F32
    )
    start = pl.multiple_of(row * tile_rows, 16)
    both = jnp.concatenate(
        [whole[pl.ds(query_at + start, tile_rows), :], whole[pl.ds(key_at + start, tile_rows), :]], axis=1
    )
    feature_grad[...] = lax.dot_general(
        both, proj_weight[...], (((1,), (1,)), ((), ())), preferred_element_type=F32
    ).astype(BF16)


def body(
    pair_input, bin_features, context_features, proj_weight, conv_weight, valid_bins, cotangent
):
    tile_rows, band_cols, channels = pair_input.shape
    row_count = lax.axis_size(ROW)
    col_count = lax.axis_size("col")
    all_bins = tile_rows * row_count
    tail = context_features.shape[0]
    chips = row_count * col_count // 2
    side_rows = -(-(tile_rows + 2 * HALO) // 16) * 16
    taken = -(-(tile_rows + 2 * HALO) // 8) * 8

    edges = jnp.concatenate(
        [pair_input[:2], pair_input[-2:], cotangent[:1], cotangent[-1:]], axis=0
    )
    edges, features = lax.all_gather((edges, bin_features), ROW, axis=0)
    features = features.reshape(all_bins, bin_features.shape[1])

    vmem = pl.BlockSpec(memory_space=pltpu.VMEM)
    low_side = pl.BlockSpec((tile_rows, SIDE, channels), lambda step: (0, 0, 0))
    high_side = pl.BlockSpec((tile_rows, SIDE, channels), lambda step: (0, band_cols // SIDE - 1, 0))
    side = jax.ShapeDtypeStruct((3, side_rows, channels), BF16)
    to_low, to_high = pl.pallas_call(
        column_kernel,
        grid=(1,),
        out_shape=(side, side),
        in_specs=[low_side, high_side, low_side, high_side, vmem],
        out_specs=(vmem, vmem),
        scratch_shapes=[pltpu.VMEM((taken * SIDE, channels), F32)],
        compiler_params=PARAMS,
        name="columns",
    )(pair_input, pair_input, cotangent, cotangent, edges)
    up = [(i, i + 1) for i in range(col_count - 1)]
    from_low = lax.ppermute(to_high, "col", up)
    from_high = lax.ppermute(to_low, "col", [(target, source) for source, target in up])

    piece = -(-(9 * channels + 2 * all_bins + tail) // (32 * chips)) * 16
    half = piece * chips
    span = (tile_rows + 2 * HALO) * 64
    near = tile_rows + band_cols + 2 * MARGIN
    pair_output, pair_grad, keep, send = pl.pallas_call(
        tile_kernel,
        out_shape=(
            jax.ShapeDtypeStruct(pair_input.shape, BF16),
            jax.ShapeDtypeStruct(pair_input.shape, BF16),
            jax.ShapeDtypeStruct((half, channels), F32),
            jax.ShapeDtypeStruct((half, channels), BF16),
        ),
        in_specs=[pl.BlockSpec(memory_space=pltpu.SMEM)] + [vmem] * 9,
        out_specs=(vmem,) * 4,
        scratch_shapes=[
            pltpu.VMEM((MARGIN + all_bins + tail + MARGIN, bin_features.shape[1]), BF16),
            pltpu.VMEM((tile_rows + 2 * MARGIN, channels), F32),
            pltpu.VMEM((near, channels), F32),
            pltpu.VMEM((near, channels), F32),
            pltpu.VMEM((taken, channels), F32),
            pltpu.VMEM((span + 64 * (taken - tile_rows), channels), F32),
            pltpu.VMEM((span + 64 * (taken - tile_rows), channels), F32),
            pltpu.VMEM((span, 3 * channels), BF16),
            pltpu.VMEM((span, 3 * channels), BF16),
            pltpu.VMEM((tile_rows * 64, channels), BF16),
            pltpu.VMEM((8, tile_rows + band_cols, channels), F32),
            pltpu.VMEM((2 * half, channels), F32),
        ],
        compiler_params=PARAMS,
        name="tile",
    )(
        valid_bins, pair_input, cotangent, from_low, from_high, edges, features, context_features,
        proj_weight, conv_weight,
    )

    swap = [(0, 1), (1, 0)]
    part = (keep + lax.ppermute(send, "core", swap).astype(F32)).astype(BF16)
    pieces = lax.all_to_all(part.reshape(chips, piece, channels), CHIPS, 0, 0)
    total = jnp.sum(pieces.astype(F32), axis=0).astype(BF16)
    mine = lax.all_to_all(
        jnp.broadcast_to(total, (chips, piece, channels)), CHIPS, 0, 0
    ).reshape(half, channels)
    theirs = lax.ppermute(mine, "core", swap)

    feature_grad, proj_grad, conv_grad = pl.pallas_call(
        finish_kernel,
        out_shape=(
            jax.ShapeDtypeStruct(bin_features.shape, BF16),
            jax.ShapeDtypeStruct(proj_weight.shape, F32),
            jax.ShapeDtypeStruct(conv_weight.shape, F32),
        ),
        in_specs=[vmem] * 5,
        out_specs=(vmem,) * 3,
        scratch_shapes=[pltpu.VMEM((2 * half, channels), BF16)],
        compiler_params=PARAMS,
        name="finish",
    )(mine, theirs, features, context_features, proj_weight)
    return (pair_output, pair_grad, feature_grad, proj_grad, conv_grad)


def solution(mesh):
    rows, cols = mesh.shape["row"], mesh.shape["col"]
    split = Mesh(mesh.devices.reshape(rows // 2, 2, cols), ("rx", "core", "col"))
    tile = P(ROW, "col", None)
    in_specs = (tile, P(ROW, None), P(), P(), P(), P(), tile)
    out_specs = (tile, tile, P(ROW, None), P(), P())
    return jax.shard_map(body, mesh=split, in_specs=in_specs, out_specs=out_specs, check_vma=False)
```

time: 282 us -> 72.2 us (0.26)
  waiting for transfers between devices: 158 us -> 2.94 us
  local copies, waits for them, and re-layouts: 25.9 us -> 3.46 us
  matrix products: 15.5 us -> 0 us
  starting transfers between devices: 19.4 us -> 5.05 us
  between operations: 14.5 us -> 0.68 us
  Pallas kernels: 0 us -> 13.8 us
    psum x1 -> x0, waiting for transfers between devices: 126 us -> none  [body(): conv_grad, proj_grad = lax.psum((conv_part, proj_part), ('row', 'col'))]
    psum x1 -> x0, blocking collectives: 38.1 us -> none  [body(): offset_total = lax.psum(bin_terms, 'col')]
    all_to_all x0 -> x2, blocking collectives: none -> 30.8 us  [the longest x1 18.1 us: body(): pieces = lax.all_to_all(part.reshape(chips, piece, channels), CHIPS, 0, 0)]
    reduce_scatter x1 -> x0, waiting for transfers between devices: 24.2 us -> none  [body(): lax.psum_scatter(offset_total, 'row', scatter_dimension=0, tiled=True)]
    gather x3 -> x0, local copies, waits for them, and re-layouts: 18 us -> none  [the longest x2 13.3 us: body(): mask = (valid_rows[:, None] * valid_window[column_index])[:, :, None]]
    dot_general x32 -> x0, matrix products: 15.5 us -> none  [the longest x9 4.47 us: body(): jnp.einsum('abc,cd->abd', shifted, conv_weight[offset_index], preferred_e...]
    ppermute x8 -> x4, starting transfers between devices: 19.3 us -> 5.05 us  [the longest x1 3.41 us: body(): from_low = lax.ppermute(to_high, 'col', up)]
    pallas_call x0 -> x3, Pallas kernels: none -> 13.8 us  [the longest x1 8.89 us: body(): pl.pallas_call(tile_kernel, out_shape=(jax.ShapeDtypeStruct(pair_input.sh...]
  transfers between devices with their start and end apart: 10 -> 4, of which waited for: 6 -> 2; matrix products, arithmetic and copies ran while one was open for 1% -> 0% of each run, Pallas kernels for 0% -> 0%
where the time goes in v1:
time: 72.2 us; the launch traced here: 71.7 us
  blocking collectives  44.6 us (62%)
  Pallas kernels  13.8 us (19%)
  starting transfers between devices  5.05 us (7%)
  local copies, waits for them, and re-layouts  3.46 us (5%)
  waiting for transfers between devices  2.94 us (4%)
  other arithmetic  1.17 us (2%)
    all_to_all x1, blocking collectives, body(): pieces = lax.all_to_all(part.reshape(chips, piece, channels), CHIPS, 0, 0)  18.1 us
    all_gather x2, blocking collectives, body(): edges, features = lax.all_gather((edges, bin_features), ROW, axis=0)  13.9 us
    all_to_all x1, blocking collectives, body(): lax.all_to_all(jnp.broadcast_to(total, (chips, piece, channels)), CHIPS,...  12.6 us
    pallas_call x1, Pallas kernels, body(): pl.pallas_call(tile_kernel, out_shape=(jax.ShapeDtypeStruct(pair_input.sh...  8.89 us
    ppermute x1, starting transfers between devices, body(): from_low = lax.ppermute(to_high, 'col', up)  3.41 us
    pallas_call x1, Pallas kernels, body(): pl.pallas_call(finish_kernel, out_shape=(jax.ShapeDtypeStruct(bin_feature...  2.8 us
    pallas_call x1, Pallas kernels, body(): pl.pallas_call(column_kernel, grid=(1,), out_shape=(side, side), in_specs...  2.09 us
    unnamed x10, local copies, waits for them, and re-layouts  1.93 us
  transfers between devices with their start and end apart: 4, of which 2 were waited for; matrix products, arithmetic and copies ran while one was open for 0% of the time, Pallas kernels for 0%

profile of v1, /device:TPU:0, one launch (start us, length us, event | category | flops | bytes accessed | tf_op | source)
XLA Modules:
  0.0 71.7 jit_solution(17573617527350038610)
XLA Ops:
  0.6 0.7 %fusion.1 = (bf16[1,48,128]{2,1,0:T(8,128)(2,1)S(1)}, bf16[1,48,128]{2,1,0:T(8,128)(2,1)S(1)}) fusion(bf16[48,48,128]{2,1,0:T(8,128)(2,1)} %cot.1), kind=kLoop, calls=%fused_computation.3 | loop fusion | bytes 49152 | tf_op jit(solution)/shard_map/slice | solution.py:258
  1.4 0.8 %fusion = (bf16[2,48,128]{2,1,0:T(8,128)(2,1)S(1)}, bf16[2,48,128]{2,1,0:T(8,128)(2,1)S(1)}) fusion(bf16[48,48,128]{2,1,0:T(8,128)(2,1)} %pair.1), kind=kLoop, calls=%fused_computation.2 | loop fusion | bytes 98304 | tf_op jit(solution)/shard_map/slice | solution.py:258
  2.1 7.8 %all-gather = bf16[24,48,128]{2,1,0:T(8,128)(2,1)} all-gather(bf16[6,48,128]{2,1,0:T(8,128)(2,1)S(1)} %pad_maximum_fusion), channel_id=2, replica_groups=mesh['rx'=2,'core'=2,'col'=8] {'rx','core'}, dimensions={0}, use_global_device_ids=true | all-gather | bytes 368640 | tf_op jit(solution)/shard_map/all_gather | solution.py:260
  10.0 0.0 copy-start.2
  10.0 2.1 %columns.1 = (bf16[3,64,128]{2,1,0:T(8,128)(2,1)}, bf16[3,64,128]{2,1,0:T(8,128)(2,1)}) custom-call(bf16[48,48,128]{2,1,0:T(8,128)(2,1)} %pair.1, bf16[48,48,128]{2,1,0:T(8,128)(2,1)} %pair.1, bf16[48,48,128]{2,1,0:T(8,128)(2,1)} %cot.1, bf16[48,48,128]{2,1,0:T(8,128)(2,1)} %cot.1, bf16[4,6,48,128]{3,2,1,0:T(8,128)(2,1)} %bitcast.3), custom_call_target="tpu_custom_call" | custom-call | tf_op jit(solution)/shard_map/columns/pallas_call | solution.py:267
  12.0 3.4 %collective-permute-start = (bf16[3,64,128]{2,1,0:T(8,128)(2,1)}, bf16[3,64,128]{2,1,0:T(8,128)(2,1)S(1)}, u32[]{:S(2)}, u32[]{:S(2)}) collective-permute-start(bf16[3,64,128]{2,1,0:T(8,128)(2,1)} %get-tuple-element.14), channel_id=1, source_target_pairs={{0,1},{1,2},{2,3},{3,4},{4,5},{5,6},{6,7},{8,9},{9,10},{10,11},{11... | collective-permute-start | bytes 147464 | tf_op jit(solution)/shard_map/ppermute | solution.py:278
  15.5 1.3 %collective-permute-start.1 = (bf16[3,64,128]{2,1,0:T(8,128)(2,1)}, bf16[3,64,128]{2,1,0:T(8,128)(2,1)S(1)}, u32[]{:S(2)}, u32[]{:S(2)}) collective-permute-start(bf16[3,64,128]{2,1,0:T(8,128)(2,1)} %get-tuple-element.15), channel_id=1, source_target_pairs={{1,0},{2,1},{3,2},{4,3},{5,4},{6,5},{7,6},{9,8},{10,9},{11,10},{12... | collective-permute-start | bytes 147464 | tf_op jit(solution)/shard_map/ppermute | solution.py:279
  16.8 0.0 copy-done.2
  16.8 6.1 %all-gather.1.features = bf16[192,512]{1,0:T(8,128)(2,1)} all-gather(bf16[48,512]{1,0:T(8,128)(2,1)S(1)} %copy-done.2), channel_id=3, replica_groups=mesh['rx'=2,'core'=2,'col'=8] {'rx','core'}, dimensions={0}, use_global_device_ids=true | all-gather | bytes 245760 | tf_op jit(solution)/shard_map/all_gather | solution.py:260
  22.8 0.0 collective-permute-done.low
  22.8 0.0 collective-permute-done.1.high
  22.8 0.6 copy-done.3
  23.4 0.6 copy-done.4
  24.1 8.9 %tile.1 = (bf16[48,48,128]{2,1,0:T(8,128)(2,1)}, bf16[48,48,128]{2,1,0:T(8,128)(2,1)}, f32[1024,128]{1,0:T(8,128)}, bf16[1024,128]{1,0:T(8,128)(2,1)}) custom-call(s32[576]{0:T(1024)} %valid.1, bf16[48,48,128]{2,1,0:T(8,128)(2,1)} %pair.1, bf16[48,48,128]{2,1,0:T(8,128)(2,1)} %cot.1, bf16[3,64,128]{2,1,0:T(8,128)(2,1)} %copy-done.3, ...), custom_call_target="tpu_custom_call" | custom-call | tf_op jit(solution)/shard_map/tile/pallas_call | solution.py:285
  33.0 0.3 collective-permute-start.2
  33.3 1.4 %collective-permute-done.2 = bf16[1024,128]{1,0:T(8,128)(2,1)S(1)} collective-permute-done((bf16[1024,128]{1,0:T(8,128)(2,1)}, bf16[1024,128]{1,0:T(8,128)(2,1)S(1)}, u32[]{:S(2)}, u32[]{:S(2)}) %collective-permute-start.2) | collective-permute-done | bytes 262176 | tf_op jit(solution)/shard_map/ppermute | solution.py:317
  34.7 1.1 %add_convert_fusion = bf16[1024,128]{1,0:T(8,128)(2,1)S(1)} fusion(f32[1024,128]{1,0:T(8,128)} %get-tuple-element.18, bf16[1024,128]{1,0:T(8,128)(2,1)S(1)} %collective-permute-done.2), kind=kLoop, calls=%fused_computation | loop fusion | flops 393216 | bytes 1048576 | tf_op jit(solution)/shard_map/convert_element_type | solution.py:317
  35.8 18.1 %all_to_all.10 = bf16[16,64,128]{2,1,0:T(8,128)(2,1)S(1)} all-to-all(bf16[16,64,128]{2,1,0:T(8,128)(2,1)S(1)} %bitcast.7), channel_id=1, replica_groups=mesh['rx'=2,'core'=2,'col'=8] {'rx','col'}, dimensions={0} | all-to-all | bytes 524288 | tf_op jit(solution)/shard_map/all_to_all | solution.py:318
  54.0 12.6 %all_to_all.11 = bf16[16,64,128]{2,1,0:T(8,128)(2,1)S(1)} all-to-all(bf16[16,64,128]{2,1,0:T(8,128)(2,1)S(1)} %broadcast_in_dim.3), channel_id=1, replica_groups=mesh['rx'=2,'core'=2,'col'=8] {'rx','col'}, dimensions={0} | all-to-all | bytes 524288 | tf_op jit(solution)/shard_map/all_to_all | solution.py:320
  66.7 0.0 collective-permute-start.3
  66.7 1.5 %collective-permute-done.3.theirs = bf16[1024,128]{1,0:T(8,128)(2,1)S(1)} collective-permute-done((bf16[1024,128]{1,0:T(8,128)(2,1)S(1)}, bf16[1024,128]{1,0:T(8,128)(2,1)S(1)}, u32[]{:S(2)}, u32[]{:S(2)}) %collective-permute-start.3) | collective-permute-done | bytes 262176 | tf_op jit(solution)/shard_map/ppermute | solution.py:323
  68.2 0.0 copy-done
  68.2 0.7 copy-done.1
  68.9 2.8 %finish.1 = (bf16[48,512]{1,0:T(8,128)(2,1)}, f32[512,256]{1,0:T(8,128)}, f32[9,128,128]{2,1,0:T(8,128)}) custom-call(bf16[1024,128]{1,0:T(8,128)(2,1)} %bitcast.6, bf16[1024,128]{1,0:T(8,128)(2,1)} %copy-done.1, bf16[192,512]{1,0:T(8,128)(2,1)} %all-gather.1.features, bf16[384,512]{1,0:T(8,128)(2,1)} %context.3, bf16[512,256]{1,0:T(8,128)(2,1)} %proj_weight.3), custom_call_target="tpu_custom_call" | custom-call | tf_op jit(solution)/shard_map/finish/pallas_call | solution.py:325
  (7 shorter events, 0.1 us)
Async XLA Ops:
  10.0 6.8 %copy-start.2 = (bf16[48,512]{1,0:T(8,128)(2,1)S(1)}, bf16[48,512]{1,0:T(8,128)(2,1)}, u32[]{:S(2)}) copy-start(bf16[48,512]{1,0:T(8,128)(2,1)} %param.8) | copy-start | bytes 147460
  12.0 10.8 %collective-permute-start = (bf16[3,64,128]{2,1,0:T(8,128)(2,1)}, bf16[3,64,128]{2,1,0:T(8,128)(2,1)S(1)}, u32[]{:S(2)}, u32[]{:S(2)}) collective-permute-start(bf16[3,64,128]{2,1,0:T(8,128)(2,1)} %get-tuple-element.14), channel_id=1, source_target_pairs={{0,1},{1,2},{2,3},{3,4},{4,5},{5,6},{6,7},{8,9},{9,10},{10,11},{11... | collective-permute-start | bytes 147464 | tf_op jit(solution)/shard_map/ppermute | solution.py:278
  15.5 7.4 %collective-permute-start.1 = (bf16[3,64,128]{2,1,0:T(8,128)(2,1)}, bf16[3,64,128]{2,1,0:T(8,128)(2,1)S(1)}, u32[]{:S(2)}, u32[]{:S(2)}) collective-permute-start(bf16[3,64,128]{2,1,0:T(8,128)(2,1)} %get-tuple-element.15), channel_id=1, source_target_pairs={{1,0},{2,1},{3,2},{4,3},{5,4},{6,5},{7,6},{9,8},{10,9},{11,10},{12... | collective-permute-start | bytes 147464 | tf_op jit(solution)/shard_map/ppermute | solution.py:279
  22.8 0.6 copy-start.3
  23.4 0.6 copy-start.4
  33.0 1.7 %collective-permute-start.2 = (bf16[1024,128]{1,0:T(8,128)(2,1)}, bf16[1024,128]{1,0:T(8,128)(2,1)S(1)}, u32[]{:S(2)}, u32[]{:S(2)}) collective-permute-start(bf16[1024,128]{1,0:T(8,128)(2,1)} %get-tuple-element.19), channel_id=1, source_target_pairs={{0,8},{8,0},{1,9},{9,1},{2,10},{10,2},{3,11},{11,3},{4,12},{12,4},... | collective-permute-start | bytes 786440 | tf_op jit(solution)/shard_map/ppermute | solution.py:317
  66.7 1.5 %copy-start = (bf16[16,64,128]{2,1,0:T(8,128)(2,1)}, bf16[16,64,128]{2,1,0:T(8,128)(2,1)S(1)}, u32[]{:S(2)}) copy-start(bf16[16,64,128]{2,1,0:T(8,128)(2,1)S(1)} %all_to_all.11) | copy-start | bytes 786436
  66.7 1.5 %collective-permute-start.3 = (bf16[1024,128]{1,0:T(8,128)(2,1)S(1)}, bf16[1024,128]{1,0:T(8,128)(2,1)S(1)}, u32[]{:S(2)}, u32[]{:S(2)}) collective-permute-start(bf16[1024,128]{1,0:T(8,128)(2,1)S(1)} %bitcast.5), channel_id=1, source_target_pairs={{0,8},{8,0},{1,9},{9,1},{2,10},{10,2},{3,11},{11,3},{4,12},{12,4},... | collective-permute-start | bytes 786440 | tf_op jit(solution)/shard_map/ppermute | solution.py:323
  68.2 0.7 copy-start.1

commit v2 on v1

v2 whole, which is shorter than its diff:
```python
import jax
import jax.numpy as jnp
from jax import lax
from jax.experimental import pallas as pl
from jax.experimental.pallas import tpu as pltpu
from jax.sharding import Mesh, PartitionSpec as P

ROW = ("rx", "core")
CHIPS = ("rx", "col")
BF16 = jnp.bfloat16
F32 = jnp.float32
HALO = 2
EDGES = 2 * HALO + 2
SIDE = 16
MARGIN = 16
PITCH = 64
PAD = 8
WIDE = pltpu.CompilerParams(vmem_limit_bytes=60 * 1024 * 1024)
PARAMS = pltpu.CompilerParams(vmem_limit_bytes=20 * 1024 * 1024)


def pack_kernel(pair, cot, features, packed, sems):
    tile_rows, channels = pair.shape[0], pair.shape[2]
    parts = [
        (pair.at[:HALO], packed.at[:HALO]),
        (pair.at[tile_rows - HALO :], packed.at[HALO : 2 * HALO]),
        (cot.at[:1], packed.at[2 * HALO : 2 * HALO + 1]),
        (cot.at[tile_rows - 1 :], packed.at[2 * HALO + 1 : EDGES]),
    ]
    for part in range(features.shape[1] // channels):
        parts.append((features.at[:, part * channels : (part + 1) * channels], packed.at[EDGES + part]))
    copies = [pltpu.make_async_copy(source, target, sems.at[i]) for i, (source, target) in enumerate(parts)]
    for copy in copies:
        copy.start()
    for copy in copies:
        copy.wait()


def column_kernel(one, other, pair_low, pair_high, cot_low, cot_high, near, to_even, to_odd, work, sides):
    tile_rows, _, channels = pair_low.shape
    band_cols = one.shape[1]
    odd_row = lax.rem(lax.axis_index(ROW), 2)
    near[1 - odd_row] = one[:EDGES]
    near[odd_row] = other[:EDGES]
    rows = tile_rows + 2 * HALO
    taken = work.shape[0] // SIDE
    work[rows * SIDE :, :] = jnp.zeros((work.shape[0] - rows * SIDE, channels), F32)
    for side, pair, cot, start, picks in (
        (0, pair_low, cot_low, 0, (0, 1)),
        (1, pair_high, cot_high, band_cols - SIDE, (SIDE - 2, SIDE - 1)),
    ):
        sides[side, :, taken:, :] = jnp.zeros((3, sides.shape[2] - taken, channels), BF16)
        for tile, first, last, columns, slot in (
            (pair, 0, 3, picks, 0),
            (cot, 4, 5, (picks[side],), 2),
        ):
            depth = HALO if slot == 0 else 1
            for index in range(-HALO, tile_rows + HALO):
                if index < -depth or index >= tile_rows + depth:
                    values = jnp.zeros((SIDE, channels), F32)
                elif 0 <= index < tile_rows:
                    values = tile[index].astype(F32)
                elif index < 0:
                    values = near[0, last + 1 + index, start : start + SIDE].astype(F32)
                else:
                    values = near[1, first + index - tile_rows, start : start + SIDE].astype(F32)
                work[(index + HALO) * SIDE : (index + HALO + 1) * SIDE, :] = values
            for position, column in enumerate(columns):
                sides[side, slot + position, :taken, :] = work[pl.ds(column, taken, stride=SIDE), :].astype(BF16)
    odd_col = lax.rem(lax.axis_index("col"), 2)
    to_even[...] = sides[1 - odd_col]
    to_odd[...] = sides[odd_col]


def prepare_kernel(
    valid, context, proj_weight, conv_weight, *refs
):
    sources, (features, query, key, window, rows_valid, forward, backward, bins) = refs[:-8], refs[-8:]
    channels = query.shape[1]
    all_bins, tail = features.shape[0], context.shape[0]
    row, col = lax.axis_index(ROW), lax.axis_index("col")
    if len(sources) == 1:
        blocks = [(sources[0].at[index], index) for index in range(sources[0].shape[0])]
    else:
        blocks = [(source, lax.bitwise_xor(row, step)) for source, step in zip(sources, (0, 1, 3, 2))]
    tile_rows = sources[0].shape[-2]
    row_start = row * tile_rows
    col_start = row_start + col * (key.shape[0] - 2 * MARGIN - tile_rows)
    bins[:MARGIN, :] = jnp.zeros((MARGIN, bins.shape[1]), BF16)
    for source, index in blocks:
        start = pl.multiple_of(MARGIN + index * tile_rows, 16)
        for part in range(bins.shape[1] // channels):
            bins[pl.ds(start, tile_rows), part * channels : (part + 1) * channels] = source[EDGES + part]
    bins[MARGIN + all_bins : MARGIN + all_bins + tail, :] = context[...]
    bins[MARGIN + all_bins + tail :, :] = jnp.zeros((MARGIN, bins.shape[1]), BF16)
    features[...] = bins[MARGIN : MARGIN + all_bins, :]
    row_bins = bins[pl.ds(pl.multiple_of(row_start, 16), query.shape[0]), :]
    query[...] = jnp.dot(row_bins, proj_weight[:, :channels], preferred_element_type=F32).astype(BF16).astype(F32)
    col_bins = bins[pl.ds(pl.multiple_of(col_start, 16), key.shape[0]), :]
    key[...] = jnp.dot(col_bins, proj_weight[:, channels:], preferred_element_type=F32).astype(BF16).astype(F32)

    flags = jnp.broadcast_to(valid[...].astype(F32).astype(BF16), (channels, all_bins + tail))
    flip = (((1,), (1,)), ((), ()))
    for target, begin, stop in ((window, col_start - MARGIN, all_bins + tail), (rows_valid, row_start - HALO, all_bins)):
        shape = (target.shape[0], all_bins + tail)
        bin_index = lax.broadcasted_iota(jnp.int32, shape, 1)
        chosen = jnp.logical_and(bin_index == lax.broadcasted_iota(jnp.int32, shape, 0) + begin, bin_index < stop)
        target[...] = lax.dot_general(chosen.astype(F32).astype(BF16), flags, flip, preferred_element_type=F32)

    forward[...] = jnp.zeros(forward.shape, BF16)
    backward[...] = jnp.zeros(backward.shape, BF16)
    for tap in range(9):
        row_step, step = tap // 3 - 1, tap % 3
        values = conv_weight[tap]
        turned = values.astype(F32).T.astype(BF16)
        for out in range(2):
            lanes = slice(out * channels, (out + 1) * channels)
            at = ((row_step + 1 + out) * 3 + step) * channels
            forward[at : at + channels, lanes] = values
            at = ((1 - row_step + out) * 3 + step) * channels
            backward[at : at + channels, lanes] = turned


def tile_kernel(
    pair, cot, from_even, from_odd, near, query, key, window, rows_valid, forward, backward,
    pair_output, pair_grad, keep, send,
    sides, mixed, carry, mixed3, carry3, own, skew, totals, output, grad, sems,
):
    tile_rows, band_cols, channels = pair.shape
    row, col = lax.axis_index(ROW), lax.axis_index("col")
    core = lax.axis_index("core")
    all_bins = lax.axis_size(ROW) * tile_rows
    tail = lax.axis_size("col") * band_cols
    row_start = row * tile_rows
    col_start = row_start + col * band_cols
    total_rows = tile_rows + 2 * HALO
    odd_col = lax.rem(col, 2)
    sides[1 - odd_col] = from_even[...]
    sides[odd_col] = from_odd[...]

    def place(index, column):
        return (index + HALO) * PITCH + PAD + column

    def mask_of(index):
        return window[pl.ds(MARGIN + index, band_cols), :] * rows_valid[pl.ds(index + HALO, 1), :]

    def halo_row(tile, index, first, last):
        if index < 0:
            return near[0, last + 1 + index]
        if index >= tile_rows:
            return near[1, first + index - tile_rows]
        return tile[index]

    rest = PITCH - band_cols - PAD
    gap = jnp.zeros((PAD + rest, channels), F32)
    for array in (mixed, carry):
        array[: 2 * PAD, :] = jnp.zeros((2 * PAD, channels), F32)
        for index in range(total_rows):
            begin = PAD + index * PITCH + PAD + band_cols
            array[begin : begin + PAD + rest, :] = gap
    empty = jnp.zeros((band_cols, channels), F32)
    carry[pl.ds(PAD + place(-HALO, 0), band_cols), :] = empty
    carry[pl.ds(PAD + place(tile_rows + 1, 0), band_cols), :] = empty
    for index in range(-HALO, tile_rows + HALO):
        mask = mask_of(index)
        source = halo_row(pair, index, 0, 3).astype(F32)
        value = mask * (source + query[pl.ds(MARGIN + index, 1), :] + key[pl.ds(MARGIN + index, band_cols), :])
        mixed[pl.ds(PAD + place(index, 0), band_cols), :] = value
        if -1 <= index <= tile_rows:
            source = halo_row(cot, index, 4, 5).astype(F32)
            carry[pl.ds(PAD + place(index, 0), band_cols), :] = mask * source
    strided = rows_valid.shape[0]
    has_low = (col > 0).astype(F32)
    has_high = (col < lax.axis_size("col") - 1).astype(F32)
    for column, side, slot, has in (
        (-2, 0, 0, has_low), (-1, 0, 1, has_low), (band_cols, 1, 0, has_high), (band_cols + 1, 1, 1, has_high),
    ):
        begin = MARGIN + column - HALO
        mask = rows_valid[...] * window[pl.ds(begin, strided), :] * has
        value = sides[side, slot, :strided].astype(F32) + query[pl.ds(MARGIN - HALO, strided), :] + key[pl.ds(begin, strided), :]
        mixed[pl.ds(PAD + place(-HALO, column), strided, stride=PITCH), :] = mask * value
        if column in (-1, band_cols):
            value = mask * sides[side, 2, :strided].astype(F32)
            carry[pl.ds(PAD + place(-HALO, column), strided, stride=PITCH), :] = value

    def spread(source, target, first, last, sign):
        for index in range(first, last):
            start = (index + HALO) * PITCH
            for step in range(3):
                target[start : start + PITCH, step * channels : (step + 1) * channels] = source[
                    pl.ds(PAD + start + sign * (step - 1), PITCH), :
                ].astype(BF16)

    def four_rows(source, first, pairs):
        columns = []
        for step in range(4):
            starts = [(first + 2 * index + step - 1 + HALO) * PITCH for index in range(pairs)]
            columns.append(jnp.concatenate([source[start : start + PITCH, :] for start in starts], axis=0))
        return jnp.concatenate(columns, axis=1)

    spread(mixed, mixed3, -HALO, tile_rows + HALO, 1)

    pairs = 5
    for first in range(-1, tile_rows + 1, 2 * pairs):
        conv = jnp.dot(four_rows(mixed3, first, pairs), forward[...], preferred_element_type=F32)
        sigma = jax.nn.sigmoid(conv)
        activated = conv * sigma
        slope = sigma * (1.0 + conv * (1.0 - sigma))
        for offset in range(2 * pairs):
            index = first + offset
            lanes = slice(offset % 2 * channels, (offset % 2 + 1) * channels)
            at = offset // 2 * PITCH
            here = pl.ds(PAD + (index + HALO) * PITCH, PITCH)
            carry[here, :] = carry[here, :] * slope[at : at + PITCH, lanes]
            if 0 <= index < tile_rows:
                output[index] = (
                    pair[index].astype(F32) + mask_of(index) * activated[at + PAD : at + PAD + band_cols, lanes]
                ).astype(BF16)
    write_output = pltpu.make_async_copy(output, pair_output, sems.at[0])
    write_output.start()

    spread(carry, carry3, -1, tile_rows + 1, -1)
    spot = lax.broadcasted_iota(jnp.int32, (PITCH, channels), 0)
    inner = jnp.logical_and(spot >= PAD, spot < PAD + band_cols)
    for index in range(tile_rows):
        begin = (index + HALO) * PITCH
        own[index * PITCH : (index + 1) * PITCH, :] = jnp.where(inner, carry[pl.ds(PAD + begin, PITCH), :], 0.0).astype(BF16)

    totals[...] = jnp.zeros(totals.shape, F32)
    skew[...] = jnp.zeros(skew.shape, F32)
    pairs = 4
    query_at = 9 * channels + all_bins + tail
    query_rows = []
    for first in range(0, tile_rows, 2 * pairs):
        back = jnp.dot(four_rows(carry3, first, pairs), backward[...], preferred_element_type=F32)
        for offset in range(2 * pairs):
            index = first + offset
            lanes = slice(offset % 2 * channels, (offset % 2 + 1) * channels)
            at = offset // 2 * PITCH + PAD
            masked = mask_of(index) * back[at : at + band_cols, lanes]
            grad[index] = (cot[index].astype(F32) + masked).astype(BF16)
            query_rows.append(jnp.sum(masked, axis=0, keepdims=True))
            skew[index % 8, index - index % 8 : index - index % 8 + band_cols, :] += masked
    write_grad = pltpu.make_async_copy(grad, pair_grad, sems.at[1])
    write_grad.start()
    totals[pl.ds(pl.multiple_of(query_at + row_start, 16), tile_rows), :] = jnp.concatenate(query_rows, axis=0)
    reach = tile_rows + band_cols - 8
    for step in range(8):
        totals[pl.ds(9 * channels + col_start + step, reach), :] += skew[step, :reach, :]

    per = 12
    grads = jnp.zeros((channels, 9 * channels), F32)
    for first in range(0, tile_rows, per):
        begin = (first + HALO) * PITCH
        around = jnp.concatenate(
            [mixed3[begin + step * PITCH : begin + (per + step) * PITCH, :] for step in (-1, 0, 1)], axis=1
        )
        grads = grads + lax.dot_general(
            own[first * PITCH : (first + per) * PITCH, :], around, (((0,), (0,)), ((), ())), preferred_element_type=F32
        )
    for tap in range(9):
        totals[tap * channels : (tap + 1) * channels, :] = grads[:, tap * channels : (tap + 1) * channels]
    half = keep.shape[0]
    keep[...] = totals[pl.ds(pl.multiple_of(core * half, half), half), :]
    send[...] = totals[pl.ds(pl.multiple_of((1 - core) * half, half), half), :].astype(BF16)
    write_output.wait()
    write_grad.wait()


def add_kernel(pieces, copies):
    total = pieces[0].astype(F32)
    for index in range(1, pieces.shape[0]):
        total = total + pieces[index].astype(F32)
    copies[...] = jnp.broadcast_to(total.astype(BF16), copies.shape)


def finish_kernel(mine, theirs, features, context, proj_weight, feature_grad, proj_grad, conv_grad, whole):
    core = lax.axis_index("core")
    row = lax.axis_index(ROW)
    half = mine.shape[0]
    channels = mine.shape[1]
    all_bins, tail = features.shape[0], context.shape[0]
    tile_rows = feature_grad.shape[0]
    whole[pl.ds(pl.multiple_of(core * half, half), half), :] = mine[...]
    whole[pl.ds(pl.multiple_of((1 - core) * half, half), half), :] = theirs[...]
    for tap in range(9):
        conv_grad[tap] = whole[tap * channels : (tap + 1) * channels, :].astype(F32).T
    key_at = 9 * channels
    query_at = key_at + all_bins + tail
    flip = (((0,), (0,)), ((), ()))
    own = features[...]
    proj_grad[:, :channels] = lax.dot_general(own, whole[query_at : query_at + all_bins, :], flip, preferred_element_type=F32)
    proj_grad[:, channels:] = lax.dot_general(
        own, whole[key_at : key_at + all_bins, :], flip, preferred_element_type=F32
    ) + lax.dot_general(
        context[...], whole[key_at + all_bins : query_at, :], flip, preferred_element_type=F32
    )
    start = pl.multiple_of(row * tile_rows, 16)
    both = jnp.concatenate(
        [whole[pl.ds(query_at + start, tile_rows), :], whole[pl.ds(key_at + start, tile_rows), :]], axis=1
    )
    feature_grad[...] = lax.dot_general(
        both, proj_weight[...], (((1,), (1,)), ((), ())), preferred_element_type=F32
    ).astype(BF16)


def body(
    pair_input, bin_features, context_features, proj_weight, conv_weight, valid_bins, cotangent
):
    tile_rows, band_cols, channels = pair_input.shape
    width = bin_features.shape[1]
    row_count = lax.axis_size(ROW)
    col_count = lax.axis_size("col")
    all_bins = tile_rows * row_count
    tail = context_features.shape[0]
    chips = row_count * col_count // 2
    side_rows = -(-(tile_rows + 2 * HALO) // 16) * 16
    taken = -(-(tile_rows + 2 * HALO) // 8) * 8
    vmem = pl.BlockSpec(memory_space=pltpu.VMEM)
    anywhere = pl.BlockSpec(memory_space=pl.ANY)

    def shape(*dims, dtype=BF16):
        return jax.ShapeDtypeStruct(dims, dtype)

    layers = EDGES + width // channels
    packed = pl.pallas_call(
        pack_kernel,
        out_shape=shape(layers, tile_rows, channels),
        in_specs=[anywhere] * 3,
        out_specs=vmem,
        scratch_shapes=[pltpu.SemaphoreType.DMA((layers,))],
        compiler_params=WIDE,
        name="pack",
    )(pair_input, cotangent, bin_features)
    other_core = [(0, 1), (1, 0)]
    if row_count == 4:
        one = lax.ppermute(packed, "core", other_core)
        other = lax.ppermute(packed, ROW, [(index, index ^ 3) for index in range(4)])
        sources = [packed, one, other, lax.ppermute(other, "core", other_core)]
    else:
        gathered = lax.all_gather(packed, ROW, axis=0)
        row = lax.axis_index(ROW)
        around = [
            lax.dynamic_index_in_dim(gathered, jnp.clip(index, 0, row_count - 1), 0, keepdims=False)
            for index in (row - 1, row + 1)
        ]
        odd = row % 2 == 1
        one = jnp.where(odd, around[0], around[1])
        other = jnp.where(odd, around[1], around[0])
        sources = [gathered]

    low_side = pl.BlockSpec((tile_rows, SIDE, channels), lambda step: (0, 0, 0))
    high_side = pl.BlockSpec((tile_rows, SIDE, channels), lambda step: (0, band_cols // SIDE - 1, 0))
    side = shape(3, side_rows, channels)
    near, to_even, to_odd = pl.pallas_call(
        column_kernel,
        grid=(1,),
        out_shape=(shape(2, EDGES, tile_rows, channels), side, side),
        in_specs=[vmem, vmem, low_side, high_side, low_side, high_side],
        out_specs=(vmem,) * 3,
        scratch_shapes=[pltpu.VMEM((taken * SIDE, channels), F32), pltpu.VMEM((2, 3, side_rows, channels), BF16)],
        compiler_params=PARAMS,
        name="columns",
    )(one, other, pair_input, pair_input, cotangent, cotangent)
    even_pairs = [(i, i ^ 1) for i in range(col_count) if i ^ 1 < col_count]
    odd_pairs = [(i, ((i + 1) ^ 1) - 1) for i in range(1, col_count) if ((i + 1) ^ 1) - 1 < col_count]
    from_even = lax.ppermute(to_even, "col", even_pairs)
    from_odd = lax.ppermute(to_odd, "col", odd_pairs)

    near_bins = tile_rows + band_cols + 2 * MARGIN
    features, query, key, window, rows_valid, forward, backward = pl.pallas_call(
        prepare_kernel,
        out_shape=(
            shape(all_bins, width),
            shape(tile_rows + 2 * MARGIN, channels, dtype=F32),
            shape(near_bins, channels, dtype=F32),
            shape(near_bins, channels, dtype=F32),
            shape(taken, channels, dtype=F32),
            shape(12 * channels, 2 * channels),
            shape(12 * channels, 2 * channels),
        ),
        in_specs=[vmem] * (4 + len(sources)),
        out_specs=(vmem,) * 7,
        scratch_shapes=[pltpu.VMEM((MARGIN + all_bins + tail + MARGIN, width), BF16)],
        compiler_params=PARAMS,
        name="prepare",
    )(valid_bins.reshape(1, all_bins + tail), context_features, proj_weight, conv_weight, *sources)

    piece = -(-(9 * channels + 2 * all_bins + tail) // (32 * chips)) * 16
    half = piece * chips
    span = (tile_rows + 2 * HALO) * PITCH
    loose = span + PITCH * (taken - tile_rows)
    pair_output, pair_grad, keep, send = pl.pallas_call(
        tile_kernel,
        out_shape=(
            shape(*pair_input.shape),
            shape(*pair_input.shape),
            shape(half, channels, dtype=F32),
            shape(half, channels),
        ),
        in_specs=[vmem] * 11,
        out_specs=(anywhere, anywhere, vmem, vmem),
        scratch_shapes=[
            pltpu.VMEM((2, 3, side_rows, channels), BF16),
            pltpu.VMEM((loose, channels), F32),
            pltpu.VMEM((loose, channels), F32),
            pltpu.VMEM((span, 3 * channels), BF16),
            pltpu.VMEM((span, 3 * channels), BF16),
            pltpu.VMEM((tile_rows * PITCH, channels), BF16),
            pltpu.VMEM((8, tile_rows + band_cols, channels), F32),
            pltpu.VMEM((2 * half, channels), F32),
            pltpu.VMEM(pair_input.shape, BF16),
            pltpu.VMEM(pair_input.shape, BF16),
            pltpu.SemaphoreType.DMA((2,)),
        ],
        compiler_params=PARAMS,
        name="tile",
    )(pair_input, cotangent, from_even, from_odd, near, query, key, window, rows_valid, forward, backward)

    part = (keep + lax.ppermute(send, "core", other_core).astype(F32)).astype(BF16)
    pieces = lax.all_to_all(part.reshape(chips, piece, channels), CHIPS, 0, 0)
    copies = pl.pallas_call(
        add_kernel,
        out_shape=shape(chips, piece, channels),
        in_specs=[vmem],
        out_specs=vmem,
        compiler_params=PARAMS,
        name="add",
    )(pieces)
    mine = lax.all_to_all(copies, CHIPS, 0, 0).reshape(half, channels)
    theirs = lax.ppermute(mine, "core", other_core)

    feature_grad, proj_grad, conv_grad = pl.pallas_call(
        finish_kernel,
        out_shape=(
            shape(*bin_features.shape),
            shape(*proj_weight.shape, dtype=F32),
            shape(*conv_weight.shape, dtype=F32),
        ),
        in_specs=[vmem] * 5,
        out_specs=(vmem,) * 3,
        scratch_shapes=[pltpu.VMEM((2 * half, channels), BF16)],
        compiler_params=PARAMS,
        name="finish",
    )(mine, theirs, features, context_features, proj_weight)
    return (pair_output, pair_grad, feature_grad, proj_grad, conv_grad)


def solution(mesh):
    rows, cols = mesh.shape["row"], mesh.shape["col"]
    split = Mesh(mesh.devices.reshape(rows // 2, 2, cols), ("rx", "core", "col"))
    tile = P(ROW, "col", None)
    in_specs = (tile, P(ROW, None), P(), P(), P(), P(), tile)
    out_specs = (tile, tile, P(ROW, None), P(), P())
    return jax.shard_map(body, mesh=split, in_specs=in_specs, out_specs=out_specs, check_vma=False)
```

time: 72.2 us -> 57.1 us (0.79)
  blocking collectives: 44.6 us -> 33 us
  Pallas kernels: 13.8 us -> 9.1 us
  waiting for transfers between devices: 2.94 us -> 7.46 us
  local copies, waits for them, and re-layouts: 3.46 us -> 0.04 us
  starting transfers between devices: 5.05 us -> 6.41 us
  other arithmetic: 1.17 us -> 0.07 us
    all_gather x2 -> x0, blocking collectives: 13.9 us -> none  [body(): edges, features = lax.all_gather((edges, bin_features), ROW, axis=0)]
    pallas_call x3 -> x6, Pallas kernels: 13.8 us -> 9.1 us  [the longest x1 5.18 us: body(): pl.pallas_call(tile_kernel, out_shape=(shape(*pair_input.shape), shape(*p...]
    ppermute x4 -> x7, waiting for transfers between devices: 2.94 us -> 7.46 us  [the longest x1 3.34 us: body(): lax.ppermute(packed, ROW, [(index, index ^ 3) for index in range(4)])]
    all_to_all x1, blocking collectives: 18.1 us -> 20.5 us  [body(): pieces = lax.all_to_all(part.reshape(chips, piece, channels), CHIPS, 0, 0)]
    unnamed x10 -> x14, local copies, waits for them, and re-layouts: 1.93 us -> 0.04 us
    slice x2 -> x0, local copies, waits for them, and re-layouts: 1.49 us -> none  [the longest x1 0.76 us: body(): pair_input[:2]]
    ppermute x4 -> x7, starting transfers between devices: 5.05 us -> 6.41 us  [the longest x1 2.47 us: body(): from_even = lax.ppermute(to_even, 'col', even_pairs)]
    convert_element_type x1, other arithmetic: 1.11 us -> 0.07 us  [body(): (keep + lax.ppermute(send, 'core', other_core).astype(F32)).astype(BF16)]
  transfers between devices with their start and end apart: 4 -> 7, of which waited for: 2 -> 4; matrix products, arithmetic and copies ran while one was open for 0% -> 0% of each run, Pallas kernels for 0% -> 1%
where the time goes in v2:
time: 57.1 us; the launch traced here: 56.9 us
  blocking collectives  33 us (58%)
  Pallas kernels  9.1 us (16%)
  waiting for transfers between devices  7.46 us (13%)
  starting transfers between devices  6.41 us (11%)
  between operations  0.8 us (1%)
    all_to_all x1, blocking collectives, body(): pieces = lax.all_to_all(part.reshape(chips, piece, channels), CHIPS, 0, 0)  20.5 us
    all_to_all x1, blocking collectives, body(): mine = lax.all_to_all(copies, CHIPS, 0, 0).reshape(half, channels)  12.5 us
    pallas_call x1, Pallas kernels, body(): pl.pallas_call(tile_kernel, out_shape=(shape(*pair_input.shape), shape(*p...  5.18 us
    ppermute x1, waiting for transfers between devices, body(): lax.ppermute(packed, ROW, [(index, index ^ 3) for index in range(4)])  3.34 us
    ppermute x1, starting transfers between devices, body(): from_even = lax.ppermute(to_even, 'col', even_pairs)  2.47 us
    ppermute x1, starting transfers between devices, body(): lax.ppermute(packed, ROW, [(index, index ^ 3) for index in range(4)])  2.44 us
    pallas_call x1, Pallas kernels, body(): pl.pallas_call(pack_kernel, out_shape=shape(layers, tile_rows, channels),...  1.64 us
    pallas_call x1, Pallas kernels, body(): pl.pallas_call(finish_kernel, out_shape=(shape(*bin_features.shape), shap...  1.55 us
  transfers between devices with their start and end apart: 7, of which 4 were waited for; matrix products, arithmetic and copies ran while one was open for 0% of the time, Pallas kernels for 1%

profile of v2, /device:TPU:0, one launch (start us, length us, event | category | flops | bytes accessed | tf_op | source)
XLA Modules:
  0.0 56.9 jit_solution(1925932233021439521)
XLA Ops:
  0.7 1.6 %pack.1.refs_0_ = bf16[10,48,128]{2,1,0:T(8,128)(2,1)} custom-call(bf16[48,48,128]{2,1,0:T(8,128)(2,1)} %pair.3, bf16[48,48,128]{2,1,0:T(8,128)(2,1)} %cot.3, bf16[48,512]{1,0:T(8,128)(2,1)} %features.1), custom_call_target="tpu_custom_call" | custom-call | tf_op jit(solution)/shard_map/pack/pallas_call | solution.py:326
  2.3 0.0 copy-start.2
  2.3 0.0 copy-start.3
  2.3 0.0 copy-start.4
  2.3 0.0 copy-start.5
  2.3 2.4 %collective-permute-start.1 = (bf16[10,48,128]{2,1,0:T(8,128)(2,1)}, bf16[10,48,128]{2,1,0:T(8,128)(2,1)S(1)}, u32[]{:S(2)}, u32[]{:S(2)}) collective-permute-start(bf16[10,48,128]{2,1,0:T(8,128)(2,1)} %pack.1.refs_0_), channel_id=1, source_target_pairs={{0,24},{8,16},{16,8},{24,0},{1,25},{9,17},{17,9},{25,1},{2,26},{10... | collective-permute-start | bytes 368648 | tf_op jit(solution)/shard_map/ppermute | solution.py:338
  4.8 0.7 %collective-permute-start = (bf16[10,48,128]{2,1,0:T(8,128)(2,1)}, bf16[10,48,128]{2,1,0:T(8,128)(2,1)S(1)}, u32[]{:S(2)}, u32[]{:S(2)}) collective-permute-start(bf16[10,48,128]{2,1,0:T(8,128)(2,1)} %pack.1.refs_0_), channel_id=1, source_target_pairs={{0,8},{8,0},{1,9},{9,1},{2,10},{10,2},{3,11},{11,3},{4,12},{12,4},... | collective-permute-start | bytes 368648 | tf_op jit(solution)/shard_map/ppermute | solution.py:337
  5.5 3.3 %collective-permute-done.1.other.refs_2_ = bf16[10,48,128]{2,1,0:T(8,128)(2,1)S(1)} collective-permute-done((bf16[10,48,128]{2,1,0:T(8,128)(2,1)}, bf16[10,48,128]{2,1,0:T(8,128)(2,1)S(1)}, u32[]{:S(2)}, u32[]{:S(2)}) %collective-permute-start.1) | collective-permute-done | bytes 122912 | tf_op jit(solution)/shard_map/ppermute | solution.py:338
  8.8 0.1 collective-permute-start.4
  8.9 0.0 collective-permute-done.one.refs_1_
  8.9 0.0 copy-start.6
  8.9 0.2 columns.1
  9.1 2.5 %collective-permute-start.2 = (bf16[3,64,128]{2,1,0:T(8,128)(2,1)S(1)}, bf16[3,64,128]{2,1,0:T(8,128)(2,1)S(1)}, u32[]{:S(2)}, u32[]{:S(2)}) collective-permute-start(bf16[3,64,128]{2,1,0:T(8,128)(2,1)S(1)} %get-tuple-element.22), channel_id=1, source_target_pairs={{0,1},{1,0},{2,3},{3,2},{4,5},{5,4},{6,7},{7,6},{8,9},{9,8},{10,11... | collective-permute-start | bytes 147464 | tf_op jit(solution)/shard_map/ppermute | solution.py:367
  11.6 0.7 %collective-permute-start.3 = (bf16[3,64,128]{2,1,0:T(8,128)(2,1)S(1)}, bf16[3,64,128]{2,1,0:T(8,128)(2,1)S(1)}, u32[]{:S(2)}, u32[]{:S(2)}) collective-permute-start(bf16[3,64,128]{2,1,0:T(8,128)(2,1)S(1)} %get-tuple-element.23), channel_id=1, source_target_pairs={{1,2},{2,1},{3,4},{4,3},{5,6},{6,5},{9,10},{10,9},{11,12},{12,11},... | collective-permute-start | bytes 147464 | tf_op jit(solution)/shard_map/ppermute | solution.py:368
  12.3 0.5 prepare.1
  12.8 1.1 %collective-permute-done.2.from_even = bf16[3,64,128]{2,1,0:T(8,128)(2,1)S(1)} collective-permute-done((bf16[3,64,128]{2,1,0:T(8,128)(2,1)S(1)}, bf16[3,64,128]{2,1,0:T(8,128)(2,1)S(1)}, u32[]{:S(2)}, u32[]{:S(2)}) %collective-permute-start.2) | collective-permute-done | bytes 49184 | tf_op jit(solution)/shard_map/ppermute | solution.py:367
  13.9 5.2 %tile.1 = (bf16[48,48,128]{2,1,0:T(8,128)(2,1)}, bf16[48,48,128]{2,1,0:T(8,128)(2,1)}, f32[1024,128]{1,0:T(8,128)S(1)}, bf16[1024,128]{1,0:T(8,128)(2,1)S(1)}) custom-call(bf16[48,48,128]{2,1,0:T(8,128)(2,1)S(1)} %copy-done, bf16[48,48,128]{2,1,0:T(8,128)(2,1)S(1)} %copy-done.1, bf16[3,64,128]{2,1,0:T(8,128)(2,1)S(1)} %collective-permute-done.2.from_even, ...), custom_call_target="tpu_custom_call" | custom-call | tf_op jit(solution)/shard_map/tile/pallas_call | solution.py:393
  19.1 0.1 collective-permute-start.5
  19.1 1.5 %collective-permute-done.5 = bf16[1024,128]{1,0:T(8,128)(2,1)S(1)} collective-permute-done((bf16[1024,128]{1,0:T(8,128)(2,1)S(1)}, bf16[1024,128]{1,0:T(8,128)(2,1)S(1)}, u32[]{:S(2)}, u32[]{:S(2)}) %collective-permute-start.5) | collective-permute-done | bytes 262176 | tf_op jit(solution)/shard_map/ppermute | solution.py:420
  20.7 0.1 add_convert_fusion
  20.7 20.5 %all_to_all.10.pieces = bf16[16,64,128]{2,1,0:T(8,128)(2,1)S(1)} all-to-all(bf16[16,64,128]{2,1,0:T(8,128)(2,1)S(1)} %bitcast.4), channel_id=1, replica_groups=mesh['rx'=2,'core'=2,'col'=8] {'rx','col'}, dimensions={0} | all-to-all | bytes 524288 | tf_op jit(solution)/shard_map/all_to_all | solution.py:421
  41.3 12.5 %all_to_all.11 = bf16[16,64,128]{2,1,0:T(8,128)(2,1)S(1)} all-to-all(bf16[16,64,128]{2,1,0:T(8,128)(2,1)S(1)} %add.6), channel_id=1, replica_groups=mesh['rx'=2,'core'=2,'col'=8] {'rx','col'}, dimensions={0} | all-to-all | bytes 524288 | tf_op jit(solution)/shard_map/all_to_all | solution.py:430
  53.8 1.5 %collective-permute-done.6.theirs = bf16[1024,128]{1,0:T(8,128)(2,1)S(1)} collective-permute-done((bf16[1024,128]{1,0:T(8,128)(2,1)S(1)}, bf16[1024,128]{1,0:T(8,128)(2,1)S(1)}, u32[]{:S(2)}, u32[]{:S(2)}) %collective-permute-start.6) | collective-permute-done | bytes 262176 | tf_op jit(solution)/shard_map/ppermute | solution.py:431
  55.3 1.6 %finish.1 = (bf16[48,512]{1,0:T(8,128)(2,1)}, f32[512,256]{1,0:T(8,128)}, f32[9,128,128]{2,1,0:T(8,128)}) custom-call(bf16[1024,128]{1,0:T(8,128)(2,1)S(1)} %bitcast.3, bf16[1024,128]{1,0:T(8,128)(2,1)S(1)} %collective-permute-done.6.theirs, bf16[192,512]{1,0:T(8,128)(2,1)S(1)} %get-tuple-element.35.features, bf16[384,512]{1,0:T(8,128)(2,1)S(1)} %copy-done.2, ...), custom_call_target="tpu_custom_call" | custom-call | tf_op jit(solution)/shard_map/finish/pallas_call | solution.py:433
  (14 shorter events, 0.1 us)
Async XLA Ops:
  0.6 8.3 %copy-start.1 = (bf16[48,48,128]{2,1,0:T(8,128)(2,1)S(1)}, bf16[48,48,128]{2,1,0:T(8,128)(2,1)}, u32[]{:S(2)}) copy-start(bf16[48,48,128]{2,1,0:T(8,128)(2,1)} %cot.3) | copy-start | bytes 1769476
  0.6 8.3 %copy-start = (bf16[48,48,128]{2,1,0:T(8,128)(2,1)S(1)}, bf16[48,48,128]{2,1,0:T(8,128)(2,1)}, u32[]{:S(2)}) copy-start(bf16[48,48,128]{2,1,0:T(8,128)(2,1)} %pair.3) | copy-start | bytes 1769476
  2.3 10.0 %copy-start.2 = (bf16[384,512]{1,0:T(8,128)(2,1)S(1)}, bf16[384,512]{1,0:T(8,128)(2,1)}, u32[]{:S(2)}) copy-start(bf16[384,512]{1,0:T(8,128)(2,1)} %context.3) | copy-start | bytes 1179652
  2.3 10.0 %copy-start.3 = (bf16[512,256]{1,0:T(8,128)(2,1)S(1)}, bf16[512,256]{1,0:T(8,128)(2,1)}, u32[]{:S(2)}) copy-start(bf16[512,256]{1,0:T(8,128)(2,1)} %proj_weight.3) | copy-start | bytes 786436
  2.3 10.0 %copy-start.4 = (bf16[10,48,128]{2,1,0:T(8,128)(2,1)S(1)}, bf16[10,48,128]{2,1,0:T(8,128)(2,1)}, u32[]{:S(2)}) copy-start(bf16[10,48,128]{2,1,0:T(8,128)(2,1)} %pack.1.refs_0_) | copy-start | bytes 368644
  2.3 10.0 %copy-start.5 = (bf16[9,128,128]{2,1,0:T(8,128)(2,1)S(1)}, bf16[9,128,128]{2,1,0:T(8,128)(2,1)}, u32[]{:S(2)}) copy-start(bf16[9,128,128]{2,1,0:T(8,128)(2,1)} %conv_weight.1) | copy-start | bytes 884740
  2.3 6.5 %collective-permute-start.1 = (bf16[10,48,128]{2,1,0:T(8,128)(2,1)}, bf16[10,48,128]{2,1,0:T(8,128)(2,1)S(1)}, u32[]{:S(2)}, u32[]{:S(2)}) collective-permute-start(bf16[10,48,128]{2,1,0:T(8,128)(2,1)} %pack.1.refs_0_), channel_id=1, source_target_pairs={{0,24},{8,16},{16,8},{24,0},{1,25},{9,17},{17,9},{25,1},{2,26},{10... | collective-permute-start | bytes 368648 | tf_op jit(solution)/shard_map/ppermute | solution.py:338
  4.8 4.1 %collective-permute-start = (bf16[10,48,128]{2,1,0:T(8,128)(2,1)}, bf16[10,48,128]{2,1,0:T(8,128)(2,1)S(1)}, u32[]{:S(2)}, u32[]{:S(2)}) collective-permute-start(bf16[10,48,128]{2,1,0:T(8,128)(2,1)} %pack.1.refs_0_), channel_id=1, source_target_pairs={{0,8},{8,0},{1,9},{9,1},{2,10},{10,2},{3,11},{11,3},{4,12},{12,4},... | collective-permute-start | bytes 368648 | tf_op jit(solution)/shard_map/ppermute | solution.py:337
  8.8 3.5 %collective-permute-start.4 = (bf16[10,48,128]{2,1,0:T(8,128)(2,1)S(1)}, bf16[10,48,128]{2,1,0:T(8,128)(2,1)S(1)}, u32[]{:S(2)}, u32[]{:S(2)}) collective-permute-start(bf16[10,48,128]{2,1,0:T(8,128)(2,1)S(1)} %collective-permute-done.1.other.refs_2_), channel_id=1, source_target_pairs={{0,8},{8,0},{1,9},{9,1},{2,10},{10,2},{3,11},{11,3},{4,12},{12,4},... | collective-permute-start | bytes 368648 | tf_op jit(solution)/shard_map/ppermute | solution.py:339
  8.9 3.3 %copy-start.6 = (s32[576]{0:T(1024)S(1)}, s32[576]{0:T(1024)}, u32[]{:S(2)}) copy-start(s32[576]{0:T(1024)} %param.12) | copy-start | bytes 6916
  9.1 4.7 %collective-permute-start.2 = (bf16[3,64,128]{2,1,0:T(8,128)(2,1)S(1)}, bf16[3,64,128]{2,1,0:T(8,128)(2,1)S(1)}, u32[]{:S(2)}, u32[]{:S(2)}) collective-permute-start(bf16[3,64,128]{2,1,0:T(8,128)(2,1)S(1)} %get-tuple-element.22), channel_id=1, source_target_pairs={{0,1},{1,0},{2,3},{3,2},{4,5},{5,4},{6,7},{7,6},{8,9},{9,8},{10,11... | collective-permute-start | bytes 147464 | tf_op jit(solution)/shard_map/ppermute | solution.py:367
  11.6 2.3 %collective-permute-start.3 = (bf16[3,64,128]{2,1,0:T(8,128)(2,1)S(1)}, bf16[3,64,128]{2,1,0:T(8,128)(2,1)S(1)}, u32[]{:S(2)}, u32[]{:S(2)}) collective-permute-start(bf16[3,64,128]{2,1,0:T(8,128)(2,1)S(1)} %get-tuple-element.23), channel_id=1, source_target_pairs={{1,2},{2,1},{3,4},{4,3},{5,6},{6,5},{9,10},{10,9},{11,12},{12,11},... | collective-permute-start | bytes 147464 | tf_op jit(solution)/shard_map/ppermute | solution.py:368
  19.1 1.6 %collective-permute-start.5 = (bf16[1024,128]{1,0:T(8,128)(2,1)S(1)}, bf16[1024,128]{1,0:T(8,128)(2,1)S(1)}, u32[]{:S(2)}, u32[]{:S(2)}) collective-permute-start(bf16[1024,128]{1,0:T(8,128)(2,1)S(1)} %get-tuple-element.34), channel_id=1, source_target_pairs={{0,8},{8,0},{1,9},{9,1},{2,10},{10,2},{3,11},{11,3},{4,12},{12,4},... | collective-permute-start | bytes 786440 | tf_op jit(solution)/shard_map/ppermute | solution.py:420
  53.8 1.5 %collective-permute-start.6 = (bf16[1024,128]{1,0:T(8,128)(2,1)S(1)}, bf16[1024,128]{1,0:T(8,128)(2,1)S(1)}, u32[]{:S(2)}, u32[]{:S(2)}) collective-permute-start(bf16[1024,128]{1,0:T(8,128)(2,1)S(1)} %bitcast.2), channel_id=1, source_target_pairs={{0,8},{8,0},{1,9},{9,1},{2,10},{10,2},{3,11},{11,3},{4,12},{12,4},... | collective-permute-start | bytes 786440 | tf_op jit(solution)/shard_map/ppermute | solution.py:431

commit v3 on v2

v3 whole, which is shorter than its diff:
```python
import jax
import jax.numpy as jnp
from jax import lax
from jax.experimental import pallas as pl
from jax.experimental.pallas import tpu as pltpu
from jax.sharding import Mesh, PartitionSpec as P

ROW = ("rx", "core")
CHIPS = ("rx", "col")
BF16 = jnp.bfloat16
F32 = jnp.float32
HALO = 2
EDGES = HALO + 1
SIDE = 16
MARGIN = 16
PITCH = 64
PAD = 8
PARAMS = pltpu.CompilerParams(vmem_limit_bytes=20 * 1024 * 1024)


def pack_kernel(
    pair, cot, features, to_core, to_chip, to_even, to_odd, pair_low, pair_high, cot_low, cot_high, work, sides, sems
):
    tile_rows, band_cols, channels = pair.shape
    odd_row = lax.rem(lax.axis_index(ROW), 2)
    odd_col = lax.rem(lax.axis_index("col"), 2)
    parts = []
    for target, at_end in ((to_chip, odd_row), (to_core, 1 - odd_row)):
        parts.append((pair.at[pl.ds(at_end * (tile_rows - HALO), HALO)], target.at[:HALO]))
        parts.append((cot.at[pl.ds(at_end * (tile_rows - 1), 1)], target.at[HALO:EDGES]))
        for part in range(features.shape[1] // channels):
            parts.append((features.at[:, part * channels : (part + 1) * channels], target.at[EDGES + part]))
    parts.append((pair.at[:, :SIDE], pair_low))
    parts.append((pair.at[:, band_cols - SIDE :], pair_high))
    parts.append((cot.at[:, :SIDE], cot_low))
    parts.append((cot.at[:, band_cols - SIDE :], cot_high))
    copies = [pltpu.make_async_copy(source, target, sems.at[i]) for i, (source, target) in enumerate(parts)]
    for copy in copies[-4:] + copies[:-4]:
        copy.start()
    for copy in copies[-4:]:
        copy.wait()
    for side, (chunk, kind) in enumerate(((pair_low, cot_low), (pair_high, cot_high))):
        for slot, source, column in (
            (0, chunk, side * (SIDE - 2)), (1, chunk, side * (SIDE - 2) + 1), (2, kind, side * (SIDE - 1)),
        ):
            if slot != 1:
                work[...] = source[...].astype(F32).reshape(tile_rows * SIDE, channels)
            sides[side, slot] = work[pl.ds(column, tile_rows, stride=SIDE), :].astype(BF16)
    to_even[...] = sides[1 - odd_col]
    to_odd[...] = sides[odd_col]
    for copy in copies[:-4]:
        copy.wait()


def corner_kernel(from_even, from_odd, sides, to_core, to_chip):
    tile_rows = from_even.shape[1]
    odd_row = lax.rem(lax.axis_index(ROW), 2)
    odd_col = lax.rem(lax.axis_index("col"), 2)
    sides[1 - odd_col] = from_even[...]
    sides[odd_col] = from_odd[...]
    for target, at_end in ((to_chip, odd_row), (to_core, 1 - odd_row)):
        start = pl.multiple_of(at_end * (tile_rows - SIDE), 16)
        target[...] = sides[:, :, pl.ds(start, SIDE), :]


def weights_kernel(
    valid, context, proj_weight, conv_weight,
    window, rows_valid, forward, backward, projection, context_key, context_turned,
):
    channels = window.shape[1]
    bins = valid.shape[0]
    band_total = context.shape[0]
    all_bins = bins - band_total
    tile_rows = all_bins // lax.axis_size(ROW)
    row_start = lax.axis_index(ROW) * tile_rows
    col_start = row_start + lax.axis_index("col") * (band_total // lax.axis_size("col"))
    flags = jnp.broadcast_to(valid[...].reshape(1, bins).astype(F32).astype(BF16), (channels, bins))
    flip = (((1,), (1,)), ((), ()))
    for target, begin, stop in ((window, col_start - MARGIN, bins), (rows_valid, row_start - HALO, all_bins)):
        shape = (target.shape[0], bins)
        bin_index = lax.broadcasted_iota(jnp.int32, shape, 1)
        chosen = jnp.logical_and(bin_index == lax.broadcasted_iota(jnp.int32, shape, 0) + begin, bin_index < stop)
        target[...] = lax.dot_general(chosen.astype(F32).astype(BF16), flags, flip, preferred_element_type=F32)
    forward[...] = jnp.zeros(forward.shape, BF16)
    backward[...] = jnp.zeros(backward.shape, BF16)
    for tap in range(9):
        row_step, step = tap // 3 - 1, tap % 3
        values = conv_weight[tap]
        turned = values.astype(F32).T.astype(BF16)
        for out in range(2):
            lanes = slice(out * channels, (out + 1) * channels)
            at = ((row_step + 1 + out) * 3 + step) * channels
            forward[at : at + channels, lanes] = values
            at = ((1 - row_step + out) * 3 + step) * channels
            backward[at : at + channels, lanes] = turned
    projection[...] = proj_weight[...]
    context_key[...] = jnp.dot(context[...], proj_weight[:, channels:], preferred_element_type=F32).astype(BF16)
    context_turned[...] = context[...].astype(F32).T.astype(BF16)


def prepare_kernel(projection, context_key, *refs):
    sources, (features_turned, query, key, features, query_rows, key_rows) = refs[:-6], refs[-6:]
    channels = query.shape[1]
    all_bins, tail = features.shape[0], context_key.shape[0]
    row, col = lax.axis_index(ROW), lax.axis_index("col")
    if len(sources) == 1:
        features[...] = sources[0][...]
    else:
        for source, step in zip(sources, (0, 1, 3, 2)):
            rows = source.shape[1]
            start = pl.multiple_of(lax.bitwise_xor(row, step) * rows, 16)
            for part in range(source.shape[0] - EDGES):
                features[pl.ds(start, rows), part * channels : (part + 1) * channels] = source[EDGES + part]
    tile_rows = query.shape[0] - 2 * MARGIN
    row_start = row * tile_rows
    col_start = row_start + col * (key.shape[0] - 2 * MARGIN - tile_rows)
    proj = jnp.dot(features[...], projection[...], preferred_element_type=F32).astype(BF16).astype(F32)
    margin = jnp.zeros((MARGIN, channels), F32)
    for target, size in ((query_rows, all_bins), (key_rows, all_bins + tail)):
        target[:MARGIN, :] = margin
        target[MARGIN + size :, :] = margin
    query_rows[MARGIN : MARGIN + all_bins, :] = proj[:, :channels]
    key_rows[MARGIN : MARGIN + all_bins, :] = proj[:, channels:]
    key_rows[MARGIN + all_bins : MARGIN + all_bins + tail, :] = context_key[...].astype(F32)
    query[...] = query_rows[pl.ds(pl.multiple_of(row_start, 16), query.shape[0]), :]
    key[...] = key_rows[pl.ds(pl.multiple_of(col_start, 16), key.shape[0]), :]
    features_turned[...] = features[...].astype(F32).T.astype(BF16)


def spread(source, target, first, last, base, sign):
    channels = source.shape[1]
    for index in range(first, last):
        start = (index - base) * PITCH
        for step in range(3):
            target[start : start + PITCH, step * channels : (step + 1) * channels] = source[
                pl.ds(PAD + start + sign * (step - 1), PITCH), :
            ].astype(BF16)


def rows_of(sources, index):
    for array, base, held in sources:
        if index in held:
            return array[(index - base) * PITCH : (index - base + 1) * PITCH, :]
    raise IndexError(index)


def four_rows(sources, first, pairs):
    columns = []
    for step in range(4):
        parts = [rows_of(sources, first + 2 * index + step - 1) for index in range(pairs)]
        columns.append(jnp.concatenate(parts, axis=0))
    return jnp.concatenate(columns, axis=1)


def silu_parts(conv):
    sigma = jax.nn.sigmoid(conv)
    return conv * sigma, sigma * (1.0 + conv * (1.0 - sigma))


def has_sides():
    col = lax.axis_index("col")
    return (col > 0).astype(F32), (col < lax.axis_size("col") - 1).astype(F32)


def keep_inner(values, band_cols):
    spot = lax.broadcasted_iota(jnp.int32, values.shape, 0)
    inner = jnp.logical_and(spot >= PAD, spot < PAD + band_cols)
    return jnp.where(inner, values, 0.0).astype(BF16)


def inner_kernel(
    pair, cot, sides, query, key, window, rows_valid, forward,
    mixed3, carry3, own, output,
    mixed, carry,
):
    tile_rows, band_cols, channels = pair.shape

    def place(index, column):
        return PAD + index * PITCH + PAD + column

    def mask_of(index):
        return window[pl.ds(MARGIN + index, band_cols), :] * rows_valid[pl.ds(index + HALO, 1), :]

    gap = jnp.zeros((PITCH - band_cols, channels), F32)
    mixed[:PAD, :] = jnp.zeros((PAD, channels), F32)
    mixed[PAD : 2 * PAD, :] = jnp.zeros((PAD, channels), F32)
    for index in range(tile_rows):
        mixed[pl.ds(place(index, band_cols), PITCH - band_cols), :] = gap
        carry[pl.ds(place(index, band_cols), PITCH - band_cols), :] = gap
    for index in range(tile_rows):
        mask = mask_of(index)
        value = mask * (
            pair[index].astype(F32) + query[pl.ds(MARGIN + index, 1), :] + key[pl.ds(MARGIN + index, band_cols), :]
        )
        mixed[pl.ds(place(index, 0), band_cols), :] = value
        carry[pl.ds(place(index, 0), band_cols), :] = mask * cot[index].astype(F32)
    has_low, has_high = has_sides()
    for column, side, slot, has in (
        (-2, 0, 0, has_low), (-1, 0, 1, has_low), (band_cols, 1, 0, has_high), (band_cols + 1, 1, 1, has_high),
    ):
        begin = MARGIN + column
        mask = rows_valid[pl.ds(HALO, tile_rows), :] * window[pl.ds(begin, tile_rows), :] * has
        value = sides[side, slot].astype(F32) + query[pl.ds(MARGIN, tile_rows), :] + key[pl.ds(begin, tile_rows), :]
        mixed[pl.ds(place(0, column), tile_rows, stride=PITCH), :] = mask * value
        if column in (-1, band_cols):
            carry[pl.ds(place(0, column), tile_rows, stride=PITCH), :] = mask * sides[side, HALO].astype(F32)
    spread(mixed, mixed3, 0, tile_rows, 0, 1)

    first, last = 1, tile_rows - 1
    sources = [(mixed3, 0, range(tile_rows))]
    while first < last:
        pairs = min(5, (last - first) // 2)
        conv = jnp.dot(four_rows(sources, first, pairs), forward[...], preferred_element_type=F32)
        activated, slope = silu_parts(conv)
        for offset in range(2 * pairs):
            index = first + offset
            lanes = slice(offset % 2 * channels, (offset % 2 + 1) * channels)
            at = offset // 2 * PITCH
            here = pl.ds(PAD + index * PITCH, PITCH)
            values = carry[here, :] * slope[at : at + PITCH, lanes]
            carry[here, :] = values
            own[index * PITCH : (index + 1) * PITCH, :] = keep_inner(values, band_cols)
            output[index] = (
                pair[index].astype(F32) + mask_of(index) * activated[at + PAD : at + PAD + band_cols, lanes]
            ).astype(BF16)
        first += 2 * pairs
    spread(carry, carry3, 1, tile_rows - 1, 0, -1)


def outer_kernel(
    pair, cot, from_core, from_chip, sides, corner_core, corner_chip, query, key, window, rows_valid, forward, backward,
    mixed3, carry3, own, output,
    pair_output, pair_grad, keep, send,
    near, corners, mixed, carry, mixed3_ends, carry3_ends, own_ends, output_ends, skew, totals, grad, sems,
):
    tile_rows, band_cols, channels = pair.shape
    row, col = lax.axis_index(ROW), lax.axis_index("col")
    core = lax.axis_index("core")
    all_bins = lax.axis_size(ROW) * tile_rows
    tail = lax.axis_size("col") * band_cols
    row_start = row * tile_rows
    col_start = row_start + col * band_cols
    odd_row = lax.rem(row, 2)
    last = tile_rows - 1
    write_output = pltpu.make_async_copy(output.at[1:last], pair_output.at[1:last], sems.at[0])
    write_output.start()
    near[1 - odd_row] = from_core[:EDGES]
    near[odd_row] = from_chip[:EDGES]
    corners[1 - odd_row] = corner_core[...]
    corners[odd_row] = corner_chip[...]

    def place(position, column):
        return PAD + position * PITCH + PAD + column

    def mask_of(index):
        return window[pl.ds(MARGIN + index, band_cols), :] * rows_valid[pl.ds(index + HALO, 1), :]

    has = has_sides()
    mixed_rows = (-2, -1, tile_rows, tile_rows + 1)
    carry_rows = (-1, 0, last, tile_rows)
    gap = jnp.zeros((PITCH - band_cols, channels), F32)
    for array in (mixed, carry):
        array[: 2 * PAD, :] = jnp.zeros((2 * PAD, channels), F32)
        for position in range(4):
            array[pl.ds(place(position, band_cols), PITCH - band_cols), :] = gap

    def corner_of(index, side, slot):
        if index < 0:
            return corners[0, side, slot].astype(F32)[SIDE + index : SIDE + index + 1, :]
        return corners[1, side, slot].astype(F32)[index - tile_rows : index - tile_rows + 1, :]

    def pixel_mask(index, column, side):
        return rows_valid[pl.ds(index + HALO, 1), :] * window[pl.ds(MARGIN + index + column, 1), :] * has[side]

    for position, index in enumerate(mixed_rows):
        source = near[0, HALO + index] if index < 0 else near[1, index - tile_rows]
        row_query = query[pl.ds(MARGIN + index, 1), :]
        mixed[pl.ds(place(position, 0), band_cols), :] = mask_of(index) * (
            source.astype(F32) + row_query + key[pl.ds(MARGIN + index, band_cols), :]
        )
        for column, side, slot in ((-2, 0, 0), (-1, 0, 1), (band_cols, 1, 0), (band_cols + 1, 1, 1)):
            value = corner_of(index, side, slot) + row_query + key[pl.ds(MARGIN + index + column, 1), :]
            mixed[pl.ds(place(position, column), 1), :] = pixel_mask(index, column, side) * value
    for position, index in enumerate(carry_rows):
        source = near[0, HALO] if index < 0 else near[1, HALO] if index > last else cot[index]
        carry[pl.ds(place(position, 0), band_cols), :] = mask_of(index) * source.astype(F32)
        for column, side in ((-1, 0), (band_cols, 1)):
            if 0 <= index <= last:
                chunk = index // SIDE * SIDE
                value = sides[side, HALO, chunk : chunk + SIDE].astype(F32)[index - chunk : index - chunk + 1, :]
            else:
                value = corner_of(index, side, HALO)
            carry[pl.ds(place(position, column), 1), :] = pixel_mask(index, column, side) * value
    spread(mixed, mixed3_ends, 0, 4, 0, 1)
    mixed_sources = [
        (mixed3, 0, range(tile_rows)), (mixed3_ends, -2, (-2, -1)), (mixed3_ends, tile_rows - 2, (tile_rows, tile_rows + 1)),
    ]
    ends = jnp.concatenate([four_rows(mixed_sources, -1, 1), four_rows(mixed_sources, last, 1)], axis=0)
    activated, slope = silu_parts(jnp.dot(ends, forward[...], preferred_element_type=F32))
    for position, index in enumerate(carry_rows):
        lanes = slice(position % 2 * channels, (position % 2 + 1) * channels)
        at = position // 2 * PITCH
        here = pl.ds(PAD + position * PITCH, PITCH)
        values = carry[here, :] * slope[at : at + PITCH, lanes]
        carry[here, :] = values
        if 0 <= index <= last:
            half = position // 2
            own_ends[half * PITCH : (half + 1) * PITCH, :] = keep_inner(values, band_cols)
            output_ends[half] = (
                pair[index].astype(F32) + mask_of(index) * activated[at + PAD : at + PAD + band_cols, lanes]
            ).astype(BF16)
    spread(carry, carry3_ends, 0, 4, 0, -1)
    write_first = pltpu.make_async_copy(output_ends.at[0], pair_output.at[0], sems.at[1])
    write_last = pltpu.make_async_copy(output_ends.at[1], pair_output.at[last], sems.at[2])
    write_first.start()
    write_last.start()
    carry_sources = [
        (carry3, 0, range(1, last)), (carry3_ends, -1, (-1, 0)), (carry3_ends, tile_rows - 3, (last, tile_rows)),
    ]
    own_sources = [(own, 0, range(1, last)), (own_ends, 0, (0,)), (own_ends, tile_rows - 2, (last,))]

    totals[...] = jnp.zeros(totals.shape, F32)
    skew[...] = jnp.zeros(skew.shape, F32)
    pairs = 4
    query_at = 9 * channels + all_bins + tail
    query_rows = []
    for first in range(0, tile_rows, 2 * pairs):
        back = jnp.dot(four_rows(carry_sources, first, pairs), backward[...], preferred_element_type=F32)
        for offset in range(2 * pairs):
            index = first + offset
            lanes = slice(offset % 2 * channels, (offset % 2 + 1) * channels)
            at = offset // 2 * PITCH + PAD
            masked = mask_of(index) * back[at : at + band_cols, lanes]
            grad[index] = (cot[index].astype(F32) + masked).astype(BF16)
            query_rows.append(jnp.sum(masked, axis=0, keepdims=True))
            skew[index % 8, index - index % 8 : index - index % 8 + band_cols, :] += masked
    write_grad = pltpu.make_async_copy(grad, pair_grad, sems.at[3])
    write_grad.start()
    totals[pl.ds(pl.multiple_of(query_at + row_start, 16), tile_rows), :] = jnp.concatenate(query_rows, axis=0)
    reach = tile_rows + band_cols - 8
    for step in range(8):
        totals[pl.ds(9 * channels + col_start + step, reach), :] += skew[step, :reach, :]

    per = 12
    grads = jnp.zeros((channels, 9 * channels), F32)
    for first in range(0, tile_rows, per):
        around = jnp.concatenate(
            [
                jnp.concatenate([rows_of(mixed_sources, index + step) for index in range(first, first + per)], axis=0)
                for step in (-1, 0, 1)
            ],
            axis=1,
        )
        cots = jnp.concatenate([rows_of(own_sources, index) for index in range(first, first + per)], axis=0)
        grads = grads + lax.dot_general(cots, around, (((0,), (0,)), ((), ())), preferred_element_type=F32)
    for tap in range(9):
        totals[tap * channels : (tap + 1) * channels, :] = grads[:, tap * channels : (tap + 1) * channels]
    half = keep.shape[0]
    keep[...] = totals[pl.ds(pl.multiple_of(core * half, half), half), :]
    send[...] = totals[pl.ds(pl.multiple_of((1 - core) * half, half), half), :].astype(BF16)
    for copy in (write_output, write_first, write_last, write_grad):
        copy.wait()


def add_kernel(pieces, copies):
    total = pieces[0].astype(F32)
    for index in range(1, pieces.shape[0]):
        total = total + pieces[index].astype(F32)
    copies[...] = jnp.broadcast_to(total.astype(BF16), copies.shape)


def finish_kernel(
    mine, theirs, features_turned, context_turned, projection, feature_grad, proj_grad, conv_grad,
    whole, feature_out, proj_out, conv_out, sems,
):
    core = lax.axis_index("core")
    row = lax.axis_index(ROW)
    half, channels = mine.shape
    all_bins, tail = features_turned.shape[1], context_turned.shape[1]
    tile_rows = feature_grad.shape[0]
    whole[pl.ds(pl.multiple_of(core * half, half), half), :] = mine[...]
    whole[pl.ds(pl.multiple_of((1 - core) * half, half), half), :] = theirs[...]
    copies = [
        pltpu.make_async_copy(source, target, sems.at[index])
        for index, (source, target) in enumerate(((conv_out, conv_grad), (proj_out, proj_grad), (feature_out, feature_grad)))
    ]
    for tap in range(9):
        conv_out[tap] = whole[tap * channels : (tap + 1) * channels, :].astype(F32).T
    copies[0].start()
    key_at = 9 * channels
    query_at = key_at + all_bins + tail
    own = features_turned[...]
    proj_out[:, :channels] = jnp.dot(own, whole[query_at : query_at + all_bins, :], preferred_element_type=F32)
    proj_out[:, channels:] = jnp.dot(
        own, whole[key_at : key_at + all_bins, :], preferred_element_type=F32
    ) + jnp.dot(context_turned[...], whole[key_at + all_bins : query_at, :], preferred_element_type=F32)
    copies[1].start()
    start = pl.multiple_of(row * tile_rows, 16)
    both = jnp.concatenate(
        [whole[pl.ds(query_at + start, tile_rows), :], whole[pl.ds(key_at + start, tile_rows), :]], axis=1
    )
    feature_out[...] = lax.dot_general(
        both, projection[...], (((1,), (1,)), ((), ())), preferred_element_type=F32
    ).astype(BF16)
    copies[2].start()
    for copy in copies:
        copy.wait()


def in_hbm(*arrays):
    return [pltpu.with_memory_space_constraint(array, pltpu.HBM) for array in arrays]


def body(
    pair_input, bin_features, context_features, proj_weight, conv_weight, valid_bins, cotangent
):
    tile_rows, band_cols, channels = pair_input.shape
    width = bin_features.shape[1]
    row_count = lax.axis_size(ROW)
    col_count = lax.axis_size("col")
    all_bins = tile_rows * row_count
    tail = context_features.shape[0]
    chips = row_count * col_count // 2
    taken = -(-(tile_rows + 2 * HALO) // 8) * 8
    vmem = pl.BlockSpec(memory_space=pltpu.VMEM)
    anywhere = pl.BlockSpec(memory_space=pl.ANY)

    def shape(*dims, dtype=BF16):
        return jax.ShapeDtypeStruct(dims, dtype)

    layers = EDGES + width // channels
    chunk = pltpu.VMEM((tile_rows, SIDE, channels), BF16)
    to_core, to_chip, to_even, to_odd = pl.pallas_call(
        pack_kernel,
        out_shape=(
            shape(layers, tile_rows, channels),
            shape(layers, tile_rows, channels),
            shape(EDGES, tile_rows, channels),
            shape(EDGES, tile_rows, channels),
        ),
        in_specs=[anywhere] * 3,
        out_specs=(vmem,) * 4,
        scratch_shapes=[
            chunk, chunk, chunk, chunk,
            pltpu.VMEM((tile_rows * SIDE, channels), F32),
            pltpu.VMEM((2, EDGES, tile_rows, channels), BF16),
            pltpu.SemaphoreType.DMA((2 * layers + 4,)),
        ],
        compiler_params=PARAMS,
        name="pack",
    )(*in_hbm(pair_input, cotangent, bin_features))
    other_core = [(0, 1), (1, 0)]
    even_cols = [(i, i ^ 1) for i in range(col_count) if i ^ 1 < col_count]
    odd_cols = []
    for row in range(row_count):
        for column in range(col_count):
            partner = ((column + 1) ^ 1) - 1
            if 0 <= partner < col_count:
                odd_cols.append((row * col_count + column, row * col_count + partner))
            else:
                odd_cols.append((row * col_count + column, (row ^ 1) * col_count + column))
    odd_rows = [(i, ((i + 1) ^ 1) - 1) for i in range(1, row_count - 1)]
    ends = [(0, 3), (3, 0)] if row_count == 4 else []
    from_chip = lax.ppermute(to_chip, ROW, odd_rows + ends)
    from_odd = lax.ppermute(to_odd, ROW + ("col",), odd_cols)
    from_even = lax.ppermute(to_even, "col", even_cols)
    from_core = lax.ppermute(to_core, "core", other_core)
    near_bins = tile_rows + band_cols + 2 * MARGIN
    valid_bins, from_chip = lax.optimization_barrier((valid_bins, from_chip))
    window, rows_valid, forward, backward, projection, context_key, context_turned = pl.pallas_call(
        weights_kernel,
        out_shape=(
            shape(near_bins, channels, dtype=F32),
            shape(taken, channels, dtype=F32),
            shape(12 * channels, 2 * channels),
            shape(12 * channels, 2 * channels),
            shape(*proj_weight.shape),
            shape(tail, channels),
            shape(width, tail),
        ),
        in_specs=[vmem] * 4,
        out_specs=(vmem,) * 7,
        compiler_params=PARAMS,
        cost_estimate=pl.CostEstimate(flops=1 << 30, bytes_accessed=1 << 21, transcendentals=0),
        name="weights",
    )(*in_hbm(valid_bins, context_features, proj_weight, conv_weight))
    if row_count == 4:
        sources = [to_core, from_core, from_chip, lax.ppermute(from_chip, "core", other_core)]
    else:
        sources = [lax.all_gather(bin_features, ROW, axis=0, tiled=True)]

    features_turned, query, key = pl.pallas_call(
        prepare_kernel,
        out_shape=(
            shape(width, all_bins),
            shape(tile_rows + 2 * MARGIN, channels, dtype=F32),
            shape(near_bins, channels, dtype=F32),
        ),
        in_specs=[vmem] * (2 + len(sources)),
        out_specs=(vmem,) * 3,
        scratch_shapes=[
            pltpu.VMEM((all_bins, width), BF16),
            pltpu.VMEM((all_bins + 2 * MARGIN, channels), F32),
            pltpu.VMEM((all_bins + tail + 2 * MARGIN, channels), F32),
        ],
        compiler_params=PARAMS,
        name="prepare",
    )(projection, context_key, *sources)
    from_even, from_odd, key = lax.optimization_barrier((from_even, from_odd, key))
    corner = shape(2, EDGES, SIDE, channels)
    sides, corner_to_core, corner_to_chip = pl.pallas_call(
        corner_kernel,
        out_shape=(shape(2, EDGES, tile_rows, channels), corner, corner),
        in_specs=[vmem] * 2,
        out_specs=(vmem,) * 3,
        compiler_params=PARAMS,
        name="corners",
    )(from_even, from_odd)
    corner_chip = lax.ppermute(corner_to_chip, ROW, odd_rows + ends)
    corner_core = lax.ppermute(corner_to_core, "core", other_core)


    piece = -(-(9 * channels + 2 * all_bins + tail) // (32 * chips)) * 16
    half = piece * chips
    span = tile_rows * PITCH
    inner = pl.pallas_call(
        inner_kernel,
        out_shape=(
            shape(span, 3 * channels), shape(span, 3 * channels), shape(span, channels), shape(*pair_input.shape),
        ),
        in_specs=[vmem] * 8,
        out_specs=(vmem,) * 4,
        scratch_shapes=[pltpu.VMEM((span + 4 * PAD, channels), F32)] * 2,
        compiler_params=PARAMS,
        name="inner",
    )(pair_input, cotangent, sides, query, key, window, rows_valid, forward)
    pair_output, pair_grad, keep, send = pl.pallas_call(
        outer_kernel,
        out_shape=(
            shape(*pair_input.shape),
            shape(*pair_input.shape),
            shape(half, channels, dtype=F32),
            shape(half, channels),
        ),
        in_specs=[vmem] * 17,
        out_specs=(anywhere, anywhere, vmem, vmem),
        scratch_shapes=[
            pltpu.VMEM((2, EDGES, tile_rows, channels), BF16),
            pltpu.VMEM((2, 2, EDGES, SIDE, channels), BF16),
            pltpu.VMEM((4 * PITCH + 4 * PAD, channels), F32),
            pltpu.VMEM((4 * PITCH + 4 * PAD, channels), F32),
            pltpu.VMEM((4 * PITCH, 3 * channels), BF16),
            pltpu.VMEM((4 * PITCH, 3 * channels), BF16),
            pltpu.VMEM((2 * PITCH, channels), BF16),
            pltpu.VMEM((2, band_cols, channels), BF16),
            pltpu.VMEM((8, tile_rows + band_cols, channels), F32),
            pltpu.VMEM((2 * half, channels), F32),
            pltpu.VMEM(pair_input.shape, BF16),
            pltpu.SemaphoreType.DMA((4,)),
        ],
        compiler_params=PARAMS,
        name="outer",
    )(
        pair_input, cotangent, from_core, from_chip, sides, corner_core, corner_chip, query, key, window, rows_valid,
        forward, backward, *inner,
    )

    part = (keep + lax.ppermute(send, "core", other_core).astype(F32)).astype(BF16)
    pieces = lax.all_to_all(part.reshape(chips, piece, channels), CHIPS, 0, 0)
    copies = pl.pallas_call(
        add_kernel,
        out_shape=shape(chips, piece, channels),
        in_specs=[vmem],
        out_specs=vmem,
        compiler_params=PARAMS,
        name="add",
    )(pieces)
    mine = lax.all_to_all(copies, CHIPS, 0, 0).reshape(half, channels)
    theirs = lax.ppermute(mine, "core", other_core)

    feature_grad, proj_grad, conv_grad = pl.pallas_call(
        finish_kernel,
        out_shape=(
            shape(*bin_features.shape),
            shape(*proj_weight.shape, dtype=F32),
            shape(*conv_weight.shape, dtype=F32),
        ),
        in_specs=[vmem] * 5,
        out_specs=(anywhere,) * 3,
        scratch_shapes=[
            pltpu.VMEM((2 * half, channels), BF16),
            pltpu.VMEM(bin_features.shape, BF16),
            pltpu.VMEM(proj_weight.shape, F32),
            pltpu.VMEM(conv_weight.shape, F32),
            pltpu.SemaphoreType.DMA((3,)),
        ],
        compiler_params=PARAMS,
        name="finish",
    )(mine, theirs, features_turned, context_turned, projection)
    return (pair_output, pair_grad, feature_grad, proj_grad, conv_grad)


def solution(mesh):
    rows, cols = mesh.shape["row"], mesh.shape["col"]
    split = Mesh(mesh.devices.reshape(rows // 2, 2, cols), ("rx", "core", "col"))
    tile = P(ROW, "col", None)
    in_specs = (tile, P(ROW, None), P(), P(), P(), P(), tile)
    out_specs = (tile, tile, P(ROW, None), P(), P())
    return jax.shard_map(body, mesh=split, in_specs=in_specs, out_specs=out_specs, check_vma=False)
```

time: 57.1 us -> 52.5 us (0.919)
  blocking collectives: 33 us -> 28.7 us
  waiting for transfers between devices: 7.46 us -> 3.6 us
  Pallas kernels: 9.1 us -> 11.5 us
  starting transfers between devices: 6.41 us -> 7.7 us
    all_to_all x1, blocking collectives: 20.5 us -> 16.2 us  [body(): pieces = lax.all_to_all(part.reshape(chips, piece, channels), CHIPS, 0, 0)]
    ppermute x5 -> x7, waiting for transfers between devices: 4.4 us -> 0.9 us  [the longest x1 0.89 us: body(): from_chip = lax.ppermute(to_chip, ROW, odd_rows + ends)]
    pallas_call x4 -> x6, Pallas kernels: 7.5 us -> 10 us  [the longest x1 3.83 us: body(): pl.pallas_call(outer_kernel, out_shape=(shape(*pair_input.shape), shape(*...]
    ppermute x5 -> x7, starting transfers between devices: 6.34 us -> 7.23 us  [the longest x1 2.44 us: body(): from_chip = lax.ppermute(to_chip, ROW, odd_rows + ends)]
  transfers between devices with their start and end apart: 7 -> 9, of which waited for: 4 -> 3; matrix products, arithmetic and copies ran while one was open for 0% -> 0% of each run, Pallas kernels for 1% -> 9%
where the time goes in v3:
time: 52.5 us; the launch traced here: 52.3 us
  blocking collectives  28.7 us (55%)
  Pallas kernels  11.5 us (22%)
  starting transfers between devices  7.7 us (15%)
  waiting for transfers between devices  3.6 us (7%)
  between operations  0.74 us (1%)
    all_to_all x1, blocking collectives, body(): pieces = lax.all_to_all(part.reshape(chips, piece, channels), CHIPS, 0, 0)  16.2 us
    all_to_all x1, blocking collectives, body(): mine = lax.all_to_all(copies, CHIPS, 0, 0).reshape(half, channels)  12.5 us
    pallas_call x1, Pallas kernels, body(): pl.pallas_call(outer_kernel, out_shape=(shape(*pair_input.shape), shape(*...  3.83 us
    pallas_call x1, Pallas kernels, body(): pl.pallas_call(inner_kernel, out_shape=(shape(span, 3 * channels), shape(...  2.65 us
    ppermute x1, starting transfers between devices, body(): from_chip = lax.ppermute(to_chip, ROW, odd_rows + ends)  2.44 us
    ppermute x1, starting transfers between devices, body(): corner_chip = lax.ppermute(corner_to_chip, ROW, odd_rows + ends)  2.18 us
    pallas_call x1, Pallas kernels, body(): pl.pallas_call(weights_kernel, out_shape=(shape(near_bins, channels, dtyp...  1.72 us
    pallas_call x1, Pallas kernels, body(): pl.pallas_call(pack_kernel, out_shape=(shape(layers, tile_rows, channels)...  1.54 us
  transfers between devices with their start and end apart: 9, of which 3 were waited for; matrix products, arithmetic and copies ran while one was open for 0% of the time, Pallas kernels for 9%

profile of v3, /device:TPU:0, one launch (start us, length us, event | category | flops | bytes accessed | tf_op | source)
XLA Modules:
  0.0 52.3 jit_solution(7792897949494306276)
XLA Ops:
  0.6 1.5 %pack.1 = (bf16[7,48,128]{2,1,0:T(8,128)(2,1)S(1)}, bf16[7,48,128]{2,1,0:T(8,128)(2,1)S(1)}, bf16[3,48,128]{2,1,0:T(8,128)(2,1)S(1)}, bf16[3,48,128]{2,1,0:T(8,128)(2,1)S(1)}) custom-call(bf16[48,48,128]{2,1,0:T(8,128)(2,1)} %pair.5, bf16[48,48,128]{2,1,0:T(8,128)(2,1)} %cot.5, bf16[48,512]{1,0:T(8,128)(2,1)} %features.1), custom_call_target="tpu_custom_call" | custom-call | tf_op jit(solution)/shard_map/pack/pallas_call | solution.py:433
  2.2 2.4 %collective-permute-start.1 = (bf16[7,48,128]{2,1,0:T(8,128)(2,1)S(1)}, bf16[7,48,128]{2,1,0:T(8,128)(2,1)S(1)}, u32[]{:S(2)}, u32[]{:S(2)}) collective-permute-start(bf16[7,48,128]{2,1,0:T(8,128)(2,1)S(1)} %get-tuple-element.39), channel_id=1, source_target_pairs={{8,16},{16,8},{0,24},{24,0},{9,17},{17,9},{1,25},{25,1},{10,18},{1... | collective-permute-start | bytes 258056 | tf_op jit(solution)/shard_map/ppermute | solution.py:464
  4.6 1.5 %collective-permute-start.2 = (bf16[3,48,128]{2,1,0:T(8,128)(2,1)S(1)}, bf16[3,48,128]{2,1,0:T(8,128)(2,1)S(1)}, u32[]{:S(2)}, u32[]{:S(2)}) collective-permute-start(bf16[3,48,128]{2,1,0:T(8,128)(2,1)S(1)} %get-tuple-element.41), channel_id=1, source_target_pairs={{0,1},{1,0},{2,3},{3,2},{4,5},{5,4},{6,7},{7,6},{8,9},{9,8},{10,11... | collective-permute-start | bytes 110600 | tf_op jit(solution)/shard_map/ppermute | solution.py:466
  6.1 0.4 collective-permute-start.3
  6.5 0.1 collective-permute-start
  6.7 0.9 %collective-permute-done.1.refs_2_.from_chip = bf16[7,48,128]{2,1,0:T(8,128)(2,1)S(1)} collective-permute-done((bf16[7,48,128]{2,1,0:T(8,128)(2,1)S(1)}, bf16[7,48,128]{2,1,0:T(8,128)(2,1)S(1)}, u32[]{:S(2)}, u32[]{:S(2)}) %collective-permute-start.1) | collective-permute-done | bytes 86048 | tf_op jit(solution)/shard_map/ppermute | solution.py:464
  7.5 0.1 collective-permute-start.4
  7.6 1.7 %weights.1 = (f32[128,128]{1,0:T(8,128)S(1)}, f32[56,128]{1,0:T(8,128)S(1)}, bf16[1536,256]{1,0:T(8,128)(2,1)S(1)}, bf16[1536,256]{1,0:T(8,128)(2,1)S(1)}, bf16[...) custom-call(s32[576]{0:T(1024)} %valid, bf16[384,512]{1,0:T(8,128)(2,1)} %context.1, ...), custom_call_target="tpu_custom_call" | custom-call | flops 1073741824 | bytes 2097152 | tf_op jit(solution)/shard_map/weights/pallas_call | solution.py:470
  9.4 0.0 collective-permute-done.refs_1_.from_core
  9.4 0.0 collective-permute-done.4.refs_3_
  9.4 0.2 prepare.1
  9.6 0.0 collective-permute-done.2.from_even
  9.7 0.5 collective-permute-start.5
  10.2 2.2 %collective-permute-start.6 = (bf16[2,3,16,128]{3,2,1,0:T(8,128)(2,1)S(1)}, bf16[2,3,16,128]{3,2,1,0:T(8,128)(2,1)S(1)}, u32[]{:S(2)}, u32[]{:S(2)}) collective-permute-start(bf16[2,3,16,128]{3,2,1,0:T(8,128)(2,1)S(1)} %get-tuple-element.51), channel_id=1, source_target_pairs={{8,16},{16,8},{0,24},{24,0},{9,17},{17,9},{1,25},{25,1},{10,18},{1... | collective-permute-start | bytes 73736 | tf_op jit(solution)/shard_map/ppermute | solution.py:519
  12.4 2.6 %inner.1 = (bf16[3072,384]{1,0:T(8,128)(2,1)S(1)}, bf16[3072,384]{1,0:T(8,128)(2,1)S(1)}, bf16[3072,128]{1,0:T(8,128)(2,1)S(1)}, bf16[48,48,128]{2,1,0:T(8,128)(2,1)S(1)}) custom-call(bf16[48,48,128]{2,1,0:T(8,128)(2,1)S(1)} %copy-done, bf16[48,48,128]{2,1,0:T(8,128)(2,1)S(1)} %copy-done.1, bf16[2,3,48,128]{3,2,1,0:T(8,128)(2,1)S(1)} %get-tuple-element.49.sides, ...), custom_call_target="tpu_custom_call" | custom-call | tf_op jit(solution)/shard_map/inner/pallas_call | solution.py:526
  15.0 0.0 collective-permute-done.5.corner_core
  15.0 3.8 %outer.1 = (bf16[48,48,128]{2,1,0:T(8,128)(2,1)}, bf16[48,48,128]{2,1,0:T(8,128)(2,1)}, f32[1024,128]{1,0:T(8,128)S(1)}, bf16[1024,128]{1,0:T(8,128)(2,1)S(1)}) custom-call(bf16[48,48,128]{2,1,0:T(8,128)(2,1)S(1)} %copy-done, bf16[48,48,128]{2,1,0:T(8,128)(2,1)S(1)} %copy-done.1, bf16[7,48,128]{2,1,0:T(8,128)(2,1)S(1)} %collective-permute-done.refs_1_.from_core, ...), custom_call_target="tpu_custom_call" | custom-call | tf_op jit(solution)/shard_map/outer/pallas_call | solution.py:537
  18.9 0.5 collective-permute-start.7
  19.4 1.2 %collective-permute-done.7 = bf16[1024,128]{1,0:T(8,128)(2,1)S(1)} collective-permute-done((bf16[1024,128]{1,0:T(8,128)(2,1)S(1)}, bf16[1024,128]{1,0:T(8,128)(2,1)S(1)}, u32[]{:S(2)}, u32[]{:S(2)}) %collective-permute-start.7) | collective-permute-done | bytes 262176 | tf_op jit(solution)/shard_map/ppermute | solution.py:568
  20.5 0.1 add_convert_fusion
  20.6 16.2 %all_to_all.10.pieces = bf16[16,64,128]{2,1,0:T(8,128)(2,1)S(1)} all-to-all(bf16[16,64,128]{2,1,0:T(8,128)(2,1)S(1)} %bitcast.4), channel_id=1, replica_groups=mesh['rx'=2,'core'=2,'col'=8] {'rx','col'}, dimensions={0} | all-to-all | bytes 524288 | tf_op jit(solution)/shard_map/all_to_all | solution.py:569
  36.8 12.5 %all_to_all.11 = bf16[16,64,128]{2,1,0:T(8,128)(2,1)S(1)} all-to-all(bf16[16,64,128]{2,1,0:T(8,128)(2,1)S(1)} %add.6), channel_id=1, replica_groups=mesh['rx'=2,'core'=2,'col'=8] {'rx','col'}, dimensions={0} | all-to-all | bytes 524288 | tf_op jit(solution)/shard_map/all_to_all | solution.py:578
  49.3 1.5 %collective-permute-done.8.theirs = bf16[1024,128]{1,0:T(8,128)(2,1)S(1)} collective-permute-done((bf16[1024,128]{1,0:T(8,128)(2,1)S(1)}, bf16[1024,128]{1,0:T(8,128)(2,1)S(1)}, u32[]{:S(2)}, u32[]{:S(2)}) %collective-permute-start.8) | collective-permute-done | bytes 262176 | tf_op jit(solution)/shard_map/ppermute | solution.py:579
  50.8 1.5 %finish.1 = (bf16[48,512]{1,0:T(8,128)(2,1)}, f32[512,256]{1,0:T(8,128)}, f32[9,128,128]{2,1,0:T(8,128)}) custom-call(bf16[1024,128]{1,0:T(8,128)(2,1)S(1)} %bitcast.3, bf16[1024,128]{1,0:T(8,128)(2,1)S(1)} %collective-permute-done.8.theirs, bf16[512,192]{1,0:T(8,128)(2,1)S(1)} %get-tuple-element.66.features_turned, ...), custom_call_target="tpu_custom_call" | custom-call | tf_op jit(solution)/shard_map/finish/pallas_call | solution.py:581
  (9 shorter events, 0.1 us)
Async XLA Ops:
  2.2 5.4 %collective-permute-start.1 = (bf16[7,48,128]{2,1,0:T(8,128)(2,1)S(1)}, bf16[7,48,128]{2,1,0:T(8,128)(2,1)S(1)}, u32[]{:S(2)}, u32[]{:S(2)}) collective-permute-start(bf16[7,48,128]{2,1,0:T(8,128)(2,1)S(1)} %get-tuple-element.39), channel_id=1, source_target_pairs={{8,16},{16,8},{0,24},{24,0},{9,17},{17,9},{1,25},{25,1},{10,18},{1... | collective-permute-start | bytes 258056 | tf_op jit(solution)/shard_map/ppermute | solution.py:464
  4.6 5.0 %collective-permute-start.2 = (bf16[3,48,128]{2,1,0:T(8,128)(2,1)S(1)}, bf16[3,48,128]{2,1,0:T(8,128)(2,1)S(1)}, u32[]{:S(2)}, u32[]{:S(2)}) collective-permute-start(bf16[3,48,128]{2,1,0:T(8,128)(2,1)S(1)} %get-tuple-element.41), channel_id=1, source_target_pairs={{0,1},{1,0},{2,3},{3,2},{4,5},{5,4},{6,7},{7,6},{8,9},{9,8},{10,11... | collective-permute-start | bytes 110600 | tf_op jit(solution)/shard_map/ppermute | solution.py:466
  6.1 3.5 %collective-permute-start.3 = (bf16[3,48,128]{2,1,0:T(8,128)(2,1)S(1)}, bf16[3,48,128]{2,1,0:T(8,128)(2,1)S(1)}, u32[]{:S(2)}, u32[]{:S(2)}) collective-permute-start(bf16[3,48,128]{2,1,0:T(8,128)(2,1)S(1)} %get-tuple-element.42), channel_id=1, source_target_pairs={{0,8},{1,2},{2,1},{3,4},{4,3},{5,6},{6,5},{7,15},{8,0},{9,10},{10,... | collective-permute-start | bytes 110600 | tf_op jit(solution)/shard_map/ppermute | solution.py:465
  6.5 5.8 %copy-start = (bf16[48,48,128]{2,1,0:T(8,128)(2,1)S(1)}, bf16[48,48,128]{2,1,0:T(8,128)(2,1)}, u32[]{:S(2)}) copy-start(bf16[48,48,128]{2,1,0:T(8,128)(2,1)} %pair.5) | copy-start | bytes 1769476
  6.5 5.8 %copy-start.1 = (bf16[48,48,128]{2,1,0:T(8,128)(2,1)S(1)}, bf16[48,48,128]{2,1,0:T(8,128)(2,1)}, u32[]{:S(2)}) copy-start(bf16[48,48,128]{2,1,0:T(8,128)(2,1)} %cot.5) | copy-start | bytes 1769476
  6.5 2.8 %collective-permute-start = (bf16[7,48,128]{2,1,0:T(8,128)(2,1)S(1)}, bf16[7,48,128]{2,1,0:T(8,128)(2,1)S(1)}, u32[]{:S(2)}, u32[]{:S(2)}) collective-permute-start(bf16[7,48,128]{2,1,0:T(8,128)(2,1)S(1)} %get-tuple-element.38.refs_0_), channel_id=1, source_target_pairs={{0,8},{8,0},{1,9},{9,1},{2,10},{10,2},{3,11},{11,3},{4,12},{12,4},... | collective-permute-start | bytes 258056 | tf_op jit(solution)/shard_map/ppermute | solution.py:467
  7.5 1.8 %collective-permute-start.4 = (bf16[7,48,128]{2,1,0:T(8,128)(2,1)S(1)}, bf16[7,48,128]{2,1,0:T(8,128)(2,1)S(1)}, u32[]{:S(2)}, u32[]{:S(2)}) collective-permute-start(bf16[7,48,128]{2,1,0:T(8,128)(2,1)S(1)} %collective-permute-done.1.refs_2_.from_chip), channel_id=1, source_target_pairs={{0,8},{8,0},{1,9},{9,1},{2,10},{10,2},{3,11},{11,3},{4,12},{12,4},... | collective-permute-start | bytes 258056 | tf_op jit(solution)/shard_map/ppermute | solution.py:488
  9.7 5.3 %collective-permute-start.5 = (bf16[2,3,16,128]{3,2,1,0:T(8,128)(2,1)S(1)}, bf16[2,3,16,128]{3,2,1,0:T(8,128)(2,1)S(1)}, u32[]{:S(2)}, u32[]{:S(2)}) collective-permute-start(bf16[2,3,16,128]{3,2,1,0:T(8,128)(2,1)S(1)} %get-tuple-element.50), channel_id=1, source_target_pairs={{0,8},{8,0},{1,9},{9,1},{2,10},{10,2},{3,11},{11,3},{4,12},{12,4},... | collective-permute-start | bytes 73736 | tf_op jit(solution)/shard_map/ppermute | solution.py:520
  10.2 4.9 %collective-permute-start.6 = (bf16[2,3,16,128]{3,2,1,0:T(8,128)(2,1)S(1)}, bf16[2,3,16,128]{3,2,1,0:T(8,128)(2,1)S(1)}, u32[]{:S(2)}, u32[]{:S(2)}) collective-permute-start(bf16[2,3,16,128]{3,2,1,0:T(8,128)(2,1)S(1)} %get-tuple-element.51), channel_id=1, source_target_pairs={{8,16},{16,8},{0,24},{24,0},{9,17},{17,9},{1,25},{25,1},{10,18},{1... | collective-permute-start | bytes 73736 | tf_op jit(solution)/shard_map/ppermute | solution.py:519
  18.9 1.6 %collective-permute-start.7 = (bf16[1024,128]{1,0:T(8,128)(2,1)S(1)}, bf16[1024,128]{1,0:T(8,128)(2,1)S(1)}, u32[]{:S(2)}, u32[]{:S(2)}) collective-permute-start(bf16[1024,128]{1,0:T(8,128)(2,1)S(1)} %get-tuple-element.65), channel_id=1, source_target_pairs={{0,8},{8,0},{1,9},{9,1},{2,10},{10,2},{3,11},{11,3},{4,12},{12,4},... | collective-permute-start | bytes 786440 | tf_op jit(solution)/shard_map/ppermute | solution.py:568
  49.3 1.5 %collective-permute-start.8 = (bf16[1024,128]{1,0:T(8,128)(2,1)S(1)}, bf16[1024,128]{1,0:T(8,128)(2,1)S(1)}, u32[]{:S(2)}, u32[]{:S(2)}) collective-permute-start(bf16[1024,128]{1,0:T(8,128)(2,1)S(1)} %bitcast.2), channel_id=1, source_target_pairs={{0,8},{8,0},{1,9},{9,1},{2,10},{10,2},{3,11},{11,3},{4,12},{12,4},... | collective-permute-start | bytes 786440 | tf_op jit(solution)/shard_map/ppermute | solution.py:579

commit v4 on v3

--- a/solution.py
+++ b/solution.py
@@ -125,6 +125,12 @@
     query[...] = query_rows[pl.ds(pl.multiple_of(row_start, 16), query.shape[0]), :]
     key[...] = key_rows[pl.ds(pl.multiple_of(col_start, 16), key.shape[0]), :]
     features_turned[...] = features[...].astype(F32).T.astype(BF16)
+
+
+def quarter_of(parts):
+    if parts == 1:
+        return 0
+    return 2 * lax.axis_index("rx") + lax.rem(lax.axis_index("col"), 2)
 
 
 def spread(source, target, first, last, base, sign):
@@ -355,9 +361,11 @@
         grads = grads + lax.dot_general(cots, around, (((0,), (0,)), ((), ())), preferred_element_type=F32)
     for tap in range(9):
         totals[tap * channels : (tap + 1) * channels, :] = grads[:, tap * channels : (tap + 1) * channels]
-    half = keep.shape[0]
-    keep[...] = totals[pl.ds(pl.multiple_of(core * half, half), half), :]
-    send[...] = totals[pl.ds(pl.multiple_of((1 - core) * half, half), half), :].astype(BF16)
+    parts, size = keep.shape[:2]
+    for part in range(parts):
+        place = lax.bitwise_xor(quarter_of(parts), part)
+        keep[part] = totals[pl.ds(pl.multiple_of((core * parts + place) * size, 16), size), :]
+        send[part] = totals[pl.ds(pl.multiple_of(((1 - core) * parts + place) * size, 16), size), :].astype(BF16)
     for copy in (write_output, write_first, write_last, write_grad):
         copy.wait()
 
@@ -375,11 +383,13 @@
 ):
     core = lax.axis_index("core")
     row = lax.axis_index(ROW)
-    half, channels = mine.shape
+    parts, size, channels = mine.shape
     all_bins, tail = features_turned.shape[1], context_turned.shape[1]
     tile_rows = feature_grad.shape[0]
-    whole[pl.ds(pl.multiple_of(core * half, half), half), :] = mine[...]
-    whole[pl.ds(pl.multiple_of((1 - core) * half, half), half), :] = theirs[...]
+    for part in range(parts):
+        place = lax.bitwise_xor(quarter_of(parts), part)
+        whole[pl.ds(pl.multiple_of((core * parts + place) * size, 16), size), :] = mine[part]
+        whole[pl.ds(pl.multiple_of(((1 - core) * parts + place) * size, 16), size), :] = theirs[part]
     copies = [
         pltpu.make_async_copy(source, target, sems.at[index])
         for index, (source, target) in enumerate(((conv_out, conv_grad), (proj_out, proj_grad), (feature_out, feature_grad)))
@@ -520,8 +530,12 @@
     corner_core = lax.ppermute(corner_to_core, "core", other_core)
 
 
-    piece = -(-(9 * channels + 2 * all_bins + tail) // (32 * chips)) * 16
-    half = piece * chips
+    total_rows = 9 * channels + 2 * all_bins + tail
+    staged = (row_count, col_count) == (4, 8) and total_rows % 128 == 0
+    if staged:
+        parts, half = 4, total_rows // 2
+    else:
+        parts, half = 1, -(-total_rows // (32 * chips)) * 16 * chips
     span = tile_rows * PITCH
     inner = pl.pallas_call(
         inner_kernel,
@@ -539,8 +553,8 @@
         out_shape=(
             shape(*pair_input.shape),
             shape(*pair_input.shape),
-            shape(half, channels, dtype=F32),
-            shape(half, channels),
+            shape(parts, half // parts, channels, dtype=F32),
+            shape(parts, half // parts, channels),
         ),
         in_specs=[vmem] * 17,
         out_specs=(anywhere, anywhere, vmem, vmem),
@@ -565,17 +579,29 @@
         forward, backward, *inner,
     )
 
-    part = (keep + lax.ppermute(send, "core", other_core).astype(F32)).astype(BF16)
-    pieces = lax.all_to_all(part.reshape(chips, piece, channels), CHIPS, 0, 0)
-    copies = pl.pallas_call(
-        add_kernel,
-        out_shape=shape(chips, piece, channels),
-        in_specs=[vmem],
-        out_specs=vmem,
-        compiler_params=PARAMS,
-        name="add",
-    )(pieces)
-    mine = lax.all_to_all(copies, CHIPS, 0, 0).reshape(half, channels)
+    halves = keep + lax.ppermute(send, "core", other_core).astype(F32)
+    if staged:
+        def across(values, bits):
+            return lax.ppermute(values, ROW + ("col",), [(index, index ^ bits) for index in range(32)])
+
+        plane = (1, 16, 17)
+        got = [across(halves[part].astype(BF16), bits).astype(F32) for part, bits in enumerate(plane, 1)]
+        mine = (halves[0] + got[0] + got[1] + got[2]).astype(BF16)
+        near, far, opposite = [across(mine, bits).astype(F32) for bits in (2, 4, 6)]
+        mine = ((mine.astype(F32) + near) + (far + opposite)).astype(BF16)
+        mine = jnp.stack([mine] + [across(mine, bits) for bits in plane])
+    else:
+        piece = half // chips
+        pieces = lax.all_to_all(halves.astype(BF16).reshape(chips, piece, channels), CHIPS, 0, 0)
+        copies = pl.pallas_call(
+            add_kernel,
+            out_shape=shape(chips, piece, channels),
+            in_specs=[vmem],
+            out_specs=vmem,
+            compiler_params=PARAMS,
+            name="add",
+        )(pieces)
+        mine = lax.all_to_all(copies, CHIPS, 0, 0).reshape(1, half, channels)
     theirs = lax.ppermute(mine, "core", other_core)
 
     feature_grad, proj_grad, conv_grad = pl.pallas_call(

time: 52.5 us -> 46.4 us (0.88)
  blocking collectives: 28.7 us -> 0 us
  starting transfers between devices: 7.7 us -> 19.3 us
  waiting for transfers between devices: 3.6 us -> 14.9 us
    all_to_all x2 -> x0, blocking collectives: 28.7 us -> none  [the longest x1 16.2 us: body(): pieces = lax.all_to_all(part.reshape(chips, piece, channels), CHIPS, 0, 0)]
    ppermute x1 -> x10, starting transfers between devices: 0.47 us -> 12 us  [the longest x9 11.6 us: across(): lax.ppermute(values, ROW + ('col',), [(index, index ^ bits) for index in...]
    ppermute x1 -> x10, waiting for transfers between devices: 1.16 us -> 12.5 us  [the longest x9 11.4 us: across(): lax.ppermute(values, ROW + ('col',), [(index, index ^ bits) for index in...]
  transfers between devices with their start and end apart: 9 -> 18, of which waited for: 3 -> 10; matrix products, arithmetic and copies ran while one was open for 0% -> 0% of each run, Pallas kernels for 9% -> 10%
where the time goes in v4:
time: 46.4 us; the launch traced here: 46.3 us
  starting transfers between devices  19.3 us (42%)
  waiting for transfers between devices  14.9 us (32%)
  Pallas kernels  11.1 us (24%)
  between operations  0.77 us (2%)
    ppermute x9, starting transfers between devices, across(): lax.ppermute(values, ROW + ('col',), [(index, index ^ bits) for index in...  11.6 us
    ppermute x9, waiting for transfers between devices, across(): lax.ppermute(values, ROW + ('col',), [(index, index ^ bits) for index in...  11.4 us
    pallas_call x1, Pallas kernels, body(): pl.pallas_call(outer_kernel, out_shape=(shape(*pair_input.shape), shape(*...  3.36 us
    pallas_call x1, Pallas kernels, body(): pl.pallas_call(inner_kernel, out_shape=(shape(span, 3 * channels), shape(...  2.7 us
    ppermute x1, starting transfers between devices, body(): from_chip = lax.ppermute(to_chip, ROW, odd_rows + ends)  2.44 us
    ppermute x1, starting transfers between devices, body(): corner_chip = lax.ppermute(corner_to_chip, ROW, odd_rows + ends)  2.18 us
    pallas_call x1, Pallas kernels, body(): pl.pallas_call(weights_kernel, out_shape=(shape(near_bins, channels, dtyp...  1.72 us
    pallas_call x1, Pallas kernels, body(): pl.pallas_call(pack_kernel, out_shape=(shape(layers, tile_rows, channels)...  1.54 us
  transfers between devices with their start and end apart: 18, of which 10 were waited for; matrix products, arithmetic and copies ran while one was open for 0% of the time, Pallas kernels for 10%

profile of v4, /device:TPU:0, one launch (start us, length us, event | category | flops | bytes accessed | tf_op | source)
XLA Modules:
  0.0 46.3 jit_solution(1168452018678092627)
XLA Ops:
  0.6 1.5 %pack.1 = (bf16[7,48,128]{2,1,0:T(8,128)(2,1)S(1)}, bf16[7,48,128]{2,1,0:T(8,128)(2,1)S(1)}, bf16[3,48,128]{2,1,0:T(8,128)(2,1)S(1)}, bf16[3,48,128]{2,1,0:T(8,128)(2,1)S(1)}) custom-call(bf16[48,48,128]{2,1,0:T(8,128)(2,1)} %pair.5, bf16[48,48,128]{2,1,0:T(8,128)(2,1)} %cot.5, bf16[48,512]{1,0:T(8,128)(2,1)} %features.1), custom_call_target="tpu_custom_call" | custom-call | tf_op jit(solution)/shard_map/pack/pallas_call | solution.py:443
  2.2 2.4 %collective-permute-start.1 = (bf16[7,48,128]{2,1,0:T(8,128)(2,1)S(1)}, bf16[7,48,128]{2,1,0:T(8,128)(2,1)S(1)}, u32[]{:S(2)}, u32[]{:S(2)}) collective-permute-start(bf16[7,48,128]{2,1,0:T(8,128)(2,1)S(1)} %get-tuple-element.39), channel_id=1, source_target_pairs={{8,16},{16,8},{0,24},{24,0},{9,17},{17,9},{1,25},{25,1},{10,18},{1... | collective-permute-start | bytes 258056 | tf_op jit(solution)/shard_map/ppermute | solution.py:474
  4.6 1.5 %collective-permute-start.2 = (bf16[3,48,128]{2,1,0:T(8,128)(2,1)S(1)}, bf16[3,48,128]{2,1,0:T(8,128)(2,1)S(1)}, u32[]{:S(2)}, u32[]{:S(2)}) collective-permute-start(bf16[3,48,128]{2,1,0:T(8,128)(2,1)S(1)} %get-tuple-element.41), channel_id=1, source_target_pairs={{0,1},{1,0},{2,3},{3,2},{4,5},{5,4},{6,7},{7,6},{8,9},{9,8},{10,11... | collective-permute-start | bytes 110600 | tf_op jit(solution)/shard_map/ppermute | solution.py:476
  6.7 0.9 %collective-permute-done.1.refs_2_.from_chip = bf16[7,48,128]{2,1,0:T(8,128)(2,1)S(1)} collective-permute-done((bf16[7,48,128]{2,1,0:T(8,128)(2,1)S(1)}, bf16[7,48,128]{2,1,0:T(8,128)(2,1)S(1)}, u32[]{:S(2)}, u32[]{:S(2)}) %collective-permute-start.1) | collective-permute-done | bytes 86048 | tf_op jit(solution)/shard_map/ppermute | solution.py:474
  7.6 1.7 %weights.1 = (f32[128,128]{1,0:T(8,128)S(1)}, f32[56,128]{1,0:T(8,128)S(1)}, bf16[1536,256]{1,0:T(8,128)(2,1)S(1)}, bf16[1536,256]{1,0:T(8,128)(2,1)S(1)}, bf16[...) custom-call(s32[576]{0:T(1024)} %valid, bf16[384,512]{1,0:T(8,128)(2,1)} %context.1, ...), custom_call_target="tpu_custom_call" | custom-call | flops 1073741824 | bytes 2097152 | tf_op jit(solution)/shard_map/weights/pallas_call | solution.py:480
  10.2 2.2 %collective-permute-start.6 = (bf16[2,3,16,128]{3,2,1,0:T(8,128)(2,1)S(1)}, bf16[2,3,16,128]{3,2,1,0:T(8,128)(2,1)S(1)}, u32[]{:S(2)}, u32[]{:S(2)}) collective-permute-start(bf16[2,3,16,128]{3,2,1,0:T(8,128)(2,1)S(1)} %get-tuple-element.51), channel_id=1, source_target_pairs={{8,16},{16,8},{0,24},{24,0},{9,17},{17,9},{1,25},{25,1},{10,18},{1... | collective-permute-start | bytes 73736 | tf_op jit(solution)/shard_map/ppermute | solution.py:529
  12.4 2.7 %inner.1 = (bf16[3072,384]{1,0:T(8,128)(2,1)S(1)}, bf16[3072,384]{1,0:T(8,128)(2,1)S(1)}, bf16[3072,128]{1,0:T(8,128)(2,1)S(1)}, bf16[48,48,128]{2,1,0:T(8,128)(2,1)S(1)}) custom-call(bf16[48,48,128]{2,1,0:T(8,128)(2,1)S(1)} %copy-done, bf16[48,48,128]{2,1,0:T(8,128)(2,1)S(1)} %copy-done.1, bf16[2,3,48,128]{3,2,1,0:T(8,128)(2,1)S(1)} %get-tuple-element.49.sides, ...), custom_call_target="tpu_custom_call" | custom-call | tf_op jit(solution)/shard_map/inner/pallas_call | solution.py:540
  15.1 3.4 %outer.1 = (bf16[48,48,128]{2,1,0:T(8,128)(2,1)}, bf16[48,48,128]{2,1,0:T(8,128)(2,1)}, f32[4,240,128]{2,1,0:T(8,128)S(1)}, bf16[4,240,128]{2,1,0:T(8,128)(2,1)S(1)}) custom-call(bf16[48,48,128]{2,1,0:T(8,128)(2,1)S(1)} %copy-done, bf16[48,48,128]{2,1,0:T(8,128)(2,1)S(1)} %copy-done.1, bf16[7,48,128]{2,1,0:T(8,128)(2,1)S(1)} %collective-permute-done.refs_1_.from_core, ...), custom_call_target="tpu_custom_call" | custom-call | tf_op jit(solution)/shard_map/outer/pallas_call | solution.py:551
  18.9 1.1 %collective-permute-done.7 = bf16[4,240,128]{2,1,0:T(8,128)(2,1)S(1)} collective-permute-done((bf16[4,240,128]{2,1,0:T(8,128)(2,1)S(1)}, bf16[4,240,128]{2,1,0:T(8,128)(2,1)S(1)}, u32[]{:S(2)}, u32[]{:S(2)}) %collective-permute-start.7) | collective-permute-done | bytes 245792 | tf_op jit(solution)/shard_map/ppermute | solution.py:582
  20.2 1.6 %collective-permute-start.8 = (bf16[240,128]{1,0:T(8,128)(2,1)S(1)}, bf16[240,128]{1,0:T(8,128)(2,1)S(1)}, u32[]{:S(2)}, u32[]{:S(2)}) collective-permute-start(bf16[240,128]{1,0:T(8,128)(2,1)S(1)} %get-tuple-element.73), channel_id=1, source_target_pairs={{0,1},{1,0},{2,3},{3,2},{4,5},{5,4},{6,7},{7,6},{8,9},{9,8},{10,11... | collective-permute-start | bytes 184328 | tf_op jit(solution)/shard_map/ppermute | solution.py:585
  22.5 1.3 %collective-permute-start.9 = (bf16[240,128]{1,0:T(8,128)(2,1)S(1)}, bf16[240,128]{1,0:T(8,128)(2,1)S(1)}, u32[]{:S(2)}, u32[]{:S(2)}) collective-permute-start(bf16[240,128]{1,0:T(8,128)(2,1)S(1)} %get-tuple-element.75), channel_id=1, source_target_pairs={{0,16},{1,17},{2,18},{3,19},{4,20},{5,21},{6,22},{7,23},{8,24},{9,... | collective-permute-start | bytes 184328 | tf_op jit(solution)/shard_map/ppermute | solution.py:585
  23.7 0.8 %collective-permute-done.8 = bf16[240,128]{1,0:T(8,128)(2,1)S(1)} collective-permute-done((bf16[240,128]{1,0:T(8,128)(2,1)S(1)}, bf16[240,128]{1,0:T(8,128)(2,1)S(1)}, u32[]{:S(2)}, u32[]{:S(2)}) %collective-permute-start.8) | collective-permute-done | bytes 61472 | tf_op jit(solution)/shard_map/ppermute | solution.py:585
  24.5 2.8 %collective-permute-done.10 = bf16[240,128]{1,0:T(8,128)(2,1)S(1)} collective-permute-done((bf16[240,128]{1,0:T(8,128)(2,1)S(1)}, bf16[240,128]{1,0:T(8,128)(2,1)S(1)}, u32[]{:S(2)}, u32[]{:S(2)}) %collective-permute-start.10) | collective-permute-done | bytes 61472 | tf_op jit(solution)/shard_map/ppermute | solution.py:585
  27.3 3.7 %collective-permute-start.13 = (bf16[240,128]{1,0:T(8,128)(2,1)S(1)}, bf16[240,128]{1,0:T(8,128)(2,1)S(1)}, u32[]{:S(2)}, u32[]{:S(2)}) collective-permute-start(bf16[240,128]{1,0:T(8,128)(2,1)S(1)} %fusion.3), channel_id=1, source_target_pairs={{0,6},{1,7},{2,4},{3,5},{4,2},{5,3},{6,0},{7,1},{8,14},{9,15},{10,... | collective-permute-start | bytes 184328 | tf_op jit(solution)/shard_map/ppermute | solution.py:585
  31.0 0.8 %collective-permute-start.11 = (bf16[240,128]{1,0:T(8,128)(2,1)S(1)}, bf16[240,128]{1,0:T(8,128)(2,1)S(1)}, u32[]{:S(2)}, u32[]{:S(2)}) collective-permute-start(bf16[240,128]{1,0:T(8,128)(2,1)S(1)} %fusion.3), channel_id=1, source_target_pairs={{0,2},{1,3},{2,0},{3,1},{4,6},{5,7},{6,4},{7,5},{8,10},{9,11},{10,... | collective-permute-start | bytes 184328 | tf_op jit(solution)/shard_map/ppermute | solution.py:585
  31.8 1.6 %collective-permute-done.13 = bf16[240,128]{1,0:T(8,128)(2,1)S(1)} collective-permute-done((bf16[240,128]{1,0:T(8,128)(2,1)S(1)}, bf16[240,128]{1,0:T(8,128)(2,1)S(1)}, u32[]{:S(2)}, u32[]{:S(2)}) %collective-permute-start.13) | collective-permute-done | bytes 61472 | tf_op jit(solution)/shard_map/ppermute | solution.py:585
  33.4 2.7 %collective-permute-done.12 = bf16[240,128]{1,0:T(8,128)(2,1)S(1)} collective-permute-done((bf16[240,128]{1,0:T(8,128)(2,1)S(1)}, bf16[240,128]{1,0:T(8,128)(2,1)S(1)}, u32[]{:S(2)}, u32[]{:S(2)}) %collective-permute-start.12) | collective-permute-done | bytes 61472 | tf_op jit(solution)/shard_map/ppermute | solution.py:585
  36.2 1.7 %collective-permute-start.16 = (bf16[240,128]{1,0:T(8,128)(2,1)S(1)}, bf16[240,128]{1,0:T(8,128)(2,1)S(1)}, u32[]{:S(2)}, u32[]{:S(2)}) collective-permute-start(bf16[240,128]{1,0:T(8,128)(2,1)S(1)} %add_convert_fusion), channel_id=1, source_target_pairs={{0,17},{1,16},{2,19},{3,18},{4,21},{5,20},{6,23},{7,22},{8,25},{9,... | collective-permute-start | bytes 184328 | tf_op jit(solution)/shard_map/ppermute | solution.py:585
  37.9 1.1 %collective-permute-start.15 = (bf16[240,128]{1,0:T(8,128)(2,1)S(1)}, bf16[240,128]{1,0:T(8,128)(2,1)S(1)}, u32[]{:S(2)}, u32[]{:S(2)}) collective-permute-start(bf16[240,128]{1,0:T(8,128)(2,1)S(1)} %add_convert_fusion), channel_id=1, source_target_pairs={{0,16},{1,17},{2,18},{3,19},{4,20},{5,21},{6,22},{7,23},{8,24},{9,... | collective-permute-start | bytes 184328 | tf_op jit(solution)/shard_map/ppermute | solution.py:585
  39.7 1.6 %collective-permute-done.16 = bf16[240,128]{1,0:T(8,128)(2,1)S(1)} collective-permute-done((bf16[240,128]{1,0:T(8,128)(2,1)S(1)}, bf16[240,128]{1,0:T(8,128)(2,1)S(1)}, u32[]{:S(2)}, u32[]{:S(2)}) %collective-permute-start.16) | collective-permute-done | bytes 61472 | tf_op jit(solution)/shard_map/ppermute | solution.py:585
  41.4 0.8 %collective-permute-done.15 = bf16[240,128]{1,0:T(8,128)(2,1)S(1)} collective-permute-done((bf16[240,128]{1,0:T(8,128)(2,1)S(1)}, bf16[240,128]{1,0:T(8,128)(2,1)S(1)}, u32[]{:S(2)}, u32[]{:S(2)}) %collective-permute-start.15) | collective-permute-done | bytes 61472 | tf_op jit(solution)/shard_map/ppermute | solution.py:585
  42.1 1.1 %collective-permute-done.14 = bf16[240,128]{1,0:T(8,128)(2,1)S(1)} collective-permute-done((bf16[240,128]{1,0:T(8,128)(2,1)S(1)}, bf16[240,128]{1,0:T(8,128)(2,1)S(1)}, u32[]{:S(2)}, u32[]{:S(2)}) %collective-permute-start.14) | collective-permute-done | bytes 61472 | tf_op jit(solution)/shard_map/ppermute | solution.py:585
  43.3 1.5 %collective-permute-done.17.theirs = bf16[4,240,128]{2,1,0:T(8,128)(2,1)S(1)} collective-permute-done((bf16[4,240,128]{2,1,0:T(8,128)(2,1)S(1)}, bf16[4,240,128]{2,1,0:T(8,128)(2,1)S(1)}, u32[]{:S(2)}, u32[]{:S(2)}) %collective-permute-start.17) | collective-permute-done | bytes 245792 | tf_op jit(solution)/shard_map/ppermute | solution.py:605
  44.8 1.5 %finish.1 = (bf16[48,512]{1,0:T(8,128)(2,1)}, f32[512,256]{1,0:T(8,128)}, f32[9,128,128]{2,1,0:T(8,128)}) custom-call(bf16[4,240,128]{2,1,0:T(8,128)(2,1)S(1)} %pad_maximum_fusion.mine, bf16[4,240,128]{2,1,0:T(8,128)(2,1)S(1)} %collective-permute-done.17.theirs, bf16[512,192]{1,0:T(8,128)(2,1)S(1)} %get-tuple-element.66.features_turned, ...), custom_call_target="tpu_custom_call" | custom-call | tf_op jit(solution)/shard_map/finish/pallas_call | solution.py:607
  (28 shorter events, 3.6 us)
Async XLA Ops:
  2.2 5.4 %collective-permute-start.1 = (bf16[7,48,128]{2,1,0:T(8,128)(2,1)S(1)}, bf16[7,48,128]{2,1,0:T(8,128)(2,1)S(1)}, u32[]{:S(2)}, u32[]{:S(2)}) collective-permute-start(bf16[7,48,128]{2,1,0:T(8,128)(2,1)S(1)} %get-tuple-element.39), channel_id=1, source_target_pairs={{8,16},{16,8},{0,24},{24,0},{9,17},{17,9},{1,25},{25,1},{10,18},{1... | collective-permute-start | bytes 258056 | tf_op jit(solution)/shard_map/ppermute | solution.py:474
  4.6 5.0 %collective-permute-start.2 = (bf16[3,48,128]{2,1,0:T(8,128)(2,1)S(1)}, bf16[3,48,128]{2,1,0:T(8,128)(2,1)S(1)}, u32[]{:S(2)}, u32[]{:S(2)}) collective-permute-start(bf16[3,48,128]{2,1,0:T(8,128)(2,1)S(1)} %get-tuple-element.41), channel_id=1, source_target_pairs={{0,1},{1,0},{2,3},{3,2},{4,5},{5,4},{6,7},{7,6},{8,9},{9,8},{10,11... | collective-permute-start | bytes 110600 | tf_op jit(solution)/shard_map/ppermute | solution.py:476
  6.1 3.5 %collective-permute-start.3 = (bf16[3,48,128]{2,1,0:T(8,128)(2,1)S(1)}, bf16[3,48,128]{2,1,0:T(8,128)(2,1)S(1)}, u32[]{:S(2)}, u32[]{:S(2)}) collective-permute-start(bf16[3,48,128]{2,1,0:T(8,128)(2,1)S(1)} %get-tuple-element.42), channel_id=1, source_target_pairs={{0,8},{1,2},{2,1},{3,4},{4,3},{5,6},{6,5},{7,15},{8,0},{9,10},{10,... | collective-permute-start | bytes 110600 | tf_op jit(solution)/shard_map/ppermute | solution.py:475
  6.5 5.8 %copy-start = (bf16[48,48,128]{2,1,0:T(8,128)(2,1)S(1)}, bf16[48,48,128]{2,1,0:T(8,128)(2,1)}, u32[]{:S(2)}) copy-start(bf16[48,48,128]{2,1,0:T(8,128)(2,1)} %pair.5) | copy-start | bytes 1769476
  6.5 5.8 %copy-start.1 = (bf16[48,48,128]{2,1,0:T(8,128)(2,1)S(1)}, bf16[48,48,128]{2,1,0:T(8,128)(2,1)}, u32[]{:S(2)}) copy-start(bf16[48,48,128]{2,1,0:T(8,128)(2,1)} %cot.5) | copy-start | bytes 1769476
  6.5 2.8 %collective-permute-start = (bf16[7,48,128]{2,1,0:T(8,128)(2,1)S(1)}, bf16[7,48,128]{2,1,0:T(8,128)(2,1)S(1)}, u32[]{:S(2)}, u32[]{:S(2)}) collective-permute-start(bf16[7,48,128]{2,1,0:T(8,128)(2,1)S(1)} %get-tuple-element.38.refs_0_), channel_id=1, source_target_pairs={{0,8},{8,0},{1,9},{9,1},{2,10},{10,2},{3,11},{11,3},{4,12},{12,4},... | collective-permute-start | bytes 258056 | tf_op jit(solution)/shard_map/ppermute | solution.py:477
  7.5 1.8 %collective-permute-start.4 = (bf16[7,48,128]{2,1,0:T(8,128)(2,1)S(1)}, bf16[7,48,128]{2,1,0:T(8,128)(2,1)S(1)}, u32[]{:S(2)}, u32[]{:S(2)}) collective-permute-start(bf16[7,48,128]{2,1,0:T(8,128)(2,1)S(1)} %collective-permute-done.1.refs_2_.from_chip), channel_id=1, source_target_pairs={{0,8},{8,0},{1,9},{9,1},{2,10},{10,2},{3,11},{11,3},{4,12},{12,4},... | collective-permute-start | bytes 258056 | tf_op jit(solution)/shard_map/ppermute | solution.py:498
  9.7 5.4 %collective-permute-start.5 = (bf16[2,3,16,128]{3,2,1,0:T(8,128)(2,1)S(1)}, bf16[2,3,16,128]{3,2,1,0:T(8,128)(2,1)S(1)}, u32[]{:S(2)}, u32[]{:S(2)}) collective-permute-start(bf16[2,3,16,128]{3,2,1,0:T(8,128)(2,1)S(1)} %get-tuple-element.50), channel_id=1, source_target_pairs={{0,8},{8,0},{1,9},{9,1},{2,10},{10,2},{3,11},{11,3},{4,12},{12,4},... | collective-permute-start | bytes 73736 | tf_op jit(solution)/shard_map/ppermute | solution.py:530
  10.2 4.9 %collective-permute-start.6 = (bf16[2,3,16,128]{3,2,1,0:T(8,128)(2,1)S(1)}, bf16[2,3,16,128]{3,2,1,0:T(8,128)(2,1)S(1)}, u32[]{:S(2)}, u32[]{:S(2)}) collective-permute-start(bf16[2,3,16,128]{3,2,1,0:T(8,128)(2,1)S(1)} %get-tuple-element.51), channel_id=1, source_target_pairs={{8,16},{16,8},{0,24},{24,0},{9,17},{17,9},{1,25},{25,1},{10,18},{1... | collective-permute-start | bytes 73736 | tf_op jit(solution)/shard_map/ppermute | solution.py:529
  18.5 1.6 %collective-permute-start.7 = (bf16[4,240,128]{2,1,0:T(8,128)(2,1)S(1)}, bf16[4,240,128]{2,1,0:T(8,128)(2,1)S(1)}, u32[]{:S(2)}, u32[]{:S(2)}) collective-permute-start(bf16[4,240,128]{2,1,0:T(8,128)(2,1)S(1)} %get-tuple-element.65), channel_id=1, source_target_pairs={{0,8},{8,0},{1,9},{9,1},{2,10},{10,2},{3,11},{11,3},{4,12},{12,4},... | collective-permute-start | bytes 737288 | tf_op jit(solution)/shard_map/ppermute | solution.py:582
  20.2 4.3 %collective-permute-start.8 = (bf16[240,128]{1,0:T(8,128)(2,1)S(1)}, bf16[240,128]{1,0:T(8,128)(2,1)S(1)}, u32[]{:S(2)}, u32[]{:S(2)}) collective-permute-start(bf16[240,128]{1,0:T(8,128)(2,1)S(1)} %get-tuple-element.73), channel_id=1, source_target_pairs={{0,1},{1,0},{2,3},{3,2},{4,5},{5,4},{6,7},{7,6},{8,9},{9,8},{10,11... | collective-permute-start | bytes 184328 | tf_op jit(solution)/shard_map/ppermute | solution.py:585
  21.7 5.5 %collective-permute-start.10 = (bf16[240,128]{1,0:T(8,128)(2,1)S(1)}, bf16[240,128]{1,0:T(8,128)(2,1)S(1)}, u32[]{:S(2)}, u32[]{:S(2)}) collective-permute-start(bf16[240,128]{1,0:T(8,128)(2,1)S(1)} %get-tuple-element.74), channel_id=1, source_target_pairs={{0,17},{1,16},{2,19},{3,18},{4,21},{5,20},{6,23},{7,22},{8,25},{9,... | collective-permute-start | bytes 184328 | tf_op jit(solution)/shard_map/ppermute | solution.py:585
  22.5 4.8 %collective-permute-start.9 = (bf16[240,128]{1,0:T(8,128)(2,1)S(1)}, bf16[240,128]{1,0:T(8,128)(2,1)S(1)}, u32[]{:S(2)}, u32[]{:S(2)}) collective-permute-start(bf16[240,128]{1,0:T(8,128)(2,1)S(1)} %get-tuple-element.75), channel_id=1, source_target_pairs={{0,16},{1,17},{2,18},{3,19},{4,20},{5,21},{6,22},{7,23},{8,24},{9,... | collective-permute-start | bytes 184328 | tf_op jit(solution)/shard_map/ppermute | solution.py:585
  27.3 6.1 %collective-permute-start.13 = (bf16[240,128]{1,0:T(8,128)(2,1)S(1)}, bf16[240,128]{1,0:T(8,128)(2,1)S(1)}, u32[]{:S(2)}, u32[]{:S(2)}) collective-permute-start(bf16[240,128]{1,0:T(8,128)(2,1)S(1)} %fusion.3), channel_id=1, source_target_pairs={{0,6},{1,7},{2,4},{3,5},{4,2},{5,3},{6,0},{7,1},{8,14},{9,15},{10,... | collective-permute-start | bytes 184328 | tf_op jit(solution)/shard_map/ppermute | solution.py:585
  31.0 5.1 %collective-permute-start.12 = (bf16[240,128]{1,0:T(8,128)(2,1)S(1)}, bf16[240,128]{1,0:T(8,128)(2,1)S(1)}, u32[]{:S(2)}, u32[]{:S(2)}) collective-permute-start(bf16[240,128]{1,0:T(8,128)(2,1)S(1)} %fusion.3), channel_id=1, source_target_pairs={{0,4},{1,5},{2,6},{3,7},{4,0},{5,1},{6,2},{7,3},{8,12},{9,13},{10,... | collective-permute-start | bytes 184328 | tf_op jit(solution)/shard_map/ppermute | solution.py:585
  31.0 5.1 %collective-permute-start.11 = (bf16[240,128]{1,0:T(8,128)(2,1)S(1)}, bf16[240,128]{1,0:T(8,128)(2,1)S(1)}, u32[]{:S(2)}, u32[]{:S(2)}) collective-permute-start(bf16[240,128]{1,0:T(8,128)(2,1)S(1)} %fusion.3), channel_id=1, source_target_pairs={{0,2},{1,3},{2,0},{3,1},{4,6},{5,7},{6,4},{7,5},{8,10},{9,11},{10,... | collective-permute-start | bytes 184328 | tf_op jit(solution)/shard_map/ppermute | solution.py:585
  36.2 5.2 %collective-permute-start.16 = (bf16[240,128]{1,0:T(8,128)(2,1)S(1)}, bf16[240,128]{1,0:T(8,128)(2,1)S(1)}, u32[]{:S(2)}, u32[]{:S(2)}) collective-permute-start(bf16[240,128]{1,0:T(8,128)(2,1)S(1)} %add_convert_fusion), channel_id=1, source_target_pairs={{0,17},{1,16},{2,19},{3,18},{4,21},{5,20},{6,23},{7,22},{8,25},{9,... | collective-permute-start | bytes 184328 | tf_op jit(solution)/shard_map/ppermute | solution.py:585
  37.9 4.2 %collective-permute-start.15 = (bf16[240,128]{1,0:T(8,128)(2,1)S(1)}, bf16[240,128]{1,0:T(8,128)(2,1)S(1)}, u32[]{:S(2)}, u32[]{:S(2)}) collective-permute-start(bf16[240,128]{1,0:T(8,128)(2,1)S(1)} %add_convert_fusion), channel_id=1, source_target_pairs={{0,16},{1,17},{2,18},{3,19},{4,20},{5,21},{6,22},{7,23},{8,24},{9,... | collective-permute-start | bytes 184328 | tf_op jit(solution)/shard_map/ppermute | solution.py:585
  39.0 4.2 %collective-permute-start.14 = (bf16[240,128]{1,0:T(8,128)(2,1)S(1)}, bf16[240,128]{1,0:T(8,128)(2,1)S(1)}, u32[]{:S(2)}, u32[]{:S(2)}) collective-permute-start(bf16[240,128]{1,0:T(8,128)(2,1)S(1)} %add_convert_fusion), channel_id=1, source_target_pairs={{0,1},{1,0},{2,3},{3,2},{4,5},{5,4},{6,7},{7,6},{8,9},{9,8},{10,11... | collective-permute-start | bytes 184328 | tf_op jit(solution)/shard_map/ppermute | solution.py:585
  43.2 1.6 %collective-permute-start.17 = (bf16[4,240,128]{2,1,0:T(8,128)(2,1)S(1)}, bf16[4,240,128]{2,1,0:T(8,128)(2,1)S(1)}, u32[]{:S(2)}, u32[]{:S(2)}) collective-permute-start(bf16[4,240,128]{2,1,0:T(8,128)(2,1)S(1)} %pad_maximum_fusion.mine), channel_id=1, source_target_pairs={{0,8},{8,0},{1,9},{9,1},{2,10},{10,2},{3,11},{11,3},{4,12},{12,4},... | collective-permute-start | bytes 737288 | tf_op jit(solution)/shard_map/ppermute | solution.py:605

commit v5 on v4

--- a/solution.py
+++ b/solution.py
@@ -19,25 +19,25 @@
 
 
 def pack_kernel(
-    pair, cot, features, to_core, to_chip, to_even, to_odd, pair_low, pair_high, cot_low, cot_high, work, sides, sems
+    pair, cot, features, to_core, to_chip, to_even, to_odd, pair_low, pair_high, cot_low, cot_high, own, work, sides, sems
 ):
     tile_rows, band_cols, channels = pair.shape
     odd_row = lax.rem(lax.axis_index(ROW), 2)
     odd_col = lax.rem(lax.axis_index("col"), 2)
-    parts = []
+    parts = [
+        (pair.at[:, :SIDE], pair_low),
+        (pair.at[:, band_cols - SIDE :], pair_high),
+        (cot.at[:, :SIDE], cot_low),
+        (cot.at[:, band_cols - SIDE :], cot_high),
+        (features, own),
+    ]
     for target, at_end in ((to_chip, odd_row), (to_core, 1 - odd_row)):
         parts.append((pair.at[pl.ds(at_end * (tile_rows - HALO), HALO)], target.at[:HALO]))
         parts.append((cot.at[pl.ds(at_end * (tile_rows - 1), 1)], target.at[HALO:EDGES]))
-        for part in range(features.shape[1] // channels):
-            parts.append((features.at[:, part * channels : (part + 1) * channels], target.at[EDGES + part]))
-    parts.append((pair.at[:, :SIDE], pair_low))
-    parts.append((pair.at[:, band_cols - SIDE :], pair_high))
-    parts.append((cot.at[:, :SIDE], cot_low))
-    parts.append((cot.at[:, band_cols - SIDE :], cot_high))
     copies = [pltpu.make_async_copy(source, target, sems.at[i]) for i, (source, target) in enumerate(parts)]
-    for copy in copies[-4:] + copies[:-4]:
+    for copy in copies:
         copy.start()
-    for copy in copies[-4:]:
+    for copy in copies[:4]:
         copy.wait()
     for side, (chunk, kind) in enumerate(((pair_low, cot_low), (pair_high, cot_high))):
         for slot, source, column in (
@@ -48,7 +48,12 @@
             sides[side, slot] = work[pl.ds(column, tile_rows, stride=SIDE), :].astype(BF16)
     to_even[...] = sides[1 - odd_col]
     to_odd[...] = sides[odd_col]
-    for copy in copies[:-4]:
+    copies[4].wait()
+    for part in range(features.shape[1] // channels):
+        values = own[:, part * channels : (part + 1) * channels]
+        to_chip[EDGES + part] = values
+        to_core[EDGES + part] = values
+    for copy in copies[5:]:
         copy.wait()
 
 
@@ -65,7 +70,7 @@
 
 def weights_kernel(
     valid, context, proj_weight, conv_weight,
-    window, rows_valid, forward, backward, projection, context_key, context_turned,
+    window, rows_valid, forward, backward, projection, context_key,
 ):
     channels = window.shape[1]
     bins = valid.shape[0]
@@ -95,11 +100,10 @@
             backward[at : at + channels, lanes] = turned
     projection[...] = proj_weight[...]
     context_key[...] = jnp.dot(context[...], proj_weight[:, channels:], preferred_element_type=F32).astype(BF16)
-    context_turned[...] = context[...].astype(F32).T.astype(BF16)
 
 
 def prepare_kernel(projection, context_key, *refs):
-    sources, (features_turned, query, key, features, query_rows, key_rows) = refs[:-6], refs[-6:]
+    sources, (features, query, key, query_rows, key_rows) = refs[:-5], refs[-5:]
     channels = query.shape[1]
     all_bins, tail = features.shape[0], context_key.shape[0]
     row, col = lax.axis_index(ROW), lax.axis_index("col")
@@ -124,7 +128,13 @@
     key_rows[MARGIN + all_bins : MARGIN + all_bins + tail, :] = context_key[...].astype(F32)
     query[...] = query_rows[pl.ds(pl.multiple_of(row_start, 16), query.shape[0]), :]
     key[...] = key_rows[pl.ds(pl.multiple_of(col_start, 16), key.shape[0]), :]
-    features_turned[...] = features[...].astype(F32).T.astype(BF16)
+
+
+def half_of(parts):
+    core = lax.axis_index("core")
+    if parts == 1:
+        return core
+    return lax.rem(core + lax.axis_index("rx") + lax.axis_index("col"), 2)
 
 
 def quarter_of(parts):
@@ -159,7 +169,7 @@
 
 
 def silu_parts(conv):
-    sigma = jax.nn.sigmoid(conv)
+    sigma = 0.5 + 0.5 * jnp.tanh(0.5 * conv)
     return conv * sigma, sigma * (1.0 + conv * (1.0 - sigma))
 
 
@@ -176,7 +186,7 @@
 
 def inner_kernel(
     pair, cot, sides, query, key, window, rows_valid, forward,
-    mixed3, carry3, own, output,
+    mixed3, carry3, own, active,
     mixed, carry,
 ):
     tile_rows, band_cols, channels = pair.shape
@@ -226,30 +236,25 @@
             values = carry[here, :] * slope[at : at + PITCH, lanes]
             carry[here, :] = values
             own[index * PITCH : (index + 1) * PITCH, :] = keep_inner(values, band_cols)
-            output[index] = (
-                pair[index].astype(F32) + mask_of(index) * activated[at + PAD : at + PAD + band_cols, lanes]
-            ).astype(BF16)
+            active[index] = activated[at + PAD : at + PAD + band_cols, lanes]
         first += 2 * pairs
     spread(carry, carry3, 1, tile_rows - 1, 0, -1)
 
 
 def outer_kernel(
     pair, cot, from_core, from_chip, sides, corner_core, corner_chip, query, key, window, rows_valid, forward, backward,
-    mixed3, carry3, own, output,
-    pair_output, pair_grad, keep, send,
-    near, corners, mixed, carry, mixed3_ends, carry3_ends, own_ends, output_ends, skew, totals, grad, sems,
+    mixed3, carry3, own,
+    active_ends, change, keep, send,
+    near, corners, mixed, carry, mixed3_ends, carry3_ends, own_ends, skew, totals,
 ):
     tile_rows, band_cols, channels = pair.shape
     row, col = lax.axis_index(ROW), lax.axis_index("col")
-    core = lax.axis_index("core")
     all_bins = lax.axis_size(ROW) * tile_rows
     tail = lax.axis_size("col") * band_cols
     row_start = row * tile_rows
     col_start = row_start + col * band_cols
     odd_row = lax.rem(row, 2)
     last = tile_rows - 1
-    write_output = pltpu.make_async_copy(output.at[1:last], pair_output.at[1:last], sems.at[0])
-    write_output.start()
     near[1 - odd_row] = from_core[:EDGES]
     near[odd_row] = from_chip[:EDGES]
     corners[1 - odd_row] = corner_core[...]
@@ -312,14 +317,8 @@
         if 0 <= index <= last:
             half = position // 2
             own_ends[half * PITCH : (half + 1) * PITCH, :] = keep_inner(values, band_cols)
-            output_ends[half] = (
-                pair[index].astype(F32) + mask_of(index) * activated[at + PAD : at + PAD + band_cols, lanes]
-            ).astype(BF16)
+            active_ends[half] = activated[at + PAD : at + PAD + band_cols, lanes]
     spread(carry, carry3_ends, 0, 4, 0, -1)
-    write_first = pltpu.make_async_copy(output_ends.at[0], pair_output.at[0], sems.at[1])
-    write_last = pltpu.make_async_copy(output_ends.at[1], pair_output.at[last], sems.at[2])
-    write_first.start()
-    write_last.start()
     carry_sources = [
         (carry3, 0, range(1, last)), (carry3_ends, -1, (-1, 0)), (carry3_ends, tile_rows - 3, (last, tile_rows)),
     ]
@@ -337,11 +336,9 @@
             lanes = slice(offset % 2 * channels, (offset % 2 + 1) * channels)
             at = offset // 2 * PITCH + PAD
             masked = mask_of(index) * back[at : at + band_cols, lanes]
-            grad[index] = (cot[index].astype(F32) + masked).astype(BF16)
+            change[index] = masked
             query_rows.append(jnp.sum(masked, axis=0, keepdims=True))
             skew[index % 8, index - index % 8 : index - index % 8 + band_cols, :] += masked
-    write_grad = pltpu.make_async_copy(grad, pair_grad, sems.at[3])
-    write_grad.start()
     totals[pl.ds(pl.multiple_of(query_at + row_start, 16), tile_rows), :] = jnp.concatenate(query_rows, axis=0)
     reach = tile_rows + band_cols - 8
     for step in range(8):
@@ -362,12 +359,26 @@
     for tap in range(9):
         totals[tap * channels : (tap + 1) * channels, :] = grads[:, tap * channels : (tap + 1) * channels]
     parts, size = keep.shape[:2]
+    mine = half_of(parts)
     for part in range(parts):
         place = lax.bitwise_xor(quarter_of(parts), part)
-        keep[part] = totals[pl.ds(pl.multiple_of((core * parts + place) * size, 16), size), :]
-        send[part] = totals[pl.ds(pl.multiple_of(((1 - core) * parts + place) * size, 16), size), :].astype(BF16)
-    for copy in (write_output, write_first, write_last, write_grad):
-        copy.wait()
+        keep[part] = totals[pl.ds(pl.multiple_of((mine * parts + place) * size, 16), size), :]
+        send[part] = totals[pl.ds(pl.multiple_of(((1 - mine) * parts + place) * size, 16), size), :].astype(BF16)
+
+
+def late_kernel(
+    pair, cot, active, active_ends, change, window, rows_valid, features, context,
+    pair_output, pair_grad, features_turned, context_turned,
+):
+    tile_rows, band_cols, _ = pair.shape
+    last = tile_rows - 1
+    for index in range(tile_rows):
+        mask = window[pl.ds(MARGIN + index, band_cols), :] * rows_valid[pl.ds(index + HALO, 1), :]
+        values = active_ends[0] if index == 0 else active_ends[1] if index == last else active[index]
+        pair_output[index] = (pair[index].astype(F32) + mask * values).astype(BF16)
+        pair_grad[index] = (cot[index].astype(F32) + change[index]).astype(BF16)
+    features_turned[...] = features[...].astype(F32).T.astype(BF16)
+    context_turned[...] = context[...].astype(F32).T.astype(BF16)
 
 
 def add_kernel(pieces, copies):
@@ -378,18 +389,20 @@
 
 
 def finish_kernel(
-    mine, theirs, features_turned, context_turned, projection, feature_grad, proj_grad, conv_grad,
-    whole, feature_out, proj_out, conv_out, sems,
+    features_turned, context_turned, projection, *refs
 ):
-    core = lax.axis_index("core")
+    *pieces, feature_grad, proj_grad, conv_grad, whole, feature_out, proj_out, conv_out, sems = refs
+    parts = len(pieces) // 2
+    mine, theirs = pieces[:parts], pieces[parts:]
     row = lax.axis_index(ROW)
-    parts, size, channels = mine.shape
+    size, channels = mine[0].shape
     all_bins, tail = features_turned.shape[1], context_turned.shape[1]
     tile_rows = feature_grad.shape[0]
+    half = half_of(parts)
     for part in range(parts):
         place = lax.bitwise_xor(quarter_of(parts), part)
-        whole[pl.ds(pl.multiple_of((core * parts + place) * size, 16), size), :] = mine[part]
-        whole[pl.ds(pl.multiple_of(((1 - core) * parts + place) * size, 16), size), :] = theirs[part]
+        whole[pl.ds(pl.multiple_of((half * parts + place) * size, 16), size), :] = mine[part][...]
+        whole[pl.ds(pl.multiple_of(((1 - half) * parts + place) * size, 16), size), :] = theirs[part][...]
     copies = [
         pltpu.make_async_copy(source, target, sems.at[index])
         for index, (source, target) in enumerate(((conv_out, conv_grad), (proj_out, proj_grad), (feature_out, feature_grad)))
@@ -452,9 +465,10 @@
         out_specs=(vmem,) * 4,
         scratch_shapes=[
             chunk, chunk, chunk, chunk,
+            pltpu.VMEM(bin_features.shape, BF16),
             pltpu.VMEM((tile_rows * SIDE, channels), F32),
             pltpu.VMEM((2, EDGES, tile_rows, channels), BF16),
-            pltpu.SemaphoreType.DMA((2 * layers + 4,)),
+            pltpu.SemaphoreType.DMA((9,)),
         ],
         compiler_params=PARAMS,
         name="pack",
@@ -477,7 +491,7 @@
     from_core = lax.ppermute(to_core, "core", other_core)
     near_bins = tile_rows + band_cols + 2 * MARGIN
     valid_bins, from_chip = lax.optimization_barrier((valid_bins, from_chip))
-    window, rows_valid, forward, backward, projection, context_key, context_turned = pl.pallas_call(
+    window, rows_valid, forward, backward, projection, context_key = pl.pallas_call(
         weights_kernel,
         out_shape=(
             shape(near_bins, channels, dtype=F32),
@@ -486,10 +500,9 @@
             shape(12 * channels, 2 * channels),
             shape(*proj_weight.shape),
             shape(tail, channels),
-            shape(width, tail),
         ),
         in_specs=[vmem] * 4,
-        out_specs=(vmem,) * 7,
+        out_specs=(vmem,) * 6,
         compiler_params=PARAMS,
         cost_estimate=pl.CostEstimate(flops=1 << 30, bytes_accessed=1 << 21, transcendentals=0),
         name="weights",
@@ -499,17 +512,16 @@
     else:
         sources = [lax.all_gather(bin_features, ROW, axis=0, tiled=True)]
 
-    features_turned, query, key = pl.pallas_call(
+    features, query, key = pl.pallas_call(
         prepare_kernel,
         out_shape=(
-            shape(width, all_bins),
+            shape(all_bins, width),
             shape(tile_rows + 2 * MARGIN, channels, dtype=F32),
             shape(near_bins, channels, dtype=F32),
         ),
         in_specs=[vmem] * (2 + len(sources)),
         out_specs=(vmem,) * 3,
         scratch_shapes=[
-            pltpu.VMEM((all_bins, width), BF16),
             pltpu.VMEM((all_bins + 2 * MARGIN, channels), F32),
             pltpu.VMEM((all_bins + tail + 2 * MARGIN, channels), F32),
         ],
@@ -537,10 +549,11 @@
     else:
         parts, half = 1, -(-total_rows // (32 * chips)) * 16 * chips
     span = tile_rows * PITCH
-    inner = pl.pallas_call(
+    *inner, active = pl.pallas_call(
         inner_kernel,
         out_shape=(
-            shape(span, 3 * channels), shape(span, 3 * channels), shape(span, channels), shape(*pair_input.shape),
+            shape(span, 3 * channels), shape(span, 3 * channels), shape(span, channels),
+            shape(*pair_input.shape, dtype=F32),
         ),
         in_specs=[vmem] * 8,
         out_specs=(vmem,) * 4,
@@ -548,16 +561,16 @@
         compiler_params=PARAMS,
         name="inner",
     )(pair_input, cotangent, sides, query, key, window, rows_valid, forward)
-    pair_output, pair_grad, keep, send = pl.pallas_call(
+    active_ends, change, keep, send = pl.pallas_call(
         outer_kernel,
         out_shape=(
-            shape(*pair_input.shape),
-            shape(*pair_input.shape),
+            shape(2, band_cols, channels, dtype=F32),
+            shape(*pair_input.shape, dtype=F32),
             shape(parts, half // parts, channels, dtype=F32),
             shape(parts, half // parts, channels),
         ),
-        in_specs=[vmem] * 17,
-        out_specs=(anywhere, anywhere, vmem, vmem),
+        in_specs=[vmem] * 16,
+        out_specs=(vmem,) * 4,
         scratch_shapes=[
             pltpu.VMEM((2, EDGES, tile_rows, channels), BF16),
             pltpu.VMEM((2, 2, EDGES, SIDE, channels), BF16),
@@ -566,11 +579,8 @@
             pltpu.VMEM((4 * PITCH, 3 * channels), BF16),
             pltpu.VMEM((4 * PITCH, 3 * channels), BF16),
             pltpu.VMEM((2 * PITCH, channels), BF16),
-            pltpu.VMEM((2, band_cols, channels), BF16),
             pltpu.VMEM((8, tile_rows + band_cols, channels), F32),
             pltpu.VMEM((2 * half, channels), F32),
-            pltpu.VMEM(pair_input.shape, BF16),
-            pltpu.SemaphoreType.DMA((4,)),
         ],
         compiler_params=PARAMS,
         name="outer",
@@ -578,18 +588,33 @@
         pair_input, cotangent, from_core, from_chip, sides, corner_core, corner_chip, query, key, window, rows_valid,
         forward, backward, *inner,
     )
+    pair_output, pair_grad, features_turned, context_turned = pl.pallas_call(
+        late_kernel,
+        out_shape=(
+            shape(*pair_input.shape), shape(*pair_input.shape), shape(width, all_bins), shape(width, tail),
+        ),
+        in_specs=[vmem] * 9,
+        out_specs=(vmem,) * 4,
+        compiler_params=PARAMS,
+        name="late",
+    )(
+        pair_input, cotangent, active, active_ends, change, window, rows_valid, features,
+        *in_hbm(context_features),
+    )
 
     halves = keep + lax.ppermute(send, "core", other_core).astype(F32)
     if staged:
         def across(values, bits):
             return lax.ppermute(values, ROW + ("col",), [(index, index ^ bits) for index in range(32)])
 
-        plane = (1, 16, 17)
+        plane = (1 + 8, 16 + 8, 16 + 1)
         got = [across(halves[part].astype(BF16), bits).astype(F32) for part, bits in enumerate(plane, 1)]
         mine = (halves[0] + got[0] + got[1] + got[2]).astype(BF16)
-        near, far, opposite = [across(mine, bits).astype(F32) for bits in (2, 4, 6)]
+        near, far, opposite = [across(mine, bits) for bits in (2, 4, 6)]
+        far, pair_output = lax.optimization_barrier((far, pair_output))
+        near, far, opposite = near.astype(F32), far.astype(F32), opposite.astype(F32)
         mine = ((mine.astype(F32) + near) + (far + opposite)).astype(BF16)
-        mine = jnp.stack([mine] + [across(mine, bits) for bits in plane])
+        mine = [mine] + [across(mine, bits) for bits in plane]
     else:
         piece = half // chips
         pieces = lax.all_to_all(halves.astype(BF16).reshape(chips, piece, channels), CHIPS, 0, 0)
@@ -601,8 +626,8 @@
             compiler_params=PARAMS,
             name="add",
         )(pieces)
-        mine = lax.all_to_all(copies, CHIPS, 0, 0).reshape(1, half, channels)
-    theirs = lax.ppermute(mine, "core", other_core)
+        mine = [lax.all_to_all(copies, CHIPS, 0, 0).reshape(half, channels)]
+    theirs = [lax.ppermute(part, "core", other_core) for part in mine]
 
     feature_grad, proj_grad, conv_grad = pl.pallas_call(
         finish_kernel,
@@ -611,7 +636,7 @@
             shape(*proj_weight.shape, dtype=F32),
             shape(*conv_weight.shape, dtype=F32),
         ),
-        in_specs=[vmem] * 5,
+        in_specs=[vmem] * (3 + 2 * len(mine)),
         out_specs=(anywhere,) * 3,
         scratch_shapes=[
             pltpu.VMEM((2 * half, channels), BF16),
@@ -622,7 +647,7 @@
         ],
         compiler_params=PARAMS,
         name="finish",
-    )(mine, theirs, features_turned, context_turned, projection)
+    )(features_turned, context_turned, projection, *mine, *theirs)
     return (pair_output, pair_grad, feature_grad, proj_grad, conv_grad)
 
 

time: 46.4 us -> 45 us (0.970)
  waiting for transfers between devices: 14.9 us -> 12.2 us
  Pallas kernels: 11.1 us -> 13 us
  starting transfers between devices: 19.3 us -> 18.7 us
    pallas_call x2 -> x3, Pallas kernels: 3.61 us -> 5.84 us  [the longest x1 3.16 us: body(): pl.pallas_call(outer_kernel, out_shape=(shape(2, band_cols, channels, dty...]
    ppermute x9, waiting for transfers between devices: 11.4 us -> 9.21 us  [across(): lax.ppermute(values, ROW + ('col',), [(index, index ^ bits) for index in...]
    ppermute x9, starting transfers between devices: 11.6 us -> 10.5 us  [across(): lax.ppermute(values, ROW + ('col',), [(index, index ^ bits) for index in...]
    ppermute x1 -> x4, waiting for transfers between devices: 1.5 us -> 0.9 us  [body(): theirs = [lax.ppermute(part, 'core', other_core) for part in mine]]
  transfers between devices with their start and end apart: 18 -> 21, of which waited for: 10 -> 12; matrix products, arithmetic and copies ran while one was open for 0% -> 0% of each run, Pallas kernels for 10% -> 15%
where the time goes in v5:
time: 45 us; the launch traced here: 44.8 us
  starting transfers between devices  18.7 us (42%)
  Pallas kernels  13 us (29%)
  waiting for transfers between devices  12.2 us (27%)
  between operations  0.76 us (2%)
    ppermute x9, starting transfers between devices, across(): lax.ppermute(values, ROW + ('col',), [(index, index ^ bits) for index in...  10.5 us
    ppermute x9, waiting for transfers between devices, across(): lax.ppermute(values, ROW + ('col',), [(index, index ^ bits) for index in...  9.21 us
    pallas_call x1, Pallas kernels, body(): pl.pallas_call(outer_kernel, out_shape=(shape(2, band_cols, channels, dty...  3.16 us
    pallas_call x1, Pallas kernels, body(): pl.pallas_call(inner_kernel, out_shape=(shape(span, 3 * channels), shape(...  2.53 us
    ppermute x1, starting transfers between devices, body(): from_chip = lax.ppermute(to_chip, ROW, odd_rows + ends)  2.44 us
    pallas_call x1, Pallas kernels, body(): pl.pallas_call(late_kernel, out_shape=(shape(*pair_input.shape), shape(*p...  2.43 us
    ppermute x1, starting transfers between devices, body(): corner_chip = lax.ppermute(corner_to_chip, ROW, odd_rows + ends)  2.17 us
    pallas_call x1, Pallas kernels, body(): pl.pallas_call(weights_kernel, out_shape=(shape(near_bins, channels, dtyp...  1.69 us
  transfers between devices with their start and end apart: 21, of which 12 were waited for; matrix products, arithmetic and copies ran while one was open for 0% of the time, Pallas kernels for 15%

profile of v5, /device:TPU:0, one launch (start us, length us, event | category | flops | bytes accessed | tf_op | source)
XLA Modules:
  0.0 44.8 jit_solution(17067828482353855749)
XLA Ops:
  0.6 1.5 %pack.1 = (bf16[7,48,128]{2,1,0:T(8,128)(2,1)S(1)}, bf16[7,48,128]{2,1,0:T(8,128)(2,1)S(1)}, bf16[3,48,128]{2,1,0:T(8,128)(2,1)S(1)}, bf16[3,48,128]{2,1,0:T(8,128)(2,1)S(1)}) custom-call(bf16[48,48,128]{2,1,0:T(8,128)(2,1)} %pair.7, bf16[48,48,128]{2,1,0:T(8,128)(2,1)} %cot.7, bf16[48,512]{1,0:T(8,128)(2,1)} %features.1), custom_call_target="tpu_custom_call" | custom-call | tf_op jit(solution)/shard_map/pack/pallas_call | solution.py:456
  2.1 2.4 %collective-permute-start.1 = (bf16[7,48,128]{2,1,0:T(8,128)(2,1)S(1)}, bf16[7,48,128]{2,1,0:T(8,128)(2,1)S(1)}, u32[]{:S(2)}, u32[]{:S(2)}) collective-permute-start(bf16[7,48,128]{2,1,0:T(8,128)(2,1)S(1)} %get-tuple-element.44), channel_id=1, source_target_pairs={{8,16},{16,8},{0,24},{24,0},{9,17},{17,9},{1,25},{25,1},{10,18},{1... | collective-permute-start | bytes 258056 | tf_op jit(solution)/shard_map/ppermute | solution.py:488
  4.5 1.5 %collective-permute-start.2 = (bf16[3,48,128]{2,1,0:T(8,128)(2,1)S(1)}, bf16[3,48,128]{2,1,0:T(8,128)(2,1)S(1)}, u32[]{:S(2)}, u32[]{:S(2)}) collective-permute-start(bf16[3,48,128]{2,1,0:T(8,128)(2,1)S(1)} %get-tuple-element.46), channel_id=1, source_target_pairs={{0,1},{1,0},{2,3},{3,2},{4,5},{5,4},{6,7},{7,6},{8,9},{9,8},{10,11... | collective-permute-start | bytes 110600 | tf_op jit(solution)/shard_map/ppermute | solution.py:490
  6.6 0.9 %collective-permute-done.1.refs_2_.from_chip = bf16[7,48,128]{2,1,0:T(8,128)(2,1)S(1)} collective-permute-done((bf16[7,48,128]{2,1,0:T(8,128)(2,1)S(1)}, bf16[7,48,128]{2,1,0:T(8,128)(2,1)S(1)}, u32[]{:S(2)}, u32[]{:S(2)}) %collective-permute-start.1) | collective-permute-done | bytes 86048 | tf_op jit(solution)/shard_map/ppermute | solution.py:488
  7.6 1.7 %weights.1 = (f32[128,128]{1,0:T(8,128)S(1)}, f32[56,128]{1,0:T(8,128)S(1)}, bf16[1536,256]{1,0:T(8,128)(2,1)S(1)}, bf16[1536,256]{1,0:T(8,128)(2,1)S(1)}, bf16[...) custom-call(s32[576]{0:T(1024)} %valid, bf16[384,512]{1,0:T(8,128)(2,1)} %context.3, bf16[512,256]{1,0:T(8,128)(2,1)} %proj_weight.1, ...), custom_call_target="tpu_custom_call" | custom-call | flops 1073741824 | bytes 2097152 | tf_op jit(solution)/shard_map/weights/pallas_call | solution.py:494
  9.6 0.5 %collective-permute-start.5 = (bf16[2,3,16,128]{3,2,1,0:T(8,128)(2,1)S(1)}, bf16[2,3,16,128]{3,2,1,0:T(8,128)(2,1)S(1)}, u32[]{:S(2)}, u32[]{:S(2)}) collective-permute-start(bf16[2,3,16,128]{3,2,1,0:T(8,128)(2,1)S(1)} %get-tuple-element.55), channel_id=1, source_target_pairs={{0,8},{8,0},{1,9},{9,1},{2,10},{10,2},{3,11},{11,3},{4,12},{12,4},... | collective-permute-start | bytes 73736 | tf_op jit(solution)/shard_map/ppermute | solution.py:542
  10.1 2.2 %collective-permute-start.6 = (bf16[2,3,16,128]{3,2,1,0:T(8,128)(2,1)S(1)}, bf16[2,3,16,128]{3,2,1,0:T(8,128)(2,1)S(1)}, u32[]{:S(2)}, u32[]{:S(2)}) collective-permute-start(bf16[2,3,16,128]{3,2,1,0:T(8,128)(2,1)S(1)} %get-tuple-element.56), channel_id=1, source_target_pairs={{8,16},{16,8},{0,24},{24,0},{9,17},{17,9},{1,25},{25,1},{10,18},{1... | collective-permute-start | bytes 73736 | tf_op jit(solution)/shard_map/ppermute | solution.py:541
  12.2 2.5 %inner.1 = (bf16[3072,384]{1,0:T(8,128)(2,1)S(1)}, bf16[3072,384]{1,0:T(8,128)(2,1)S(1)}, bf16[3072,128]{1,0:T(8,128)(2,1)S(1)}, f32[48,48,128]{2,1,0:T(8,128)S(1)}) custom-call(bf16[48,48,128]{2,1,0:T(8,128)(2,1)S(1)} %copy-done, bf16[48,48,128]{2,1,0:T(8,128)(2,1)S(1)} %copy-done.1, bf16[2,3,48,128]{3,2,1,0:T(8,128)(2,1)S(1)} %get-tuple-element.54.sides, ...), custom_call_target="tpu_custom_call" | custom-call | tf_op jit(solution)/shard_map/inner/pallas_call | solution.py:552
  14.8 3.2 %outer.1 = (f32[2,48,128]{2,1,0:T(8,128)S(1)}, f32[48,48,128]{2,1,0:T(8,128)S(1)}, f32[4,240,128]{2,1,0:T(8,128)S(1)}, bf16[4,240,128]{2,1,0:T(8,128)(2,1)S(1)}) custom-call(bf16[48,48,128]{2,1,0:T(8,128)(2,1)S(1)} %copy-done, bf16[48,48,128]{2,1,0:T(8,128)(2,1)S(1)} %copy-done.1, bf16[7,48,128]{2,1,0:T(8,128)(2,1)S(1)} %collective-permute-done.refs_1_.from_core, ...), custom_call_target="tpu_custom_call" | custom-call | tf_op jit(solution)/shard_map/outer/pallas_call | solution.py:564
  18.0 0.5 %collective-permute-start.7 = (bf16[4,240,128]{2,1,0:T(8,128)(2,1)S(1)}, bf16[4,240,128]{2,1,0:T(8,128)(2,1)S(1)}, u32[]{:S(2)}, u32[]{:S(2)}) collective-permute-start(bf16[4,240,128]{2,1,0:T(8,128)(2,1)S(1)} %get-tuple-element.67), channel_id=1, source_target_pairs={{0,8},{8,0},{1,9},{9,1},{2,10},{10,2},{3,11},{11,3},{4,12},{12,4},... | collective-permute-start | bytes 737288 | tf_op jit(solution)/shard_map/ppermute | solution.py:605
  18.4 1.1 %collective-permute-done.7 = bf16[4,240,128]{2,1,0:T(8,128)(2,1)S(1)} collective-permute-done((bf16[4,240,128]{2,1,0:T(8,128)(2,1)S(1)}, bf16[4,240,128]{2,1,0:T(8,128)(2,1)S(1)}, u32[]{:S(2)}, u32[]{:S(2)}) %collective-permute-start.7) | collective-permute-done | bytes 245792 | tf_op jit(solution)/shard_map/ppermute | solution.py:605
  19.7 1.6 %collective-permute-start.8 = (bf16[240,128]{1,0:T(8,128)(2,1)S(1)}, bf16[240,128]{1,0:T(8,128)(2,1)S(1)}, u32[]{:S(2)}, u32[]{:S(2)}) collective-permute-start(bf16[240,128]{1,0:T(8,128)(2,1)S(1)} %get-tuple-element.83), channel_id=1, source_target_pairs={{0,9},{1,8},{2,11},{3,10},{4,13},{5,12},{6,15},{7,14},{8,1},{9,0},... | collective-permute-start | bytes 184328 | tf_op jit(solution)/shard_map/ppermute | solution.py:608
  21.2 0.7 %collective-permute-start.10 = (bf16[240,128]{1,0:T(8,128)(2,1)S(1)}, bf16[240,128]{1,0:T(8,128)(2,1)S(1)}, u32[]{:S(2)}, u32[]{:S(2)}) collective-permute-start(bf16[240,128]{1,0:T(8,128)(2,1)S(1)} %get-tuple-element.84), channel_id=1, source_target_pairs={{0,17},{1,16},{2,19},{3,18},{4,21},{5,20},{6,23},{7,22},{8,25},{9,... | collective-permute-start | bytes 184328 | tf_op jit(solution)/shard_map/ppermute | solution.py:608
  21.9 0.8 %collective-permute-start.9 = (bf16[240,128]{1,0:T(8,128)(2,1)S(1)}, bf16[240,128]{1,0:T(8,128)(2,1)S(1)}, u32[]{:S(2)}, u32[]{:S(2)}) collective-permute-start(bf16[240,128]{1,0:T(8,128)(2,1)S(1)} %get-tuple-element.85), channel_id=1, source_target_pairs={{0,24},{1,25},{2,26},{3,27},{4,28},{5,29},{6,30},{7,31},{8,16},{9,... | collective-permute-start | bytes 184328 | tf_op jit(solution)/shard_map/ppermute | solution.py:608
  22.7 0.9 %collective-permute-done.8 = bf16[240,128]{1,0:T(8,128)(2,1)S(1)} collective-permute-done((bf16[240,128]{1,0:T(8,128)(2,1)S(1)}, bf16[240,128]{1,0:T(8,128)(2,1)S(1)}, u32[]{:S(2)}, u32[]{:S(2)}) %collective-permute-start.8) | collective-permute-done | bytes 61472 | tf_op jit(solution)/shard_map/ppermute | solution.py:608
  23.6 3.3 %collective-permute-done.10 = bf16[240,128]{1,0:T(8,128)(2,1)S(1)} collective-permute-done((bf16[240,128]{1,0:T(8,128)(2,1)S(1)}, bf16[240,128]{1,0:T(8,128)(2,1)S(1)}, u32[]{:S(2)}, u32[]{:S(2)}) %collective-permute-start.10) | collective-permute-done | bytes 61472 | tf_op jit(solution)/shard_map/ppermute | solution.py:608
  26.9 2.7 %collective-permute-start.11 = (bf16[240,128]{1,0:T(8,128)(2,1)S(1)}, bf16[240,128]{1,0:T(8,128)(2,1)S(1)}, u32[]{:S(2)}, u32[]{:S(2)}) collective-permute-start(bf16[240,128]{1,0:T(8,128)(2,1)S(1)} %fusion.3), channel_id=1, source_target_pairs={{0,4},{1,5},{2,6},{3,7},{4,0},{5,1},{6,2},{7,3},{8,12},{9,13},{10,... | collective-permute-start | bytes 184328 | tf_op jit(solution)/shard_map/ppermute | solution.py:608
  29.6 1.3 %collective-permute-start.13 = (bf16[240,128]{1,0:T(8,128)(2,1)S(1)}, bf16[240,128]{1,0:T(8,128)(2,1)S(1)}, u32[]{:S(2)}, u32[]{:S(2)}) collective-permute-start(bf16[240,128]{1,0:T(8,128)(2,1)S(1)} %fusion.3), channel_id=1, source_target_pairs={{0,6},{1,7},{2,4},{3,5},{4,2},{5,3},{6,0},{7,1},{8,14},{9,15},{10,... | collective-permute-start | bytes 184328 | tf_op jit(solution)/shard_map/ppermute | solution.py:608
  31.1 2.4 %late.1 = (bf16[48,48,128]{2,1,0:T(8,128)(2,1)}, bf16[48,48,128]{2,1,0:T(8,128)(2,1)}, bf16[512,192]{1,0:T(8,128)(2,1)S(1)}, bf16[512,384]{1,0:T(8,128)(2,1)S(1)}) custom-call(bf16[48,48,128]{2,1,0:T(8,128)(2,1)S(1)} %copy-done, bf16[48,48,128]{2,1,0:T(8,128)(2,1)S(1)} %copy-done.1, f32[48,48,128]{2,1,0:T(8,128)S(1)} %get-tuple-element.68.active, ...), custom_call_target="tpu_custom_call" | custom-call | tf_op jit(solution)/shard_map/late/pallas_call | solution.py:591
  33.7 2.1 %collective-permute-done.13 = bf16[240,128]{1,0:T(8,128)(2,1)S(1)} collective-permute-done((bf16[240,128]{1,0:T(8,128)(2,1)S(1)}, bf16[240,128]{1,0:T(8,128)(2,1)S(1)}, u32[]{:S(2)}, u32[]{:S(2)}) %collective-permute-start.13) | collective-permute-done | bytes 61472 | tf_op jit(solution)/shard_map/ppermute | solution.py:608
  35.9 1.8 %collective-permute-start.16 = (bf16[240,128]{1,0:T(8,128)(2,1)S(1)}, bf16[240,128]{1,0:T(8,128)(2,1)S(1)}, u32[]{:S(2)}, u32[]{:S(2)}) collective-permute-start(bf16[240,128]{1,0:T(8,128)(2,1)S(1)} %add_convert_fusion.refs_0_), channel_id=1, source_target_pairs={{0,17},{1,16},{2,19},{3,18},{4,21},{5,20},{6,23},{7,22},{8,25},{9,... | collective-permute-start | bytes 184328 | tf_op jit(solution)/shard_map/ppermute | solution.py:608
  37.7 1.5 %collective-permute-start.14 = (bf16[240,128]{1,0:T(8,128)(2,1)S(1)}, bf16[240,128]{1,0:T(8,128)(2,1)S(1)}, u32[]{:S(2)}, u32[]{:S(2)}) collective-permute-start(bf16[240,128]{1,0:T(8,128)(2,1)S(1)} %add_convert_fusion.refs_0_), channel_id=1, source_target_pairs={{0,9},{1,8},{2,11},{3,10},{4,13},{5,12},{6,15},{7,14},{8,1},{9,0},... | collective-permute-start | bytes 184328 | tf_op jit(solution)/shard_map/ppermute | solution.py:608
  39.2 2.4 %collective-permute-done.16.refs_3_ = bf16[240,128]{1,0:T(8,128)(2,1)S(1)} collective-permute-done((bf16[240,128]{1,0:T(8,128)(2,1)S(1)}, bf16[240,128]{1,0:T(8,128)(2,1)S(1)}, u32[]{:S(2)}, u32[]{:S(2)}) %collective-permute-start.16) | collective-permute-done | bytes 61472 | tf_op jit(solution)/shard_map/ppermute | solution.py:608
  43.3 1.5 %finish.1 = (bf16[48,512]{1,0:T(8,128)(2,1)}, f32[512,256]{1,0:T(8,128)}, f32[9,128,128]{2,1,0:T(8,128)}) custom-call(bf16[512,192]{1,0:T(8,128)(2,1)S(1)} %get-tuple-element.75.features_turned, bf16[512,384]{1,0:T(8,128)(2,1)S(1)} %get-tuple-element.76.context_turned, bf16[512,256]{1,0:T(8,128)(2,1)S(1)} %get-tuple-element.49.projection, ...), custom_call_target="tpu_custom_call" | custom-call | tf_op jit(solution)/shard_map/finish/pallas_call | solution.py:632
  (34 shorter events, 3.2 us)
Async XLA Ops:
  2.1 5.4 %collective-permute-start.1 = (bf16[7,48,128]{2,1,0:T(8,128)(2,1)S(1)}, bf16[7,48,128]{2,1,0:T(8,128)(2,1)S(1)}, u32[]{:S(2)}, u32[]{:S(2)}) collective-permute-start(bf16[7,48,128]{2,1,0:T(8,128)(2,1)S(1)} %get-tuple-element.44), channel_id=1, source_target_pairs={{8,16},{16,8},{0,24},{24,0},{9,17},{17,9},{1,25},{25,1},{10,18},{1... | collective-permute-start | bytes 258056 | tf_op jit(solution)/shard_map/ppermute | solution.py:488
  4.5 5.0 %collective-permute-start.2 = (bf16[3,48,128]{2,1,0:T(8,128)(2,1)S(1)}, bf16[3,48,128]{2,1,0:T(8,128)(2,1)S(1)}, u32[]{:S(2)}, u32[]{:S(2)}) collective-permute-start(bf16[3,48,128]{2,1,0:T(8,128)(2,1)S(1)} %get-tuple-element.46), channel_id=1, source_target_pairs={{0,1},{1,0},{2,3},{3,2},{4,5},{5,4},{6,7},{7,6},{8,9},{9,8},{10,11... | collective-permute-start | bytes 110600 | tf_op jit(solution)/shard_map/ppermute | solution.py:490
  6.1 3.5 %collective-permute-start.3 = (bf16[3,48,128]{2,1,0:T(8,128)(2,1)S(1)}, bf16[3,48,128]{2,1,0:T(8,128)(2,1)S(1)}, u32[]{:S(2)}, u32[]{:S(2)}) collective-permute-start(bf16[3,48,128]{2,1,0:T(8,128)(2,1)S(1)} %get-tuple-element.47), channel_id=1, source_target_pairs={{0,8},{1,2},{2,1},{3,4},{4,3},{5,6},{6,5},{7,15},{8,0},{9,10},{10,... | collective-permute-start | bytes 110600 | tf_op jit(solution)/shard_map/ppermute | solution.py:489
  6.5 5.8 %copy-start = (bf16[48,48,128]{2,1,0:T(8,128)(2,1)S(1)}, bf16[48,48,128]{2,1,0:T(8,128)(2,1)}, u32[]{:S(2)}) copy-start(bf16[48,48,128]{2,1,0:T(8,128)(2,1)} %pair.7) | copy-start | bytes 1769476
  6.5 5.8 %copy-start.1 = (bf16[48,48,128]{2,1,0:T(8,128)(2,1)S(1)}, bf16[48,48,128]{2,1,0:T(8,128)(2,1)}, u32[]{:S(2)}) copy-start(bf16[48,48,128]{2,1,0:T(8,128)(2,1)} %cot.7) | copy-start | bytes 1769476
  6.5 2.8 %collective-permute-start = (bf16[7,48,128]{2,1,0:T(8,128)(2,1)S(1)}, bf16[7,48,128]{2,1,0:T(8,128)(2,1)S(1)}, u32[]{:S(2)}, u32[]{:S(2)}) collective-permute-start(bf16[7,48,128]{2,1,0:T(8,128)(2,1)S(1)} %get-tuple-element.43.refs_0_), channel_id=1, source_target_pairs={{0,8},{8,0},{1,9},{9,1},{2,10},{10,2},{3,11},{11,3},{4,12},{12,4},... | collective-permute-start | bytes 258056 | tf_op jit(solution)/shard_map/ppermute | solution.py:491
  7.5 1.8 %collective-permute-start.4 = (bf16[7,48,128]{2,1,0:T(8,128)(2,1)S(1)}, bf16[7,48,128]{2,1,0:T(8,128)(2,1)S(1)}, u32[]{:S(2)}, u32[]{:S(2)}) collective-permute-start(bf16[7,48,128]{2,1,0:T(8,128)(2,1)S(1)} %collective-permute-done.1.refs_2_.from_chip), channel_id=1, source_target_pairs={{0,8},{8,0},{1,9},{9,1},{2,10},{10,2},{3,11},{11,3},{4,12},{12,4},... | collective-permute-start | bytes 258056 | tf_op jit(solution)/shard_map/ppermute | solution.py:511
  9.6 5.2 %collective-permute-start.5 = (bf16[2,3,16,128]{3,2,1,0:T(8,128)(2,1)S(1)}, bf16[2,3,16,128]{3,2,1,0:T(8,128)(2,1)S(1)}, u32[]{:S(2)}, u32[]{:S(2)}) collective-permute-start(bf16[2,3,16,128]{3,2,1,0:T(8,128)(2,1)S(1)} %get-tuple-element.55), channel_id=1, source_target_pairs={{0,8},{8,0},{1,9},{9,1},{2,10},{10,2},{3,11},{11,3},{4,12},{12,4},... | collective-permute-start | bytes 73736 | tf_op jit(solution)/shard_map/ppermute | solution.py:542
  10.1 4.7 %collective-permute-start.6 = (bf16[2,3,16,128]{3,2,1,0:T(8,128)(2,1)S(1)}, bf16[2,3,16,128]{3,2,1,0:T(8,128)(2,1)S(1)}, u32[]{:S(2)}, u32[]{:S(2)}) collective-permute-start(bf16[2,3,16,128]{3,2,1,0:T(8,128)(2,1)S(1)} %get-tuple-element.56), channel_id=1, source_target_pairs={{8,16},{16,8},{0,24},{24,0},{9,17},{17,9},{1,25},{25,1},{10,18},{1... | collective-permute-start | bytes 73736 | tf_op jit(solution)/shard_map/ppermute | solution.py:541
  18.0 1.6 %collective-permute-start.7 = (bf16[4,240,128]{2,1,0:T(8,128)(2,1)S(1)}, bf16[4,240,128]{2,1,0:T(8,128)(2,1)S(1)}, u32[]{:S(2)}, u32[]{:S(2)}) collective-permute-start(bf16[4,240,128]{2,1,0:T(8,128)(2,1)S(1)} %get-tuple-element.67), channel_id=1, source_target_pairs={{0,8},{8,0},{1,9},{9,1},{2,10},{10,2},{3,11},{11,3},{4,12},{12,4},... | collective-permute-start | bytes 737288 | tf_op jit(solution)/shard_map/ppermute | solution.py:605
  19.7 3.9 %collective-permute-start.8 = (bf16[240,128]{1,0:T(8,128)(2,1)S(1)}, bf16[240,128]{1,0:T(8,128)(2,1)S(1)}, u32[]{:S(2)}, u32[]{:S(2)}) collective-permute-start(bf16[240,128]{1,0:T(8,128)(2,1)S(1)} %get-tuple-element.83), channel_id=1, source_target_pairs={{0,9},{1,8},{2,11},{3,10},{4,13},{5,12},{6,15},{7,14},{8,1},{9,0},... | collective-permute-start | bytes 184328 | tf_op jit(solution)/shard_map/ppermute | solution.py:608
  21.2 5.6 %collective-permute-start.10 = (bf16[240,128]{1,0:T(8,128)(2,1)S(1)}, bf16[240,128]{1,0:T(8,128)(2,1)S(1)}, u32[]{:S(2)}, u32[]{:S(2)}) collective-permute-start(bf16[240,128]{1,0:T(8,128)(2,1)S(1)} %get-tuple-element.84), channel_id=1, source_target_pairs={{0,17},{1,16},{2,19},{3,18},{4,21},{5,20},{6,23},{7,22},{8,25},{9,... | collective-permute-start | bytes 184328 | tf_op jit(solution)/shard_map/ppermute | solution.py:608
  21.9 5.0 %collective-permute-start.9 = (bf16[240,128]{1,0:T(8,128)(2,1)S(1)}, bf16[240,128]{1,0:T(8,128)(2,1)S(1)}, u32[]{:S(2)}, u32[]{:S(2)}) collective-permute-start(bf16[240,128]{1,0:T(8,128)(2,1)S(1)} %get-tuple-element.85), channel_id=1, source_target_pairs={{0,24},{1,25},{2,26},{3,27},{4,28},{5,29},{6,30},{7,31},{8,16},{9,... | collective-permute-start | bytes 184328 | tf_op jit(solution)/shard_map/ppermute | solution.py:608
  26.9 6.8 %collective-permute-start.11 = (bf16[240,128]{1,0:T(8,128)(2,1)S(1)}, bf16[240,128]{1,0:T(8,128)(2,1)S(1)}, u32[]{:S(2)}, u32[]{:S(2)}) collective-permute-start(bf16[240,128]{1,0:T(8,128)(2,1)S(1)} %fusion.3), channel_id=1, source_target_pairs={{0,4},{1,5},{2,6},{3,7},{4,0},{5,1},{6,2},{7,3},{8,12},{9,13},{10,... | collective-permute-start | bytes 184328 | tf_op jit(solution)/shard_map/ppermute | solution.py:608
  29.6 6.2 %collective-permute-start.13 = (bf16[240,128]{1,0:T(8,128)(2,1)S(1)}, bf16[240,128]{1,0:T(8,128)(2,1)S(1)}, u32[]{:S(2)}, u32[]{:S(2)}) collective-permute-start(bf16[240,128]{1,0:T(8,128)(2,1)S(1)} %fusion.3), channel_id=1, source_target_pairs={{0,6},{1,7},{2,4},{3,5},{4,2},{5,3},{6,0},{7,1},{8,14},{9,15},{10,... | collective-permute-start | bytes 184328 | tf_op jit(solution)/shard_map/ppermute | solution.py:608
  30.9 4.9 %collective-permute-start.12 = (bf16[240,128]{1,0:T(8,128)(2,1)S(1)}, bf16[240,128]{1,0:T(8,128)(2,1)S(1)}, u32[]{:S(2)}, u32[]{:S(2)}) collective-permute-start(bf16[240,128]{1,0:T(8,128)(2,1)S(1)} %fusion.3), channel_id=1, source_target_pairs={{0,2},{1,3},{2,0},{3,1},{4,6},{5,7},{6,4},{7,5},{8,10},{9,11},{10,... | collective-permute-start | bytes 184328 | tf_op jit(solution)/shard_map/ppermute | solution.py:608
  35.9 5.7 %collective-permute-start.16 = (bf16[240,128]{1,0:T(8,128)(2,1)S(1)}, bf16[240,128]{1,0:T(8,128)(2,1)S(1)}, u32[]{:S(2)}, u32[]{:S(2)}) collective-permute-start(bf16[240,128]{1,0:T(8,128)(2,1)S(1)} %add_convert_fusion.refs_0_), channel_id=1, source_target_pairs={{0,17},{1,16},{2,19},{3,18},{4,21},{5,20},{6,23},{7,22},{8,25},{9,... | collective-permute-start | bytes 184328 | tf_op jit(solution)/shard_map/ppermute | solution.py:608
  37.7 4.2 %collective-permute-start.15 = (bf16[240,128]{1,0:T(8,128)(2,1)S(1)}, bf16[240,128]{1,0:T(8,128)(2,1)S(1)}, u32[]{:S(2)}, u32[]{:S(2)}) collective-permute-start(bf16[240,128]{1,0:T(8,128)(2,1)S(1)} %add_convert_fusion.refs_0_), channel_id=1, source_target_pairs={{0,24},{1,25},{2,26},{3,27},{4,28},{5,29},{6,30},{7,31},{8,16},{9,... | collective-permute-start | bytes 184328 | tf_op jit(solution)/shard_map/ppermute | solution.py:608
  37.7 4.4 %collective-permute-start.14 = (bf16[240,128]{1,0:T(8,128)(2,1)S(1)}, bf16[240,128]{1,0:T(8,128)(2,1)S(1)}, u32[]{:S(2)}, u32[]{:S(2)}) collective-permute-start(bf16[240,128]{1,0:T(8,128)(2,1)S(1)} %add_convert_fusion.refs_0_), channel_id=1, source_target_pairs={{0,9},{1,8},{2,11},{3,10},{4,13},{5,12},{6,15},{7,14},{8,1},{9,0},... | collective-permute-start | bytes 184328 | tf_op jit(solution)/shard_map/ppermute | solution.py:608
  39.2 3.3 %collective-permute-start.17 = (bf16[240,128]{1,0:T(8,128)(2,1)S(1)}, bf16[240,128]{1,0:T(8,128)(2,1)S(1)}, u32[]{:S(2)}, u32[]{:S(2)}) collective-permute-start(bf16[240,128]{1,0:T(8,128)(2,1)S(1)} %add_convert_fusion.refs_0_), channel_id=1, source_target_pairs={{0,8},{8,0},{1,9},{9,1},{2,10},{10,2},{3,11},{11,3},{4,12},{12,4},... | collective-permute-start | bytes 184328 | tf_op jit(solution)/shard_map/ppermute | solution.py:630
  41.6 1.2 %collective-permute-start.20 = (bf16[240,128]{1,0:T(8,128)(2,1)S(1)}, bf16[240,128]{1,0:T(8,128)(2,1)S(1)}, u32[]{:S(2)}, u32[]{:S(2)}) collective-permute-start(bf16[240,128]{1,0:T(8,128)(2,1)S(1)} %collective-permute-done.16.refs_3_), channel_id=1, source_target_pairs={{0,8},{8,0},{1,9},{9,1},{2,10},{10,2},{3,11},{11,3},{4,12},{12,4},... | collective-permute-start | bytes 184328 | tf_op jit(solution)/shard_map/ppermute | solution.py:630
  41.9 1.2 %collective-permute-start.19 = (bf16[240,128]{1,0:T(8,128)(2,1)S(1)}, bf16[240,128]{1,0:T(8,128)(2,1)S(1)}, u32[]{:S(2)}, u32[]{:S(2)}) collective-permute-start(bf16[240,128]{1,0:T(8,128)(2,1)S(1)} %collective-permute-done.15.refs_2_), channel_id=1, source_target_pairs={{0,8},{8,0},{1,9},{9,1},{2,10},{10,2},{3,11},{11,3},{4,12},{12,4},... | collective-permute-start | bytes 184328 | tf_op jit(solution)/shard_map/ppermute | solution.py:630
  42.1 1.2 %collective-permute-start.18 = (bf16[240,128]{1,0:T(8,128)(2,1)S(1)}, bf16[240,128]{1,0:T(8,128)(2,1)S(1)}, u32[]{:S(2)}, u32[]{:S(2)}) collective-permute-start(bf16[240,128]{1,0:T(8,128)(2,1)S(1)} %collective-permute-done.14.refs_1_), channel_id=1, source_target_pairs={{0,8},{8,0},{1,9},{9,1},{2,10},{10,2},{3,11},{11,3},{4,12},{12,4},... | collective-permute-start | bytes 184328 | tf_op jit(solution)/shard_map/ppermute | solution.py:630

commit v6 on v5

--- a/solution.py
+++ b/solution.py
@@ -19,7 +19,8 @@
 
 
 def pack_kernel(
-    pair, cot, features, to_core, to_chip, to_even, to_odd, pair_low, pair_high, cot_low, cot_high, own, work, sides, sems
+    pair, cot, features, context_in, proj_weight_in, conv_weight_in, valid_in,
+    to_core, to_chip, to_even, to_odd, context, proj_weight, conv_weight, valid, pair_low, pair_high, cot_low, cot_high, own, work, sides, sems
 ):
     tile_rows, band_cols, channels = pair.shape
     odd_row = lax.rem(lax.axis_index(ROW), 2)
@@ -34,6 +35,7 @@
     for target, at_end in ((to_chip, odd_row), (to_core, 1 - odd_row)):
         parts.append((pair.at[pl.ds(at_end * (tile_rows - HALO), HALO)], target.at[:HALO]))
         parts.append((cot.at[pl.ds(at_end * (tile_rows - 1), 1)], target.at[HALO:EDGES]))
+    parts += [(context_in, context), (proj_weight_in, proj_weight), (conv_weight_in, conv_weight), (valid_in, valid)]
     copies = [pltpu.make_async_copy(source, target, sems.at[i]) for i, (source, target) in enumerate(parts)]
     for copy in copies:
         copy.start()
@@ -70,7 +72,7 @@
 
 def weights_kernel(
     valid, context, proj_weight, conv_weight,
-    window, rows_valid, forward, backward, projection, context_key,
+    window, rows_valid, forward, backward, context_key,
 ):
     channels = window.shape[1]
     bins = valid.shape[0]
@@ -98,7 +100,6 @@
             forward[at : at + channels, lanes] = values
             at = ((1 - row_step + out) * 3 + step) * channels
             backward[at : at + channels, lanes] = turned
-    projection[...] = proj_weight[...]
     context_key[...] = jnp.dot(context[...], proj_weight[:, channels:], preferred_element_type=F32).astype(BF16)
 
 
@@ -328,8 +329,10 @@
     skew[...] = jnp.zeros(skew.shape, F32)
     pairs = 4
     query_at = 9 * channels + all_bins + tail
-    query_rows = []
-    for first in range(0, tile_rows, 2 * pairs):
+    query_rows = {}
+    order = list(range(0, tile_rows, 2 * pairs))
+    order = order[1:-1] + [order[0], order[-1]]
+    for first in order:
         back = jnp.dot(four_rows(carry_sources, first, pairs), backward[...], preferred_element_type=F32)
         for offset in range(2 * pairs):
             index = first + offset
@@ -337,9 +340,9 @@
             at = offset // 2 * PITCH + PAD
             masked = mask_of(index) * back[at : at + band_cols, lanes]
             change[index] = masked
-            query_rows.append(jnp.sum(masked, axis=0, keepdims=True))
+            query_rows[index] = jnp.sum(masked, axis=0, keepdims=True)
             skew[index % 8, index - index % 8 : index - index % 8 + band_cols, :] += masked
-    totals[pl.ds(pl.multiple_of(query_at + row_start, 16), tile_rows), :] = jnp.concatenate(query_rows, axis=0)
+    totals[pl.ds(pl.multiple_of(query_at + row_start, 16), tile_rows), :] = jnp.concatenate([query_rows[index] for index in range(tile_rows)], axis=0)
     reach = tile_rows + band_cols - 8
     for step in range(8):
         totals[pl.ds(9 * channels + col_start + step, reach), :] += skew[step, :reach, :]
@@ -404,12 +407,16 @@
         whole[pl.ds(pl.multiple_of((half * parts + place) * size, 16), size), :] = mine[part][...]
         whole[pl.ds(pl.multiple_of(((1 - half) * parts + place) * size, 16), size), :] = theirs[part][...]
     copies = [
-        pltpu.make_async_copy(source, target, sems.at[index])
-        for index, (source, target) in enumerate(((conv_out, conv_grad), (proj_out, proj_grad), (feature_out, feature_grad)))
+        pltpu.make_async_copy(conv_out.at[tap : tap + 3], conv_grad.at[tap : tap + 3], sems.at[tap // 3])
+        for tap in range(0, 9, 3)
+    ] + [
+        pltpu.make_async_copy(proj_out, proj_grad, sems.at[3]),
+        pltpu.make_async_copy(feature_out, feature_grad, sems.at[4]),
     ]
     for tap in range(9):
         conv_out[tap] = whole[tap * channels : (tap + 1) * channels, :].astype(F32).T
-    copies[0].start()
+        if tap % 3 == 2:
+            copies[tap // 3].start()
     key_at = 9 * channels
     query_at = key_at + all_bins + tail
     own = features_turned[...]
@@ -417,7 +424,7 @@
     proj_out[:, channels:] = jnp.dot(
         own, whole[key_at : key_at + all_bins, :], preferred_element_type=F32
     ) + jnp.dot(context_turned[...], whole[key_at + all_bins : query_at, :], preferred_element_type=F32)
-    copies[1].start()
+    copies[3].start()
     start = pl.multiple_of(row * tile_rows, 16)
     both = jnp.concatenate(
         [whole[pl.ds(query_at + start, tile_rows), :], whole[pl.ds(key_at + start, tile_rows), :]], axis=1
@@ -425,7 +432,7 @@
     feature_out[...] = lax.dot_general(
         both, projection[...], (((1,), (1,)), ((), ())), preferred_element_type=F32
     ).astype(BF16)
-    copies[2].start()
+    copies[4].start()
     for copy in copies:
         copy.wait()
 
@@ -453,26 +460,30 @@
 
     layers = EDGES + width // channels
     chunk = pltpu.VMEM((tile_rows, SIDE, channels), BF16)
-    to_core, to_chip, to_even, to_odd = pl.pallas_call(
+    to_core, to_chip, to_even, to_odd, context_near, projection, conv_near, valid = pl.pallas_call(
         pack_kernel,
         out_shape=(
             shape(layers, tile_rows, channels),
             shape(layers, tile_rows, channels),
             shape(EDGES, tile_rows, channels),
             shape(EDGES, tile_rows, channels),
+            shape(*context_features.shape),
+            shape(*proj_weight.shape),
+            shape(*conv_weight.shape),
+            shape(*valid_bins.shape, dtype=jnp.int32),
         ),
-        in_specs=[anywhere] * 3,
-        out_specs=(vmem,) * 4,
+        in_specs=[anywhere] * 7,
+        out_specs=(vmem,) * 8,
         scratch_shapes=[
             chunk, chunk, chunk, chunk,
             pltpu.VMEM(bin_features.shape, BF16),
             pltpu.VMEM((tile_rows * SIDE, channels), F32),
             pltpu.VMEM((2, EDGES, tile_rows, channels), BF16),
-            pltpu.SemaphoreType.DMA((9,)),
+            pltpu.SemaphoreType.DMA((13,)),
         ],
         compiler_params=PARAMS,
         name="pack",
-    )(*in_hbm(pair_input, cotangent, bin_features))
+    )(*in_hbm(pair_input, cotangent, bin_features, context_features, proj_weight, conv_weight, valid_bins))
     other_core = [(0, 1), (1, 0)]
     even_cols = [(i, i ^ 1) for i in range(col_count) if i ^ 1 < col_count]
     odd_cols = []
@@ -490,23 +501,21 @@
     from_even = lax.ppermute(to_even, "col", even_cols)
     from_core = lax.ppermute(to_core, "core", other_core)
     near_bins = tile_rows + band_cols + 2 * MARGIN
-    valid_bins, from_chip = lax.optimization_barrier((valid_bins, from_chip))
-    window, rows_valid, forward, backward, projection, context_key = pl.pallas_call(
+    window, rows_valid, forward, backward, context_key = pl.pallas_call(
         weights_kernel,
         out_shape=(
             shape(near_bins, channels, dtype=F32),
             shape(taken, channels, dtype=F32),
             shape(12 * channels, 2 * channels),
             shape(12 * channels, 2 * channels),
-            shape(*proj_weight.shape),
             shape(tail, channels),
         ),
         in_specs=[vmem] * 4,
-        out_specs=(vmem,) * 6,
+        out_specs=(vmem,) * 5,
         compiler_params=PARAMS,
         cost_estimate=pl.CostEstimate(flops=1 << 30, bytes_accessed=1 << 21, transcendentals=0),
         name="weights",
-    )(*in_hbm(valid_bins, context_features, proj_weight, conv_weight))
+    )(valid, context_near, projection, conv_near)
     if row_count == 4:
         sources = [to_core, from_core, from_chip, lax.ppermute(from_chip, "core", other_core)]
     else:
@@ -599,7 +608,7 @@
         name="late",
     )(
         pair_input, cotangent, active, active_ends, change, window, rows_valid, features,
-        *in_hbm(context_features),
+        context_near,
     )
 
     halves = keep + lax.ppermute(send, "core", other_core).astype(F32)
@@ -608,7 +617,8 @@
             return lax.ppermute(values, ROW + ("col",), [(index, index ^ bits) for index in range(32)])
 
         plane = (1 + 8, 16 + 8, 16 + 1)
-        got = [across(halves[part].astype(BF16), bits).astype(F32) for part, bits in enumerate(plane, 1)]
+        got = lax.optimization_barrier([across(halves[part].astype(BF16), bits) for part, bits in enumerate(plane, 1)])
+        got = [values.astype(F32) for values in got]
         mine = (halves[0] + got[0] + got[1] + got[2]).astype(BF16)
         near, far, opposite = [across(mine, bits) for bits in (2, 4, 6)]
         far, pair_output = lax.optimization_barrier((far, pair_output))
@@ -643,7 +653,7 @@
             pltpu.VMEM(bin_features.shape, BF16),
             pltpu.VMEM(proj_weight.shape, F32),
             pltpu.VMEM(conv_weight.shape, F32),
-            pltpu.SemaphoreType.DMA((3,)),
+            pltpu.SemaphoreType.DMA((5,)),
         ],
         compiler_params=PARAMS,
         name="finish",

time: 45 us -> 43.7 us (0.971)
  Pallas kernels: 13 us -> 10.7 us
  waiting for transfers between devices: 12.2 us -> 13.3 us
    pallas_call x1, Pallas kernels: 1.69 us -> 0.45 us  [body(): pl.pallas_call(weights_kernel, out_shape=(shape(near_bins, channels, dtyp...]
    pallas_call x1, Pallas kernels: 2.43 us -> 1.44 us  [body(): pl.pallas_call(late_kernel, out_shape=(shape(*pair_input.shape), shape(*p...]
    ppermute x1, waiting for transfers between devices: 0.01 us -> 0.73 us  [body(): lax.ppermute(from_chip, 'core', other_core)]
  transfers between devices with their start and end apart: 21 -> 21, of which waited for: 12 -> 14; matrix products, arithmetic and copies ran while one was open for 0% -> 0% of each run, Pallas kernels for 15% -> 11%
where the time goes in v6:
time: 43.7 us; the launch traced here: 43.6 us
  starting transfers between devices  18.7 us (43%)
  waiting for transfers between devices  13.3 us (30%)
  Pallas kernels  10.7 us (24%)
  between operations  0.75 us (2%)
    ppermute x9, starting transfers between devices, across(): lax.ppermute(values, ROW + ('col',), [(index, index ^ bits) for index in...  10.7 us
    ppermute x9, waiting for transfers between devices, across(): lax.ppermute(values, ROW + ('col',), [(index, index ^ bits) for index in...  9.46 us
    pallas_call x1, Pallas kernels, body(): pl.pallas_call(outer_kernel, out_shape=(shape(2, band_cols, channels, dty...  2.89 us
    pallas_call x1, Pallas kernels, body(): pl.pallas_call(inner_kernel, out_shape=(shape(span, 3 * channels), shape(...  2.49 us
    ppermute x1, starting transfers between devices, body(): from_chip = lax.ppermute(to_chip, ROW, odd_rows + ends)  2.44 us
    ppermute x1, starting transfers between devices, body(): corner_chip = lax.ppermute(corner_to_chip, ROW, odd_rows + ends)  2.42 us
    pallas_call x1, Pallas kernels, body(): pl.pallas_call(pack_kernel, out_shape=(shape(layers, tile_rows, channels)...  1.72 us
    ppermute x1, starting transfers between devices, body(): from_even = lax.ppermute(to_even, 'col', even_cols)  1.52 us
  transfers between devices with their start and end apart: 21, of which 14 were waited for; matrix products, arithmetic and copies ran while one was open for 0% of the time, Pallas kernels for 11%

profile of v6, /device:TPU:0, one launch (start us, length us, event | category | flops | bytes accessed | tf_op | source)
XLA Modules:
  0.0 43.6 jit_solution(9006372158882374089)
XLA Ops:
  0.6 1.7 %pack.1 = (bf16[7,48,128]{2,1,0:T(8,128)(2,1)S(1)}, bf16[7,48,128]{2,1,0:T(8,128)(2,1)S(1)}, bf16[3,48,128]{2,1,0:T(8,128)(2,1)S(1)}, bf16[3,48,128]{2,1,0:T(8,1...) custom-call(bf16[48,48,128]{2,1,0:T(8,128)(2,1)} %pair.7, ...), custom_call_target="tpu_custom_call" | custom-call | tf_op jit(solution)/shard_map/pack/pallas_call | solution.py:463
  2.4 2.4 %collective-permute-start.1 = (bf16[7,48,128]{2,1,0:T(8,128)(2,1)S(1)}, bf16[7,48,128]{2,1,0:T(8,128)(2,1)S(1)}, u32[]{:S(2)}, u32[]{:S(2)}) collective-permute-start(bf16[7,48,128]{2,1,0:T(8,128)(2,1)S(1)} %get-tuple-element.48), channel_id=1, source_target_pairs={{8,16},{16,8},{0,24},{24,0},{9,17},{17,9},{1,25},{25,1},{10,18},{1... | collective-permute-start | bytes 258056 | tf_op jit(solution)/shard_map/ppermute | solution.py:499
  4.8 1.5 %collective-permute-start.2 = (bf16[3,48,128]{2,1,0:T(8,128)(2,1)S(1)}, bf16[3,48,128]{2,1,0:T(8,128)(2,1)S(1)}, u32[]{:S(2)}, u32[]{:S(2)}) collective-permute-start(bf16[3,48,128]{2,1,0:T(8,128)(2,1)S(1)} %get-tuple-element.49), channel_id=1, source_target_pairs={{0,1},{1,0},{2,3},{3,2},{4,5},{5,4},{6,7},{7,6},{8,9},{9,8},{10,11... | collective-permute-start | bytes 110600 | tf_op jit(solution)/shard_map/ppermute | solution.py:501
  6.8 0.9 %collective-permute-done.1.refs_2_.from_chip = bf16[7,48,128]{2,1,0:T(8,128)(2,1)S(1)} collective-permute-done((bf16[7,48,128]{2,1,0:T(8,128)(2,1)S(1)}, bf16[7,48,128]{2,1,0:T(8,128)(2,1)S(1)}, u32[]{:S(2)}, u32[]{:S(2)}) %collective-permute-start.1) | collective-permute-done | bytes 86048 | tf_op jit(solution)/shard_map/ppermute | solution.py:499
  8.3 0.7 %collective-permute-done.4.refs_3_ = bf16[7,48,128]{2,1,0:T(8,128)(2,1)S(1)} collective-permute-done((bf16[7,48,128]{2,1,0:T(8,128)(2,1)S(1)}, bf16[7,48,128]{2,1,0:T(8,128)(2,1)S(1)}, u32[]{:S(2)}, u32[]{:S(2)}) %collective-permute-start.4) | collective-permute-done | bytes 86048 | tf_op jit(solution)/shard_map/ppermute | solution.py:520
  9.5 2.4 %collective-permute-start.6 = (bf16[2,3,16,128]{3,2,1,0:T(8,128)(2,1)S(1)}, bf16[2,3,16,128]{3,2,1,0:T(8,128)(2,1)S(1)}, u32[]{:S(2)}, u32[]{:S(2)}) collective-permute-start(bf16[2,3,16,128]{3,2,1,0:T(8,128)(2,1)S(1)} %get-tuple-element.61), channel_id=1, source_target_pairs={{8,16},{16,8},{0,24},{24,0},{9,17},{17,9},{1,25},{25,1},{10,18},{1... | collective-permute-start | bytes 73736 | tf_op jit(solution)/shard_map/ppermute | solution.py:550
  12.0 2.5 %inner.1 = (bf16[3072,384]{1,0:T(8,128)(2,1)S(1)}, bf16[3072,384]{1,0:T(8,128)(2,1)S(1)}, bf16[3072,128]{1,0:T(8,128)(2,1)S(1)}, f32[48,48,128]{2,1,0:T(8,128)S(1)}) custom-call(bf16[48,48,128]{2,1,0:T(8,128)(2,1)S(1)} %copy-done, bf16[48,48,128]{2,1,0:T(8,128)(2,1)S(1)} %copy-done.1, bf16[2,3,48,128]{3,2,1,0:T(8,128)(2,1)S(1)} %get-tuple-element.59.sides, ...), custom_call_target="tpu_custom_call" | custom-call | tf_op jit(solution)/shard_map/inner/pallas_call | solution.py:561
  14.5 2.9 %outer.1 = (f32[2,48,128]{2,1,0:T(8,128)S(1)}, f32[48,48,128]{2,1,0:T(8,128)S(1)}, f32[4,240,128]{2,1,0:T(8,128)S(1)}, bf16[4,240,128]{2,1,0:T(8,128)(2,1)S(1)}) custom-call(bf16[48,48,128]{2,1,0:T(8,128)(2,1)S(1)} %copy-done, bf16[48,48,128]{2,1,0:T(8,128)(2,1)S(1)} %copy-done.1, bf16[7,48,128]{2,1,0:T(8,128)(2,1)S(1)} %collective-permute-done.refs_1_.from_core, ...), custom_call_target="tpu_custom_call" | custom-call | tf_op jit(solution)/shard_map/outer/pallas_call | solution.py:573
  17.6 1.3 %collective-permute-done.7 = bf16[4,240,128]{2,1,0:T(8,128)(2,1)S(1)} collective-permute-done((bf16[4,240,128]{2,1,0:T(8,128)(2,1)S(1)}, bf16[4,240,128]{2,1,0:T(8,128)(2,1)S(1)}, u32[]{:S(2)}, u32[]{:S(2)}) %collective-permute-start.7) | collective-permute-done | bytes 245792 | tf_op jit(solution)/shard_map/ppermute | solution.py:614
  19.1 1.8 %collective-permute-start.10 = (bf16[240,128]{1,0:T(8,128)(2,1)S(1)}, bf16[240,128]{1,0:T(8,128)(2,1)S(1)}, u32[]{:S(2)}, u32[]{:S(2)}) collective-permute-start(bf16[240,128]{1,0:T(8,128)(2,1)S(1)} %get-tuple-element.91), channel_id=1, source_target_pairs={{0,17},{1,16},{2,19},{3,18},{4,21},{5,20},{6,23},{7,22},{8,25},{9,... | collective-permute-start | bytes 184328 | tf_op jit(solution)/shard_map/ppermute | solution.py:617
  20.8 0.7 %collective-permute-start.9 = (bf16[240,128]{1,0:T(8,128)(2,1)S(1)}, bf16[240,128]{1,0:T(8,128)(2,1)S(1)}, u32[]{:S(2)}, u32[]{:S(2)}) collective-permute-start(bf16[240,128]{1,0:T(8,128)(2,1)S(1)} %get-tuple-element.92), channel_id=1, source_target_pairs={{0,24},{1,25},{2,26},{3,27},{4,28},{5,29},{6,30},{7,31},{8,16},{9,... | collective-permute-start | bytes 184328 | tf_op jit(solution)/shard_map/ppermute | solution.py:617
  21.6 0.7 %collective-permute-start.8 = (bf16[240,128]{1,0:T(8,128)(2,1)S(1)}, bf16[240,128]{1,0:T(8,128)(2,1)S(1)}, u32[]{:S(2)}, u32[]{:S(2)}) collective-permute-start(bf16[240,128]{1,0:T(8,128)(2,1)S(1)} %get-tuple-element.93), channel_id=1, source_target_pairs={{0,9},{1,8},{2,11},{3,10},{4,13},{5,12},{6,15},{7,14},{8,1},{9,0},... | collective-permute-start | bytes 184328 | tf_op jit(solution)/shard_map/ppermute | solution.py:617
  22.3 2.4 %collective-permute-done.10 = bf16[240,128]{1,0:T(8,128)(2,1)S(1)} collective-permute-done((bf16[240,128]{1,0:T(8,128)(2,1)S(1)}, bf16[240,128]{1,0:T(8,128)(2,1)S(1)}, u32[]{:S(2)}, u32[]{:S(2)}) %collective-permute-start.10) | collective-permute-done | bytes 61472 | tf_op jit(solution)/shard_map/ppermute | solution.py:617
  25.3 2.6 %collective-permute-start.11 = (bf16[240,128]{1,0:T(8,128)(2,1)S(1)}, bf16[240,128]{1,0:T(8,128)(2,1)S(1)}, u32[]{:S(2)}, u32[]{:S(2)}) collective-permute-start(bf16[240,128]{1,0:T(8,128)(2,1)S(1)} %fusion.3), channel_id=1, source_target_pairs={{0,4},{1,5},{2,6},{3,7},{4,0},{5,1},{6,2},{7,3},{8,12},{9,13},{10,... | collective-permute-start | bytes 184328 | tf_op jit(solution)/shard_map/ppermute | solution.py:617
  27.9 1.4 %collective-permute-start.13 = (bf16[240,128]{1,0:T(8,128)(2,1)S(1)}, bf16[240,128]{1,0:T(8,128)(2,1)S(1)}, u32[]{:S(2)}, u32[]{:S(2)}) collective-permute-start(bf16[240,128]{1,0:T(8,128)(2,1)S(1)} %fusion.3), channel_id=1, source_target_pairs={{0,6},{1,7},{2,4},{3,5},{4,2},{5,3},{6,0},{7,1},{8,14},{9,15},{10,... | collective-permute-start | bytes 184328 | tf_op jit(solution)/shard_map/ppermute | solution.py:617
  29.5 1.4 %late.1 = (bf16[48,48,128]{2,1,0:T(8,128)(2,1)}, bf16[48,48,128]{2,1,0:T(8,128)(2,1)}, bf16[512,192]{1,0:T(8,128)(2,1)S(1)}, bf16[512,384]{1,0:T(8,128)(2,1)S(1)}) custom-call(bf16[48,48,128]{2,1,0:T(8,128)(2,1)S(1)} %copy-done, bf16[48,48,128]{2,1,0:T(8,128)(2,1)S(1)} %copy-done.1, f32[48,48,128]{2,1,0:T(8,128)S(1)} %get-tuple-element.76.active, ...), custom_call_target="tpu_custom_call" | custom-call | tf_op jit(solution)/shard_map/late/pallas_call | solution.py:600
  30.9 1.3 %collective-permute-done.11 = bf16[240,128]{1,0:T(8,128)(2,1)S(1)} collective-permute-done((bf16[240,128]{1,0:T(8,128)(2,1)S(1)}, bf16[240,128]{1,0:T(8,128)(2,1)S(1)}, u32[]{:S(2)}, u32[]{:S(2)}) %collective-permute-start.11) | collective-permute-done | bytes 61472 | tf_op jit(solution)/shard_map/ppermute | solution.py:617
  32.2 2.3 %collective-permute-done.13 = bf16[240,128]{1,0:T(8,128)(2,1)S(1)} collective-permute-done((bf16[240,128]{1,0:T(8,128)(2,1)S(1)}, bf16[240,128]{1,0:T(8,128)(2,1)S(1)}, u32[]{:S(2)}, u32[]{:S(2)}) %collective-permute-start.13) | collective-permute-done | bytes 61472 | tf_op jit(solution)/shard_map/ppermute | solution.py:617
  34.8 1.7 %collective-permute-start.16 = (bf16[240,128]{1,0:T(8,128)(2,1)S(1)}, bf16[240,128]{1,0:T(8,128)(2,1)S(1)}, u32[]{:S(2)}, u32[]{:S(2)}) collective-permute-start(bf16[240,128]{1,0:T(8,128)(2,1)S(1)} %add_convert_fusion.refs_0_), channel_id=1, source_target_pairs={{0,17},{1,16},{2,19},{3,18},{4,21},{5,20},{6,23},{7,22},{8,25},{9,... | collective-permute-start | bytes 184328 | tf_op jit(solution)/shard_map/ppermute | solution.py:617
  36.5 1.5 %collective-permute-start.14 = (bf16[240,128]{1,0:T(8,128)(2,1)S(1)}, bf16[240,128]{1,0:T(8,128)(2,1)S(1)}, u32[]{:S(2)}, u32[]{:S(2)}) collective-permute-start(bf16[240,128]{1,0:T(8,128)(2,1)S(1)} %add_convert_fusion.refs_0_), channel_id=1, source_target_pairs={{0,9},{1,8},{2,11},{3,10},{4,13},{5,12},{6,15},{7,14},{8,1},{9,0},... | collective-permute-start | bytes 184328 | tf_op jit(solution)/shard_map/ppermute | solution.py:617
  38.1 2.1 %collective-permute-done.16.refs_3_ = bf16[240,128]{1,0:T(8,128)(2,1)S(1)} collective-permute-done((bf16[240,128]{1,0:T(8,128)(2,1)S(1)}, bf16[240,128]{1,0:T(8,128)(2,1)S(1)}, u32[]{:S(2)}, u32[]{:S(2)}) %collective-permute-start.16) | collective-permute-done | bytes 61472 | tf_op jit(solution)/shard_map/ppermute | solution.py:617
  40.2 0.6 %collective-permute-done.15.refs_2_ = bf16[240,128]{1,0:T(8,128)(2,1)S(1)} collective-permute-done((bf16[240,128]{1,0:T(8,128)(2,1)S(1)}, bf16[240,128]{1,0:T(8,128)(2,1)S(1)}, u32[]{:S(2)}, u32[]{:S(2)}) %collective-permute-start.15) | collective-permute-done | bytes 61472 | tf_op jit(solution)/shard_map/ppermute | solution.py:617
  41.4 0.6 %collective-permute-done.19.refs_6_ = bf16[240,128]{1,0:T(8,128)(2,1)S(1)} collective-permute-done((bf16[240,128]{1,0:T(8,128)(2,1)S(1)}, bf16[240,128]{1,0:T(8,128)(2,1)S(1)}, u32[]{:S(2)}, u32[]{:S(2)}) %collective-permute-start.19) | collective-permute-done | bytes 61472 | tf_op jit(solution)/shard_map/ppermute | solution.py:640
  42.2 1.4 %finish.1 = (bf16[48,512]{1,0:T(8,128)(2,1)}, f32[512,256]{1,0:T(8,128)}, f32[9,128,128]{2,1,0:T(8,128)}) custom-call(bf16[512,192]{1,0:T(8,128)(2,1)S(1)} %get-tuple-element.83.features_turned, bf16[512,384]{1,0:T(8,128)(2,1)S(1)} %get-tuple-element.84.context_turned, bf16[512,256]{1,0:T(8,128)(2,1)S(1)} %get-tuple-element.51.proj_weight.projection, ...), custom_call_target="tpu_custom_call" | custom-call | tf_op jit(solution)/shard_map/finish/pallas_call | solution.py:642
  (34 shorter events, 3.8 us)
Async XLA Ops:
  2.4 5.4 %collective-permute-start.1 = (bf16[7,48,128]{2,1,0:T(8,128)(2,1)S(1)}, bf16[7,48,128]{2,1,0:T(8,128)(2,1)S(1)}, u32[]{:S(2)}, u32[]{:S(2)}) collective-permute-start(bf16[7,48,128]{2,1,0:T(8,128)(2,1)S(1)} %get-tuple-element.48), channel_id=1, source_target_pairs={{8,16},{16,8},{0,24},{24,0},{9,17},{17,9},{1,25},{25,1},{10,18},{1... | collective-permute-start | bytes 258056 | tf_op jit(solution)/shard_map/ppermute | solution.py:499
  4.8 4.5 %collective-permute-start.2 = (bf16[3,48,128]{2,1,0:T(8,128)(2,1)S(1)}, bf16[3,48,128]{2,1,0:T(8,128)(2,1)S(1)}, u32[]{:S(2)}, u32[]{:S(2)}) collective-permute-start(bf16[3,48,128]{2,1,0:T(8,128)(2,1)S(1)} %get-tuple-element.49), channel_id=1, source_target_pairs={{0,1},{1,0},{2,3},{3,2},{4,5},{5,4},{6,7},{7,6},{8,9},{9,8},{10,11... | collective-permute-start | bytes 110600 | tf_op jit(solution)/shard_map/ppermute | solution.py:501
  6.3 2.9 %collective-permute-start.3 = (bf16[3,48,128]{2,1,0:T(8,128)(2,1)S(1)}, bf16[3,48,128]{2,1,0:T(8,128)(2,1)S(1)}, u32[]{:S(2)}, u32[]{:S(2)}) collective-permute-start(bf16[3,48,128]{2,1,0:T(8,128)(2,1)S(1)} %get-tuple-element.50), channel_id=1, source_target_pairs={{0,8},{1,2},{2,1},{3,4},{4,3},{5,6},{6,5},{7,15},{8,0},{9,10},{10,... | collective-permute-start | bytes 110600 | tf_op jit(solution)/shard_map/ppermute | solution.py:500
  6.7 1.6 %collective-permute-start = (bf16[7,48,128]{2,1,0:T(8,128)(2,1)S(1)}, bf16[7,48,128]{2,1,0:T(8,128)(2,1)S(1)}, u32[]{:S(2)}, u32[]{:S(2)}) collective-permute-start(bf16[7,48,128]{2,1,0:T(8,128)(2,1)S(1)} %get-tuple-element.47.refs_0_), channel_id=1, source_target_pairs={{0,8},{8,0},{1,9},{9,1},{2,10},{10,2},{3,11},{11,3},{4,12},{12,4},... | collective-permute-start | bytes 258056 | tf_op jit(solution)/shard_map/ppermute | solution.py:502
  7.7 1.3 %collective-permute-start.4 = (bf16[7,48,128]{2,1,0:T(8,128)(2,1)S(1)}, bf16[7,48,128]{2,1,0:T(8,128)(2,1)S(1)}, u32[]{:S(2)}, u32[]{:S(2)}) collective-permute-start(bf16[7,48,128]{2,1,0:T(8,128)(2,1)S(1)} %collective-permute-done.1.refs_2_.from_chip), channel_id=1, source_target_pairs={{0,8},{8,0},{1,9},{9,1},{2,10},{10,2},{3,11},{11,3},{4,12},{12,4},... | collective-permute-start | bytes 258056 | tf_op jit(solution)/shard_map/ppermute | solution.py:520
  7.8 4.1 %copy-start = (bf16[48,48,128]{2,1,0:T(8,128)(2,1)S(1)}, bf16[48,48,128]{2,1,0:T(8,128)(2,1)}, u32[]{:S(2)}) copy-start(bf16[48,48,128]{2,1,0:T(8,128)(2,1)} %pair.7) | copy-start | bytes 1769476
  7.8 4.1 %copy-start.1 = (bf16[48,48,128]{2,1,0:T(8,128)(2,1)S(1)}, bf16[48,48,128]{2,1,0:T(8,128)(2,1)}, u32[]{:S(2)}) copy-start(bf16[48,48,128]{2,1,0:T(8,128)(2,1)} %cot.7) | copy-start | bytes 1769476
  9.3 5.1 %collective-permute-start.5 = (bf16[2,3,16,128]{3,2,1,0:T(8,128)(2,1)S(1)}, bf16[2,3,16,128]{3,2,1,0:T(8,128)(2,1)S(1)}, u32[]{:S(2)}, u32[]{:S(2)}) collective-permute-start(bf16[2,3,16,128]{3,2,1,0:T(8,128)(2,1)S(1)} %get-tuple-element.60), channel_id=1, source_target_pairs={{0,8},{8,0},{1,9},{9,1},{2,10},{10,2},{3,11},{11,3},{4,12},{12,4},... | collective-permute-start | bytes 73736 | tf_op jit(solution)/shard_map/ppermute | solution.py:551
  9.5 4.9 %collective-permute-start.6 = (bf16[2,3,16,128]{3,2,1,0:T(8,128)(2,1)S(1)}, bf16[2,3,16,128]{3,2,1,0:T(8,128)(2,1)S(1)}, u32[]{:S(2)}, u32[]{:S(2)}) collective-permute-start(bf16[2,3,16,128]{3,2,1,0:T(8,128)(2,1)S(1)} %get-tuple-element.61), channel_id=1, source_target_pairs={{8,16},{16,8},{0,24},{24,0},{9,17},{17,9},{1,25},{25,1},{10,18},{1... | collective-permute-start | bytes 73736 | tf_op jit(solution)/shard_map/ppermute | solution.py:550
  17.4 1.6 %collective-permute-start.7 = (bf16[4,240,128]{2,1,0:T(8,128)(2,1)S(1)}, bf16[4,240,128]{2,1,0:T(8,128)(2,1)S(1)}, u32[]{:S(2)}, u32[]{:S(2)}) collective-permute-start(bf16[4,240,128]{2,1,0:T(8,128)(2,1)S(1)} %get-tuple-element.72), channel_id=1, source_target_pairs={{0,8},{8,0},{1,9},{9,1},{2,10},{10,2},{3,11},{11,3},{4,12},{12,4},... | collective-permute-start | bytes 737288 | tf_op jit(solution)/shard_map/ppermute | solution.py:614
  19.1 5.6 %collective-permute-start.10 = (bf16[240,128]{1,0:T(8,128)(2,1)S(1)}, bf16[240,128]{1,0:T(8,128)(2,1)S(1)}, u32[]{:S(2)}, u32[]{:S(2)}) collective-permute-start(bf16[240,128]{1,0:T(8,128)(2,1)S(1)} %get-tuple-element.91), channel_id=1, source_target_pairs={{0,17},{1,16},{2,19},{3,18},{4,21},{5,20},{6,23},{7,22},{8,25},{9,... | collective-permute-start | bytes 184328 | tf_op jit(solution)/shard_map/ppermute | solution.py:617
  20.8 4.3 %collective-permute-start.9 = (bf16[240,128]{1,0:T(8,128)(2,1)S(1)}, bf16[240,128]{1,0:T(8,128)(2,1)S(1)}, u32[]{:S(2)}, u32[]{:S(2)}) collective-permute-start(bf16[240,128]{1,0:T(8,128)(2,1)S(1)} %get-tuple-element.92), channel_id=1, source_target_pairs={{0,24},{1,25},{2,26},{3,27},{4,28},{5,29},{6,30},{7,31},{8,16},{9,... | collective-permute-start | bytes 184328 | tf_op jit(solution)/shard_map/ppermute | solution.py:617
  21.6 3.7 %collective-permute-start.8 = (bf16[240,128]{1,0:T(8,128)(2,1)S(1)}, bf16[240,128]{1,0:T(8,128)(2,1)S(1)}, u32[]{:S(2)}, u32[]{:S(2)}) collective-permute-start(bf16[240,128]{1,0:T(8,128)(2,1)S(1)} %get-tuple-element.93), channel_id=1, source_target_pairs={{0,9},{1,8},{2,11},{3,10},{4,13},{5,12},{6,15},{7,14},{8,1},{9,0},... | collective-permute-start | bytes 184328 | tf_op jit(solution)/shard_map/ppermute | solution.py:617
  25.3 6.9 %collective-permute-start.11 = (bf16[240,128]{1,0:T(8,128)(2,1)S(1)}, bf16[240,128]{1,0:T(8,128)(2,1)S(1)}, u32[]{:S(2)}, u32[]{:S(2)}) collective-permute-start(bf16[240,128]{1,0:T(8,128)(2,1)S(1)} %fusion.3), channel_id=1, source_target_pairs={{0,4},{1,5},{2,6},{3,7},{4,0},{5,1},{6,2},{7,3},{8,12},{9,13},{10,... | collective-permute-start | bytes 184328 | tf_op jit(solution)/shard_map/ppermute | solution.py:617
  27.9 6.6 %collective-permute-start.13 = (bf16[240,128]{1,0:T(8,128)(2,1)S(1)}, bf16[240,128]{1,0:T(8,128)(2,1)S(1)}, u32[]{:S(2)}, u32[]{:S(2)}) collective-permute-start(bf16[240,128]{1,0:T(8,128)(2,1)S(1)} %fusion.3), channel_id=1, source_target_pairs={{0,6},{1,7},{2,4},{3,5},{4,2},{5,3},{6,0},{7,1},{8,14},{9,15},{10,... | collective-permute-start | bytes 184328 | tf_op jit(solution)/shard_map/ppermute | solution.py:617
  29.3 5.4 %collective-permute-start.12 = (bf16[240,128]{1,0:T(8,128)(2,1)S(1)}, bf16[240,128]{1,0:T(8,128)(2,1)S(1)}, u32[]{:S(2)}, u32[]{:S(2)}) collective-permute-start(bf16[240,128]{1,0:T(8,128)(2,1)S(1)} %fusion.3), channel_id=1, source_target_pairs={{0,2},{1,3},{2,0},{3,1},{4,6},{5,7},{6,4},{7,5},{8,10},{9,11},{10,... | collective-permute-start | bytes 184328 | tf_op jit(solution)/shard_map/ppermute | solution.py:617
  34.8 5.4 %collective-permute-start.16 = (bf16[240,128]{1,0:T(8,128)(2,1)S(1)}, bf16[240,128]{1,0:T(8,128)(2,1)S(1)}, u32[]{:S(2)}, u32[]{:S(2)}) collective-permute-start(bf16[240,128]{1,0:T(8,128)(2,1)S(1)} %add_convert_fusion.refs_0_), channel_id=1, source_target_pairs={{0,17},{1,16},{2,19},{3,18},{4,21},{5,20},{6,23},{7,22},{8,25},{9,... | collective-permute-start | bytes 184328 | tf_op jit(solution)/shard_map/ppermute | solution.py:617
  36.5 4.2 %collective-permute-start.15 = (bf16[240,128]{1,0:T(8,128)(2,1)S(1)}, bf16[240,128]{1,0:T(8,128)(2,1)S(1)}, u32[]{:S(2)}, u32[]{:S(2)}) collective-permute-start(bf16[240,128]{1,0:T(8,128)(2,1)S(1)} %add_convert_fusion.refs_0_), channel_id=1, source_target_pairs={{0,24},{1,25},{2,26},{3,27},{4,28},{5,29},{6,30},{7,31},{8,16},{9,... | collective-permute-start | bytes 184328 | tf_op jit(solution)/shard_map/ppermute | solution.py:617
  36.5 4.3 %collective-permute-start.14 = (bf16[240,128]{1,0:T(8,128)(2,1)S(1)}, bf16[240,128]{1,0:T(8,128)(2,1)S(1)}, u32[]{:S(2)}, u32[]{:S(2)}) collective-permute-start(bf16[240,128]{1,0:T(8,128)(2,1)S(1)} %add_convert_fusion.refs_0_), channel_id=1, source_target_pairs={{0,9},{1,8},{2,11},{3,10},{4,13},{5,12},{6,15},{7,14},{8,1},{9,0},... | collective-permute-start | bytes 184328 | tf_op jit(solution)/shard_map/ppermute | solution.py:617
  38.1 3.2 %collective-permute-start.17 = (bf16[240,128]{1,0:T(8,128)(2,1)S(1)}, bf16[240,128]{1,0:T(8,128)(2,1)S(1)}, u32[]{:S(2)}, u32[]{:S(2)}) collective-permute-start(bf16[240,128]{1,0:T(8,128)(2,1)S(1)} %add_convert_fusion.refs_0_), channel_id=1, source_target_pairs={{0,8},{8,0},{1,9},{9,1},{2,10},{10,2},{3,11},{11,3},{4,12},{12,4},... | collective-permute-start | bytes 184328 | tf_op jit(solution)/shard_map/ppermute | solution.py:640
  40.2 1.2 %collective-permute-start.20 = (bf16[240,128]{1,0:T(8,128)(2,1)S(1)}, bf16[240,128]{1,0:T(8,128)(2,1)S(1)}, u32[]{:S(2)}, u32[]{:S(2)}) collective-permute-start(bf16[240,128]{1,0:T(8,128)(2,1)S(1)} %collective-permute-done.16.refs_3_), channel_id=1, source_target_pairs={{0,8},{8,0},{1,9},{9,1},{2,10},{10,2},{3,11},{11,3},{4,12},{12,4},... | collective-permute-start | bytes 184328 | tf_op jit(solution)/shard_map/ppermute | solution.py:640
  40.8 1.2 %collective-permute-start.19 = (bf16[240,128]{1,0:T(8,128)(2,1)S(1)}, bf16[240,128]{1,0:T(8,128)(2,1)S(1)}, u32[]{:S(2)}, u32[]{:S(2)}) collective-permute-start(bf16[240,128]{1,0:T(8,128)(2,1)S(1)} %collective-permute-done.15.refs_2_), channel_id=1, source_target_pairs={{0,8},{8,0},{1,9},{9,1},{2,10},{10,2},{3,11},{11,3},{4,12},{12,4},... | collective-permute-start | bytes 184328 | tf_op jit(solution)/shard_map/ppermute | solution.py:640
  40.9 1.3 %collective-permute-start.18 = (bf16[240,128]{1,0:T(8,128)(2,1)S(1)}, bf16[240,128]{1,0:T(8,128)(2,1)S(1)}, u32[]{:S(2)}, u32[]{:S(2)}) collective-permute-start(bf16[240,128]{1,0:T(8,128)(2,1)S(1)} %collective-permute-done.14.refs_1_), channel_id=1, source_target_pairs={{0,8},{8,0},{1,9},{9,1},{2,10},{10,2},{3,11},{11,3},{4,12},{12,4},... | collective-permute-start | bytes 184328 | tf_op jit(solution)/shard_map/ppermute | solution.py:640

commit v7 on v6

--- a/solution.py
+++ b/solution.py
@@ -20,7 +20,7 @@
 
 def pack_kernel(
     pair, cot, features, context_in, proj_weight_in, conv_weight_in, valid_in,
-    to_core, to_chip, to_even, to_odd, context, proj_weight, conv_weight, valid, pair_low, pair_high, cot_low, cot_high, own, work, sides, sems
+    to_core, to_chip, outgoing, to_even, to_odd, context, proj_weight, conv_weight, valid, pair_low, pair_high, cot_low, cot_high, own, work, sides, sems
 ):
     tile_rows, band_cols, channels = pair.shape
     odd_row = lax.rem(lax.axis_index(ROW), 2)
@@ -53,7 +53,7 @@
     copies[4].wait()
     for part in range(features.shape[1] // channels):
         values = own[:, part * channels : (part + 1) * channels]
-        to_chip[EDGES + part] = values
+        outgoing[part] = values
         to_core[EDGES + part] = values
     for copy in copies[5:]:
         copy.wait()
@@ -113,9 +113,10 @@
     else:
         for source, step in zip(sources, (0, 1, 3, 2)):
             rows = source.shape[1]
+            skip = source.shape[0] - features.shape[1] // channels
             start = pl.multiple_of(lax.bitwise_xor(row, step) * rows, 16)
-            for part in range(source.shape[0] - EDGES):
-                features[pl.ds(start, rows), part * channels : (part + 1) * channels] = source[EDGES + part]
+            for part in range(source.shape[0] - skip):
+                features[pl.ds(start, rows), part * channels : (part + 1) * channels] = source[skip + part]
     tile_rows = query.shape[0] - 2 * MARGIN
     row_start = row * tile_rows
     col_start = row_start + col * (key.shape[0] - 2 * MARGIN - tile_rows)
@@ -327,7 +328,7 @@
 
     totals[...] = jnp.zeros(totals.shape, F32)
     skew[...] = jnp.zeros(skew.shape, F32)
-    pairs = 4
+    pairs = 6
     query_at = 9 * channels + all_bins + tail
     query_rows = {}
     order = list(range(0, tile_rows, 2 * pairs))
@@ -342,12 +343,7 @@
             change[index] = masked
             query_rows[index] = jnp.sum(masked, axis=0, keepdims=True)
             skew[index % 8, index - index % 8 : index - index % 8 + band_cols, :] += masked
-    totals[pl.ds(pl.multiple_of(query_at + row_start, 16), tile_rows), :] = jnp.concatenate([query_rows[index] for index in range(tile_rows)], axis=0)
-    reach = tile_rows + band_cols - 8
-    for step in range(8):
-        totals[pl.ds(9 * channels + col_start + step, reach), :] += skew[step, :reach, :]
-
-    per = 12
+    per = 24
     grads = jnp.zeros((channels, 9 * channels), F32)
     for first in range(0, tile_rows, per):
         around = jnp.concatenate(
@@ -359,6 +355,11 @@
         )
         cots = jnp.concatenate([rows_of(own_sources, index) for index in range(first, first + per)], axis=0)
         grads = grads + lax.dot_general(cots, around, (((0,), (0,)), ((), ())), preferred_element_type=F32)
+    totals[pl.ds(pl.multiple_of(query_at + row_start, 16), tile_rows), :] = jnp.concatenate([query_rows[index] for index in range(tile_rows)], axis=0)
+    reach = tile_rows + band_cols - 8
+    for step in range(8):
+        totals[pl.ds(9 * channels + col_start + step, reach), :] += skew[step, :reach, :]
+
     for tap in range(9):
         totals[tap * channels : (tap + 1) * channels, :] = grads[:, tap * channels : (tap + 1) * channels]
     parts, size = keep.shape[:2]
@@ -460,11 +461,12 @@
 
     layers = EDGES + width // channels
     chunk = pltpu.VMEM((tile_rows, SIDE, channels), BF16)
-    to_core, to_chip, to_even, to_odd, context_near, projection, conv_near, valid = pl.pallas_call(
+    to_core, to_chip, outgoing, to_even, to_odd, context_near, projection, conv_near, valid = pl.pallas_call(
         pack_kernel,
         out_shape=(
             shape(layers, tile_rows, channels),
-            shape(layers, tile_rows, channels),
+            shape(EDGES, tile_rows, channels),
+            shape(layers - EDGES, tile_rows, channels),
             shape(EDGES, tile_rows, channels),
             shape(EDGES, tile_rows, channels),
             shape(*context_features.shape),
@@ -473,7 +475,7 @@
             shape(*valid_bins.shape, dtype=jnp.int32),
         ),
         in_specs=[anywhere] * 7,
-        out_specs=(vmem,) * 8,
+        out_specs=(vmem,) * 9,
         scratch_shapes=[
             chunk, chunk, chunk, chunk,
             pltpu.VMEM(bin_features.shape, BF16),
@@ -517,7 +519,8 @@
         name="weights",
     )(valid, context_near, projection, conv_near)
     if row_count == 4:
-        sources = [to_core, from_core, from_chip, lax.ppermute(from_chip, "core", other_core)]
+        arrived = lax.ppermute(outgoing, ROW, odd_rows + ends)
+        sources = [to_core, from_core, arrived, lax.ppermute(arrived, "core", other_core)]
     else:
         sources = [lax.all_gather(bin_features, ROW, axis=0, tiled=True)]
 
@@ -537,7 +540,7 @@
         compiler_params=PARAMS,
         name="prepare",
     )(projection, context_key, *sources)
-    from_even, from_odd, key = lax.optimization_barrier((from_even, from_odd, key))
+    from_odd, from_even, from_chip, key = lax.optimization_barrier((from_odd, from_even, from_chip, key))
     corner = shape(2, EDGES, SIDE, channels)
     sides, corner_to_core, corner_to_chip = pl.pallas_call(
         corner_kernel,

time: 43.7 us -> 43.6 us (level)
    ppermute x1 -> x2, starting transfers between devices: 0.09 us -> 2.45 us  [the longest x1 2.44 us: body(): arrived = lax.ppermute(outgoing, ROW, odd_rows + ends)]
    ppermute x1, starting transfers between devices: 2.44 us -> 0.26 us  [body(): from_chip = lax.ppermute(to_chip, ROW, odd_rows + ends)]
    ppermute x1, starting transfers between devices: 2.42 us -> 0.74 us  [body(): corner_chip = lax.ppermute(corner_to_chip, ROW, odd_rows + ends)]
    ppermute x1, starting transfers between devices: 1.52 us -> 2.36 us  [body(): from_even = lax.ppermute(to_even, 'col', even_cols)]
    ppermute x1, waiting for transfers between devices: 0.01 us -> 0.46 us  [body(): from_core = lax.ppermute(to_core, 'core', other_core)]
  transfers between devices with their start and end apart: 21 -> 22, of which waited for: 14 -> 15; matrix products, arithmetic and copies ran while one was open for 0% -> 0% of each run, Pallas kernels for 11% -> 11%
where the time goes in v7:
time: 43.6 us; the launch traced here: 43.5 us
  starting transfers between devices  18.7 us (43%)
  waiting for transfers between devices  13.3 us (31%)
  Pallas kernels  10.6 us (24%)
  between operations  0.75 us (2%)
    ppermute x9, starting transfers between devices, across(): lax.ppermute(values, ROW + ('col',), [(index, index ^ bits) for index in...  10.6 us
    ppermute x9, waiting for transfers between devices, across(): lax.ppermute(values, ROW + ('col',), [(index, index ^ bits) for index in...  9.23 us
    pallas_call x1, Pallas kernels, body(): pl.pallas_call(outer_kernel, out_shape=(shape(2, band_cols, channels, dty...  2.83 us
    pallas_call x1, Pallas kernels, body(): pl.pallas_call(inner_kernel, out_shape=(shape(span, 3 * channels), shape(...  2.49 us
    ppermute x1, starting transfers between devices, body(): arrived = lax.ppermute(outgoing, ROW, odd_rows + ends)  2.44 us
    ppermute x1, starting transfers between devices, body(): from_even = lax.ppermute(to_even, 'col', even_cols)  2.36 us
    pallas_call x1, Pallas kernels, body(): pl.pallas_call(pack_kernel, out_shape=(shape(layers, tile_rows, channels)...  1.72 us
    pallas_call x1, Pallas kernels, body(): pl.pallas_call(late_kernel, out_shape=(shape(*pair_input.shape), shape(*p...  1.44 us
  transfers between devices with their start and end apart: 22, of which 15 were waited for; matrix products, arithmetic and copies ran while one was open for 0% of the time, Pallas kernels for 11%

profile of v7, /device:TPU:0, one launch (start us, length us, event | category | flops | bytes accessed | tf_op | source)
XLA Modules:
  0.0 43.5 jit_solution(11990939340555510279)
XLA Ops:
  0.6 1.7 %pack.1 = (bf16[7,48,128]{2,1,0:T(8,128)(2,1)S(1)}, bf16[3,48,128]{2,1,0:T(8,128)(2,1)S(1)}, bf16[4,48,128]{2,1,0:T(8,128)(2,1)S(1)}, bf16[3,48,128]{2,1,0:T(8,1...) custom-call(bf16[48,48,128]{2,1,0:T(8,128)(2,1)} %pair.7, ...), custom_call_target="tpu_custom_call" | custom-call | tf_op jit(solution)/shard_map/pack/pallas_call | solution.py:464
  2.4 2.4 %collective-permute-start.4 = (bf16[4,48,128]{2,1,0:T(8,128)(2,1)S(1)}, bf16[4,48,128]{2,1,0:T(8,128)(2,1)S(1)}, u32[]{:S(2)}, u32[]{:S(2)}) collective-permute-start(bf16[4,48,128]{2,1,0:T(8,128)(2,1)S(1)} %get-tuple-element.58), channel_id=1, source_target_pairs={{8,16},{16,8},{0,24},{24,0},{9,17},{17,9},{1,25},{25,1},{10,18},{1... | collective-permute-start | bytes 147464 | tf_op jit(solution)/shard_map/ppermute | solution.py:522
  4.8 0.7 %collective-permute-start.1 = (bf16[3,48,128]{2,1,0:T(8,128)(2,1)S(1)}, bf16[3,48,128]{2,1,0:T(8,128)(2,1)S(1)}, u32[]{:S(2)}, u32[]{:S(2)}) collective-permute-start(bf16[3,48,128]{2,1,0:T(8,128)(2,1)S(1)} %get-tuple-element.50), channel_id=1, source_target_pairs={{0,8},{1,2},{2,1},{3,4},{4,3},{5,6},{6,5},{7,15},{8,0},{9,10},{10,... | collective-permute-start | bytes 110600 | tf_op jit(solution)/shard_map/ppermute | solution.py:502
  5.5 2.4 %collective-permute-start.2 = (bf16[3,48,128]{2,1,0:T(8,128)(2,1)S(1)}, bf16[3,48,128]{2,1,0:T(8,128)(2,1)S(1)}, u32[]{:S(2)}, u32[]{:S(2)}) collective-permute-start(bf16[3,48,128]{2,1,0:T(8,128)(2,1)S(1)} %get-tuple-element.51), channel_id=1, source_target_pairs={{0,1},{1,0},{2,3},{3,2},{4,5},{5,4},{6,7},{7,6},{8,9},{9,8},{10,11... | collective-permute-start | bytes 110600 | tf_op jit(solution)/shard_map/ppermute | solution.py:503
  10.1 1.2 %collective-permute-done.3.from_chip = bf16[3,48,128]{2,1,0:T(8,128)(2,1)S(1)} collective-permute-done((bf16[3,48,128]{2,1,0:T(8,128)(2,1)S(1)}, bf16[3,48,128]{2,1,0:T(8,128)(2,1)S(1)}, u32[]{:S(2)}, u32[]{:S(2)}) %collective-permute-start.3) | collective-permute-done | bytes 36896 | tf_op jit(solution)/shard_map/ppermute | solution.py:501
  11.5 0.7 %collective-permute-start.7 = (bf16[2,3,16,128]{3,2,1,0:T(8,128)(2,1)S(1)}, bf16[2,3,16,128]{3,2,1,0:T(8,128)(2,1)S(1)}, u32[]{:S(2)}, u32[]{:S(2)}) collective-permute-start(bf16[2,3,16,128]{3,2,1,0:T(8,128)(2,1)S(1)} %get-tuple-element.65), channel_id=1, source_target_pairs={{8,16},{16,8},{0,24},{24,0},{9,17},{17,9},{1,25},{25,1},{10,18},{1... | collective-permute-start | bytes 73736 | tf_op jit(solution)/shard_map/ppermute | solution.py:553
  12.3 2.5 %inner.1 = (bf16[3072,384]{1,0:T(8,128)(2,1)S(1)}, bf16[3072,384]{1,0:T(8,128)(2,1)S(1)}, bf16[3072,128]{1,0:T(8,128)(2,1)S(1)}, f32[48,48,128]{2,1,0:T(8,128)S(1)}) custom-call(bf16[48,48,128]{2,1,0:T(8,128)(2,1)S(1)} %copy-done, bf16[48,48,128]{2,1,0:T(8,128)(2,1)S(1)} %copy-done.1, bf16[2,3,48,128]{3,2,1,0:T(8,128)(2,1)S(1)} %get-tuple-element.63.sides, ...), custom_call_target="tpu_custom_call" | custom-call | tf_op jit(solution)/shard_map/inner/pallas_call | solution.py:564
  14.8 2.8 %outer.1 = (f32[2,48,128]{2,1,0:T(8,128)S(1)}, f32[48,48,128]{2,1,0:T(8,128)S(1)}, f32[4,240,128]{2,1,0:T(8,128)S(1)}, bf16[4,240,128]{2,1,0:T(8,128)(2,1)S(1)}) custom-call(bf16[48,48,128]{2,1,0:T(8,128)(2,1)S(1)} %copy-done, bf16[48,48,128]{2,1,0:T(8,128)(2,1)S(1)} %copy-done.1, bf16[7,48,128]{2,1,0:T(8,128)(2,1)S(1)} %collective-permute-done.refs_1_.from_core, ...), custom_call_target="tpu_custom_call" | custom-call | tf_op jit(solution)/shard_map/outer/pallas_call | solution.py:576
  18.1 1.2 %collective-permute-done.8 = bf16[4,240,128]{2,1,0:T(8,128)(2,1)S(1)} collective-permute-done((bf16[4,240,128]{2,1,0:T(8,128)(2,1)S(1)}, bf16[4,240,128]{2,1,0:T(8,128)(2,1)S(1)}, u32[]{:S(2)}, u32[]{:S(2)}) %collective-permute-start.8) | collective-permute-done | bytes 245792 | tf_op jit(solution)/shard_map/ppermute | solution.py:617
  19.3 1.5 %collective-permute-start.11 = (bf16[240,128]{1,0:T(8,128)(2,1)S(1)}, bf16[240,128]{1,0:T(8,128)(2,1)S(1)}, u32[]{:S(2)}, u32[]{:S(2)}) collective-permute-start(bf16[240,128]{1,0:T(8,128)(2,1)S(1)} %get-tuple-element.95), channel_id=1, source_target_pairs={{0,17},{1,16},{2,19},{3,18},{4,21},{5,20},{6,23},{7,22},{8,25},{9,... | collective-permute-start | bytes 184328 | tf_op jit(solution)/shard_map/ppermute | solution.py:620
  21.3 1.3 %collective-permute-start.9 = (bf16[240,128]{1,0:T(8,128)(2,1)S(1)}, bf16[240,128]{1,0:T(8,128)(2,1)S(1)}, u32[]{:S(2)}, u32[]{:S(2)}) collective-permute-start(bf16[240,128]{1,0:T(8,128)(2,1)S(1)} %get-tuple-element.97), channel_id=1, source_target_pairs={{0,9},{1,8},{2,11},{3,10},{4,13},{5,12},{6,15},{7,14},{8,1},{9,0},... | collective-permute-start | bytes 184328 | tf_op jit(solution)/shard_map/ppermute | solution.py:620
  22.6 2.0 %collective-permute-done.11 = bf16[240,128]{1,0:T(8,128)(2,1)S(1)} collective-permute-done((bf16[240,128]{1,0:T(8,128)(2,1)S(1)}, bf16[240,128]{1,0:T(8,128)(2,1)S(1)}, u32[]{:S(2)}, u32[]{:S(2)}) %collective-permute-start.11) | collective-permute-done | bytes 61472 | tf_op jit(solution)/shard_map/ppermute | solution.py:620
  24.6 0.6 %collective-permute-done.10 = bf16[240,128]{1,0:T(8,128)(2,1)S(1)} collective-permute-done((bf16[240,128]{1,0:T(8,128)(2,1)S(1)}, bf16[240,128]{1,0:T(8,128)(2,1)S(1)}, u32[]{:S(2)}, u32[]{:S(2)}) %collective-permute-start.10) | collective-permute-done | bytes 61472 | tf_op jit(solution)/shard_map/ppermute | solution.py:620
  25.6 2.7 %collective-permute-start.12 = (bf16[240,128]{1,0:T(8,128)(2,1)S(1)}, bf16[240,128]{1,0:T(8,128)(2,1)S(1)}, u32[]{:S(2)}, u32[]{:S(2)}) collective-permute-start(bf16[240,128]{1,0:T(8,128)(2,1)S(1)} %fusion.3), channel_id=1, source_target_pairs={{0,4},{1,5},{2,6},{3,7},{4,0},{5,1},{6,2},{7,3},{8,12},{9,13},{10,... | collective-permute-start | bytes 184328 | tf_op jit(solution)/shard_map/ppermute | solution.py:620
  28.2 1.3 %collective-permute-start.14 = (bf16[240,128]{1,0:T(8,128)(2,1)S(1)}, bf16[240,128]{1,0:T(8,128)(2,1)S(1)}, u32[]{:S(2)}, u32[]{:S(2)}) collective-permute-start(bf16[240,128]{1,0:T(8,128)(2,1)S(1)} %fusion.3), channel_id=1, source_target_pairs={{0,6},{1,7},{2,4},{3,5},{4,2},{5,3},{6,0},{7,1},{8,14},{9,15},{10,... | collective-permute-start | bytes 184328 | tf_op jit(solution)/shard_map/ppermute | solution.py:620
  29.6 1.4 %late.1 = (bf16[48,48,128]{2,1,0:T(8,128)(2,1)}, bf16[48,48,128]{2,1,0:T(8,128)(2,1)}, bf16[512,192]{1,0:T(8,128)(2,1)S(1)}, bf16[512,384]{1,0:T(8,128)(2,1)S(1)}) custom-call(bf16[48,48,128]{2,1,0:T(8,128)(2,1)S(1)} %copy-done, bf16[48,48,128]{2,1,0:T(8,128)(2,1)S(1)} %copy-done.1, f32[48,48,128]{2,1,0:T(8,128)S(1)} %get-tuple-element.80.active, ...), custom_call_target="tpu_custom_call" | custom-call | tf_op jit(solution)/shard_map/late/pallas_call | solution.py:603
  31.0 1.4 %collective-permute-done.12 = bf16[240,128]{1,0:T(8,128)(2,1)S(1)} collective-permute-done((bf16[240,128]{1,0:T(8,128)(2,1)S(1)}, bf16[240,128]{1,0:T(8,128)(2,1)S(1)}, u32[]{:S(2)}, u32[]{:S(2)}) %collective-permute-start.12) | collective-permute-done | bytes 61472 | tf_op jit(solution)/shard_map/ppermute | solution.py:620
  32.4 2.1 %collective-permute-done.14 = bf16[240,128]{1,0:T(8,128)(2,1)S(1)} collective-permute-done((bf16[240,128]{1,0:T(8,128)(2,1)S(1)}, bf16[240,128]{1,0:T(8,128)(2,1)S(1)}, u32[]{:S(2)}, u32[]{:S(2)}) %collective-permute-start.14) | collective-permute-done | bytes 61472 | tf_op jit(solution)/shard_map/ppermute | solution.py:620
  34.7 1.7 %collective-permute-start.17 = (bf16[240,128]{1,0:T(8,128)(2,1)S(1)}, bf16[240,128]{1,0:T(8,128)(2,1)S(1)}, u32[]{:S(2)}, u32[]{:S(2)}) collective-permute-start(bf16[240,128]{1,0:T(8,128)(2,1)S(1)} %add_convert_fusion.refs_0_), channel_id=1, source_target_pairs={{0,17},{1,16},{2,19},{3,18},{4,21},{5,20},{6,23},{7,22},{8,25},{9,... | collective-permute-start | bytes 184328 | tf_op jit(solution)/shard_map/ppermute | solution.py:620
  36.4 1.6 %collective-permute-start.15 = (bf16[240,128]{1,0:T(8,128)(2,1)S(1)}, bf16[240,128]{1,0:T(8,128)(2,1)S(1)}, u32[]{:S(2)}, u32[]{:S(2)}) collective-permute-start(bf16[240,128]{1,0:T(8,128)(2,1)S(1)} %add_convert_fusion.refs_0_), channel_id=1, source_target_pairs={{0,9},{1,8},{2,11},{3,10},{4,13},{5,12},{6,15},{7,14},{8,1},{9,0},... | collective-permute-start | bytes 184328 | tf_op jit(solution)/shard_map/ppermute | solution.py:620
  38.0 2.0 %collective-permute-done.17.refs_3_ = bf16[240,128]{1,0:T(8,128)(2,1)S(1)} collective-permute-done((bf16[240,128]{1,0:T(8,128)(2,1)S(1)}, bf16[240,128]{1,0:T(8,128)(2,1)S(1)}, u32[]{:S(2)}, u32[]{:S(2)}) %collective-permute-start.17) | collective-permute-done | bytes 61472 | tf_op jit(solution)/shard_map/ppermute | solution.py:620
  40.0 0.7 %collective-permute-done.16.refs_2_ = bf16[240,128]{1,0:T(8,128)(2,1)S(1)} collective-permute-done((bf16[240,128]{1,0:T(8,128)(2,1)S(1)}, bf16[240,128]{1,0:T(8,128)(2,1)S(1)}, u32[]{:S(2)}, u32[]{:S(2)}) %collective-permute-start.16) | collective-permute-done | bytes 61472 | tf_op jit(solution)/shard_map/ppermute | solution.py:620
  41.2 0.7 %collective-permute-done.20.refs_6_ = bf16[240,128]{1,0:T(8,128)(2,1)S(1)} collective-permute-done((bf16[240,128]{1,0:T(8,128)(2,1)S(1)}, bf16[240,128]{1,0:T(8,128)(2,1)S(1)}, u32[]{:S(2)}, u32[]{:S(2)}) %collective-permute-start.20) | collective-permute-done | bytes 61472 | tf_op jit(solution)/shard_map/ppermute | solution.py:643
  42.1 1.4 %finish.1 = (bf16[48,512]{1,0:T(8,128)(2,1)}, f32[512,256]{1,0:T(8,128)}, f32[9,128,128]{2,1,0:T(8,128)}) custom-call(bf16[512,192]{1,0:T(8,128)(2,1)S(1)} %get-tuple-element.87.features_turned, bf16[512,384]{1,0:T(8,128)(2,1)S(1)} %get-tuple-element.88.context_turned, bf16[512,256]{1,0:T(8,128)(2,1)S(1)} %get-tuple-element.53.proj_weight.projection, ...), custom_call_target="tpu_custom_call" | custom-call | tf_op jit(solution)/shard_map/finish/pallas_call | solution.py:645
  (36 shorter events, 4.8 us)
Async XLA Ops:
  2.4 9.9 %copy-start = (bf16[48,48,128]{2,1,0:T(8,128)(2,1)S(1)}, bf16[48,48,128]{2,1,0:T(8,128)(2,1)}, u32[]{:S(2)}) copy-start(bf16[48,48,128]{2,1,0:T(8,128)(2,1)} %pair.7) | copy-start | bytes 1769476
  2.4 9.9 %copy-start.1 = (bf16[48,48,128]{2,1,0:T(8,128)(2,1)S(1)}, bf16[48,48,128]{2,1,0:T(8,128)(2,1)}, u32[]{:S(2)}) copy-start(bf16[48,48,128]{2,1,0:T(8,128)(2,1)} %cot.7) | copy-start | bytes 1769476
  2.4 6.2 %collective-permute-start.4 = (bf16[4,48,128]{2,1,0:T(8,128)(2,1)S(1)}, bf16[4,48,128]{2,1,0:T(8,128)(2,1)S(1)}, u32[]{:S(2)}, u32[]{:S(2)}) collective-permute-start(bf16[4,48,128]{2,1,0:T(8,128)(2,1)S(1)} %get-tuple-element.58), channel_id=1, source_target_pairs={{8,16},{16,8},{0,24},{24,0},{9,17},{17,9},{1,25},{25,1},{10,18},{1... | collective-permute-start | bytes 147464 | tf_op jit(solution)/shard_map/ppermute | solution.py:522
  4.8 5.3 %collective-permute-start.1 = (bf16[3,48,128]{2,1,0:T(8,128)(2,1)S(1)}, bf16[3,48,128]{2,1,0:T(8,128)(2,1)S(1)}, u32[]{:S(2)}, u32[]{:S(2)}) collective-permute-start(bf16[3,48,128]{2,1,0:T(8,128)(2,1)S(1)} %get-tuple-element.50), channel_id=1, source_target_pairs={{0,8},{1,2},{2,1},{3,4},{4,3},{5,6},{6,5},{7,15},{8,0},{9,10},{10,... | collective-permute-start | bytes 110600 | tf_op jit(solution)/shard_map/ppermute | solution.py:502
  5.5 4.6 %collective-permute-start.2 = (bf16[3,48,128]{2,1,0:T(8,128)(2,1)S(1)}, bf16[3,48,128]{2,1,0:T(8,128)(2,1)S(1)}, u32[]{:S(2)}, u32[]{:S(2)}) collective-permute-start(bf16[3,48,128]{2,1,0:T(8,128)(2,1)S(1)} %get-tuple-element.51), channel_id=1, source_target_pairs={{0,1},{1,0},{2,3},{3,2},{4,5},{5,4},{6,7},{7,6},{8,9},{9,8},{10,11... | collective-permute-start | bytes 110600 | tf_op jit(solution)/shard_map/ppermute | solution.py:503
  7.9 3.4 %collective-permute-start.3 = (bf16[3,48,128]{2,1,0:T(8,128)(2,1)S(1)}, bf16[3,48,128]{2,1,0:T(8,128)(2,1)S(1)}, u32[]{:S(2)}, u32[]{:S(2)}) collective-permute-start(bf16[3,48,128]{2,1,0:T(8,128)(2,1)S(1)} %get-tuple-element.52), channel_id=1, source_target_pairs={{8,16},{16,8},{0,24},{24,0},{9,17},{17,9},{1,25},{25,1},{10,18},{1... | collective-permute-start | bytes 110600 | tf_op jit(solution)/shard_map/ppermute | solution.py:501
  8.1 1.4 %collective-permute-start = (bf16[7,48,128]{2,1,0:T(8,128)(2,1)S(1)}, bf16[7,48,128]{2,1,0:T(8,128)(2,1)S(1)}, u32[]{:S(2)}, u32[]{:S(2)}) collective-permute-start(bf16[7,48,128]{2,1,0:T(8,128)(2,1)S(1)} %get-tuple-element.49.refs_0_), channel_id=1, source_target_pairs={{0,8},{8,0},{1,9},{9,1},{2,10},{10,2},{3,11},{11,3},{4,12},{12,4},... | collective-permute-start | bytes 258056 | tf_op jit(solution)/shard_map/ppermute | solution.py:504
  8.6 1.2 %collective-permute-start.5 = (bf16[4,48,128]{2,1,0:T(8,128)(2,1)S(1)}, bf16[4,48,128]{2,1,0:T(8,128)(2,1)S(1)}, u32[]{:S(2)}, u32[]{:S(2)}) collective-permute-start(bf16[4,48,128]{2,1,0:T(8,128)(2,1)S(1)} %collective-permute-done.4.refs_2_), channel_id=1, source_target_pairs={{0,8},{8,0},{1,9},{9,1},{2,10},{10,2},{3,11},{11,3},{4,12},{12,4},... | collective-permute-start | bytes 147464 | tf_op jit(solution)/shard_map/ppermute | solution.py:523
  11.3 3.5 %collective-permute-start.6 = (bf16[2,3,16,128]{3,2,1,0:T(8,128)(2,1)S(1)}, bf16[2,3,16,128]{3,2,1,0:T(8,128)(2,1)S(1)}, u32[]{:S(2)}, u32[]{:S(2)}) collective-permute-start(bf16[2,3,16,128]{3,2,1,0:T(8,128)(2,1)S(1)} %get-tuple-element.64), channel_id=1, source_target_pairs={{0,8},{8,0},{1,9},{9,1},{2,10},{10,2},{3,11},{11,3},{4,12},{12,4},... | collective-permute-start | bytes 73736 | tf_op jit(solution)/shard_map/ppermute | solution.py:554
  11.5 3.3 %collective-permute-start.7 = (bf16[2,3,16,128]{3,2,1,0:T(8,128)(2,1)S(1)}, bf16[2,3,16,128]{3,2,1,0:T(8,128)(2,1)S(1)}, u32[]{:S(2)}, u32[]{:S(2)}) collective-permute-start(bf16[2,3,16,128]{3,2,1,0:T(8,128)(2,1)S(1)} %get-tuple-element.65), channel_id=1, source_target_pairs={{8,16},{16,8},{0,24},{24,0},{9,17},{17,9},{1,25},{25,1},{10,18},{1... | collective-permute-start | bytes 73736 | tf_op jit(solution)/shard_map/ppermute | solution.py:553
  17.7 1.6 %collective-permute-start.8 = (bf16[4,240,128]{2,1,0:T(8,128)(2,1)S(1)}, bf16[4,240,128]{2,1,0:T(8,128)(2,1)S(1)}, u32[]{:S(2)}, u32[]{:S(2)}) collective-permute-start(bf16[4,240,128]{2,1,0:T(8,128)(2,1)S(1)} %get-tuple-element.76), channel_id=1, source_target_pairs={{0,8},{8,0},{1,9},{9,1},{2,10},{10,2},{3,11},{11,3},{4,12},{12,4},... | collective-permute-start | bytes 737288 | tf_op jit(solution)/shard_map/ppermute | solution.py:617
  19.3 5.2 %collective-permute-start.11 = (bf16[240,128]{1,0:T(8,128)(2,1)S(1)}, bf16[240,128]{1,0:T(8,128)(2,1)S(1)}, u32[]{:S(2)}, u32[]{:S(2)}) collective-permute-start(bf16[240,128]{1,0:T(8,128)(2,1)S(1)} %get-tuple-element.95), channel_id=1, source_target_pairs={{0,17},{1,16},{2,19},{3,18},{4,21},{5,20},{6,23},{7,22},{8,25},{9,... | collective-permute-start | bytes 184328 | tf_op jit(solution)/shard_map/ppermute | solution.py:620
  20.9 4.3 %collective-permute-start.10 = (bf16[240,128]{1,0:T(8,128)(2,1)S(1)}, bf16[240,128]{1,0:T(8,128)(2,1)S(1)}, u32[]{:S(2)}, u32[]{:S(2)}) collective-permute-start(bf16[240,128]{1,0:T(8,128)(2,1)S(1)} %get-tuple-element.96), channel_id=1, source_target_pairs={{0,24},{1,25},{2,26},{3,27},{4,28},{5,29},{6,30},{7,31},{8,16},{9,... | collective-permute-start | bytes 184328 | tf_op jit(solution)/shard_map/ppermute | solution.py:620
  21.3 4.2 %collective-permute-start.9 = (bf16[240,128]{1,0:T(8,128)(2,1)S(1)}, bf16[240,128]{1,0:T(8,128)(2,1)S(1)}, u32[]{:S(2)}, u32[]{:S(2)}) collective-permute-start(bf16[240,128]{1,0:T(8,128)(2,1)S(1)} %get-tuple-element.97), channel_id=1, source_target_pairs={{0,9},{1,8},{2,11},{3,10},{4,13},{5,12},{6,15},{7,14},{8,1},{9,0},... | collective-permute-start | bytes 184328 | tf_op jit(solution)/shard_map/ppermute | solution.py:620
  25.6 6.8 %collective-permute-start.12 = (bf16[240,128]{1,0:T(8,128)(2,1)S(1)}, bf16[240,128]{1,0:T(8,128)(2,1)S(1)}, u32[]{:S(2)}, u32[]{:S(2)}) collective-permute-start(bf16[240,128]{1,0:T(8,128)(2,1)S(1)} %fusion.3), channel_id=1, source_target_pairs={{0,4},{1,5},{2,6},{3,7},{4,0},{5,1},{6,2},{7,3},{8,12},{9,13},{10,... | collective-permute-start | bytes 184328 | tf_op jit(solution)/shard_map/ppermute | solution.py:620
  28.2 6.3 %collective-permute-start.14 = (bf16[240,128]{1,0:T(8,128)(2,1)S(1)}, bf16[240,128]{1,0:T(8,128)(2,1)S(1)}, u32[]{:S(2)}, u32[]{:S(2)}) collective-permute-start(bf16[240,128]{1,0:T(8,128)(2,1)S(1)} %fusion.3), channel_id=1, source_target_pairs={{0,6},{1,7},{2,4},{3,5},{4,2},{5,3},{6,0},{7,1},{8,14},{9,15},{10,... | collective-permute-start | bytes 184328 | tf_op jit(solution)/shard_map/ppermute | solution.py:620
  29.6 5.1 %collective-permute-start.13 = (bf16[240,128]{1,0:T(8,128)(2,1)S(1)}, bf16[240,128]{1,0:T(8,128)(2,1)S(1)}, u32[]{:S(2)}, u32[]{:S(2)}) collective-permute-start(bf16[240,128]{1,0:T(8,128)(2,1)S(1)} %fusion.3), channel_id=1, source_target_pairs={{0,2},{1,3},{2,0},{3,1},{4,6},{5,7},{6,4},{7,5},{8,10},{9,11},{10,... | collective-permute-start | bytes 184328 | tf_op jit(solution)/shard_map/ppermute | solution.py:620
  34.7 5.3 %collective-permute-start.17 = (bf16[240,128]{1,0:T(8,128)(2,1)S(1)}, bf16[240,128]{1,0:T(8,128)(2,1)S(1)}, u32[]{:S(2)}, u32[]{:S(2)}) collective-permute-start(bf16[240,128]{1,0:T(8,128)(2,1)S(1)} %add_convert_fusion.refs_0_), channel_id=1, source_target_pairs={{0,17},{1,16},{2,19},{3,18},{4,21},{5,20},{6,23},{7,22},{8,25},{9,... | collective-permute-start | bytes 184328 | tf_op jit(solution)/shard_map/ppermute | solution.py:620
  36.4 4.2 %collective-permute-start.16 = (bf16[240,128]{1,0:T(8,128)(2,1)S(1)}, bf16[240,128]{1,0:T(8,128)(2,1)S(1)}, u32[]{:S(2)}, u32[]{:S(2)}) collective-permute-start(bf16[240,128]{1,0:T(8,128)(2,1)S(1)} %add_convert_fusion.refs_0_), channel_id=1, source_target_pairs={{0,24},{1,25},{2,26},{3,27},{4,28},{5,29},{6,30},{7,31},{8,16},{9,... | collective-permute-start | bytes 184328 | tf_op jit(solution)/shard_map/ppermute | solution.py:620
  36.4 4.3 %collective-permute-start.15 = (bf16[240,128]{1,0:T(8,128)(2,1)S(1)}, bf16[240,128]{1,0:T(8,128)(2,1)S(1)}, u32[]{:S(2)}, u32[]{:S(2)}) collective-permute-start(bf16[240,128]{1,0:T(8,128)(2,1)S(1)} %add_convert_fusion.refs_0_), channel_id=1, source_target_pairs={{0,9},{1,8},{2,11},{3,10},{4,13},{5,12},{6,15},{7,14},{8,1},{9,0},... | collective-permute-start | bytes 184328 | tf_op jit(solution)/shard_map/ppermute | solution.py:620
  38.0 3.2 %collective-permute-start.18 = (bf16[240,128]{1,0:T(8,128)(2,1)S(1)}, bf16[240,128]{1,0:T(8,128)(2,1)S(1)}, u32[]{:S(2)}, u32[]{:S(2)}) collective-permute-start(bf16[240,128]{1,0:T(8,128)(2,1)S(1)} %add_convert_fusion.refs_0_), channel_id=1, source_target_pairs={{0,8},{8,0},{1,9},{9,1},{2,10},{10,2},{3,11},{11,3},{4,12},{12,4},... | collective-permute-start | bytes 184328 | tf_op jit(solution)/shard_map/ppermute | solution.py:643
  40.0 1.2 %collective-permute-start.21 = (bf16[240,128]{1,0:T(8,128)(2,1)S(1)}, bf16[240,128]{1,0:T(8,128)(2,1)S(1)}, u32[]{:S(2)}, u32[]{:S(2)}) collective-permute-start(bf16[240,128]{1,0:T(8,128)(2,1)S(1)} %collective-permute-done.17.refs_3_), channel_id=1, source_target_pairs={{0,8},{8,0},{1,9},{9,1},{2,10},{10,2},{3,11},{11,3},{4,12},{12,4},... | collective-permute-start | bytes 184328 | tf_op jit(solution)/shard_map/ppermute | solution.py:643
  40.6 1.2 %collective-permute-start.20 = (bf16[240,128]{1,0:T(8,128)(2,1)S(1)}, bf16[240,128]{1,0:T(8,128)(2,1)S(1)}, u32[]{:S(2)}, u32[]{:S(2)}) collective-permute-start(bf16[240,128]{1,0:T(8,128)(2,1)S(1)} %collective-permute-done.16.refs_2_), channel_id=1, source_target_pairs={{0,8},{8,0},{1,9},{9,1},{2,10},{10,2},{3,11},{11,3},{4,12},{12,4},... | collective-permute-start | bytes 184328 | tf_op jit(solution)/shard_map/ppermute | solution.py:643
  40.7 1.3 %collective-permute-start.19 = (bf16[240,128]{1,0:T(8,128)(2,1)S(1)}, bf16[240,128]{1,0:T(8,128)(2,1)S(1)}, u32[]{:S(2)}, u32[]{:S(2)}) collective-permute-start(bf16[240,128]{1,0:T(8,128)(2,1)S(1)} %collective-permute-done.15.refs_1_), channel_id=1, source_target_pairs={{0,8},{8,0},{1,9},{9,1},{2,10},{10,2},{3,11},{11,3},{4,12},{12,4},... | collective-permute-start | bytes 184328 | tf_op jit(solution)/shard_map/ppermute | solution.py:643
